TPU v7x, 32 devices: a whole 2x2x4 slice. The times are simulated.
32 devices in a mesh: seq: 8 (over z, x), head: 4 (over y, core).
Axes of the slice: x: 2, y: 2, z: 4, core: 2. Of those that a mesh axis runs over, the one named last changes fastest.
Arguments:
- queries: bfloat16 [4096, 2048], P('seq', 'head'), may hold values from -12 to 12
- keys: bfloat16 [4096, 2048], P('seq', 'head'), may hold values from -12 to 12
- values: bfloat16 [4096, 2048], P('seq', 'head'), may hold values from -6 to 6
- cluster_ids: int32 [16, 4096], P('head', 'seq'), may hold values from 0 to 255, as said below
- out_weight: bfloat16 [2048, 2048], P('head'), may hold values from -0.5 to 0.5
Outputs:
- mixed: bfloat16 [4096, 2048], P('seq', 'head')
Inputs may be any that keep to these rules, and one draw needn't show every extreme that they name: `cluster_ids`: within one head, the 512 tokens of one aligned block name no cluster more than 4 times, and in every block some cluster exactly 4 times.
All inputs are finite; a program needn't handle non-finite values.
Results may differ from a plain program's by a relative error of at most 0.0055.
Values may be sent and summed in bfloat16 or wider, within the bound.
No kernel may reach another device: no remote copies, remote signals or barrier semaphores. Data moves between devices by JAX's collectives and lax.ppermute only.
A program may use at most 64 MiB of HBM per device.

v0:
```python
import math

import jax
import jax.numpy as jnp
from jax import lax
from jax.sharding import PartitionSpec as P

CLUSTERS = 256
MOST = 4


def attend_block(query_part, key_part, value_part, filled_part, score_scale):
    owners, local_slots, head_width = query_part.shape
    local_count = filled_part.shape[1]
    slot_count = local_slots // local_count
    query_rows = query_part.reshape(owners, local_count, slot_count, head_width)
    key_rows = key_part.reshape(owners, local_count, slot_count, head_width)
    value_rows = value_part.reshape(owners, local_count, slot_count, head_width)
    scores = (
        jnp.einsum("scmd,tcnd->csmtn", query_rows, key_rows, preferred_element_type=jnp.float32)
        * score_scale
    )
    order_index = jnp.arange(owners * slot_count, dtype=jnp.int32).reshape(owners, slot_count)
    before = order_index[None, None, :, :] <= order_index[:, :, None, None]
    itself = order_index[None, None, :, :] == order_index[:, :, None, None]
    slot_value = jnp.arange(slot_count, dtype=jnp.float32)[None, None, :]
    taken_slot = slot_value < jnp.transpose(filled_part).astype(jnp.float32)[:, :, None]
    allowed = before[None] & (taken_slot[:, None, None, :, :] | itself[None])
    scores = jnp.where(allowed, scores, -1e30)
    row_top = jnp.max(scores, axis=(3, 4), keepdims=True)
    spread = jnp.exp(scores - row_top)
    weights = (spread / jnp.sum(spread, axis=(3, 4), keepdims=True)).astype(jnp.bfloat16)
    combined = jnp.einsum(
        "csmtn,tcnd->scmd", weights, value_rows, preferred_element_type=jnp.float32
    )
    return combined.astype(jnp.bfloat16).reshape(owners, local_slots, head_width)


def local(queries, keys, values, cluster_ids, out_weight):
    token_count = queries.shape[0]
    groups = cluster_ids.shape[0]
    head_width = queries.shape[1] // groups
    owners = lax.axis_size("seq")
    local_count = CLUSTERS // owners
    position = jnp.arange(token_count, dtype=jnp.int32)
    earlier = position[None, :] < position[:, None]
    matching = cluster_ids[:, :, None] == cluster_ids[:, None, :]
    slot_rank = jnp.sum((matching & earlier[None]).astype(jnp.int32), axis=2)
    owner_index = jnp.transpose(cluster_ids // local_count)
    within_owner = jnp.transpose(cluster_ids % local_count * MOST + slot_rank)
    head_index = jnp.arange(groups, dtype=jnp.int32)[None, :]

    def place(source):
        shaped = source.reshape(token_count, groups, head_width)
        blank = jnp.zeros((owners, groups, local_count * MOST, head_width), jnp.bfloat16)
        return blank.at[owner_index, head_index, within_owner].set(shaped)

    cluster_axis = jnp.arange(CLUSTERS, dtype=jnp.int32)
    filled = jnp.sum(
        (cluster_ids[:, :, None] == cluster_axis[None, None, :]).astype(jnp.int32), axis=1
    )
    filled = jnp.transpose(filled.reshape(groups, owners, local_count), (1, 0, 2)).astype(
        jnp.bfloat16
    )
    score_scale = 1.0 / math.sqrt(head_width)
    query_in = lax.all_to_all(place(queries), "seq", split_axis=0, concat_axis=0, tiled=True)
    key_in = lax.all_to_all(place(keys), "seq", split_axis=0, concat_axis=0, tiled=True)
    value_in = lax.all_to_all(place(values), "seq", split_axis=0, concat_axis=0, tiled=True)
    count_in = lax.all_to_all(filled, "seq", split_axis=0, concat_axis=0, tiled=True)

    def one_head(position_head):
        return attend_block(
            lax.dynamic_index_in_dim(query_in, position_head, 1, False),
            lax.dynamic_index_in_dim(key_in, position_head, 1, False),
            lax.dynamic_index_in_dim(value_in, position_head, 1, False),
            lax.dynamic_index_in_dim(count_in, position_head, 1, False),
            score_scale,
        )

    results = lax.map(one_head, jnp.arange(query_in.shape[1], dtype=jnp.int32))
    returned = lax.all_to_all(results, "seq", split_axis=1, concat_axis=1, tiled=True)
    gathered = returned[head_index, owner_index, within_owner]
    attended = gathered.reshape(token_count, groups * head_width)
    partial_sums = jnp.dot(attended, out_weight, preferred_element_type=jnp.float32)
    summed = lax.psum_scatter(partial_sums, "head", scatter_dimension=1, tiled=True)
    return summed.astype(jnp.bfloat16)


def solution(mesh):
    placed = (
        P("seq", "head"),
        P("seq", "head"),
        P("seq", "head"),
        P("head", "seq"),
        P("head", None),
    )
    return jax.shard_map(
        local, mesh=mesh, in_specs=placed, out_specs=P("seq", "head"), check_vma=False
    )
```

profile of v0, /device:TPU:0, one launch (start us, length us, event | category | flops | bytes accessed | tf_op | source)
XLA Modules:
  0.0 265.0 jit_solution(10372748927514885159)
XLA Ops:
  6.5 1.2 convert_reduce_fusion.1
  8.4 7.3 %all-to-all-start.1 = ((bf16[8,4,32]{2,1,0:T(4,128)(2,1)}), bf16[8,4,32]{2,1,0:T(4,128)(2,1)S(1)}, u32[]{:S(2)}, u32[]{:S(2)}) async-start(bf16[8,4,32]{2,1,0:T(4,128)(2,1)} %copy.27), calls=%async_computation.1 | async-start | bytes 16384 | tf_op jit(solution)/shard_map/all_to_all | solution.py:69
  16.5 2.0 convert_reduce_fusion
  21.1 1.4 reshape.115
  22.4 6.8 %scatter_custom_fusion = bf16[4096,128]{1,0:T(8,128)(2,1)} fusion(s32[2048]{0:T(1024)S(1)} %reshape.113, bf16[2048,128]{1,0:T(8,128)(2,1)S(1)} %reshape.115, bf16[]{:T(256)} %constant.63.clone.1), kind=kCustom, calls=%fused_computation.28 | custom fusion | bytes 1048578
  29.3 6.0 %all-to-all-start = ((bf16[8,4,128,128]{3,2,1,0:T(8,128)(2,1)}), bf16[8,4,128,128]{3,2,1,0:T(8,128)(2,1)S(1)}, u32[]{:S(2)}, u32[]{:S(2)}) async-start(bf16[8,4,128,128]{3,2,1,0:T(8,128)(2,1)} %bitcast.90), calls=%async_computation | async-start | bytes 2097152 | tf_op jit(solution)/shard_map/all_to_all | solution.py:68
  35.3 2.1 reshape.121
  37.4 7.2 %scatter_custom_fusion.1 = bf16[4096,128]{1,0:T(8,128)(2,1)} fusion(s32[2048]{0:T(1024)S(1)} %reshape.113, bf16[2048,128]{1,0:T(8,128)(2,1)} %reshape.121, bf16[]{:T(256)} %constant.63.clone.1), kind=kCustom, calls=%fused_computation.26 | custom fusion | bytes 1049088
  44.6 16.1 %all-to-all-done = bf16[8,4,128,128]{3,2,1,0:T(8,128)(2,1)S(1)} async-done(((bf16[8,4,128,128]{3,2,1,0:T(8,128)(2,1)}), bf16[8,4,128,128]{3,2,1,0:T(8,128)(2,1)S(1)}, u32[]{:S(2)}, u32[]{:S(2)}) %all-to-all-start) | async-done | bytes 1048608 | tf_op jit(solution)/shard_map/all_to_all | solution.py:68
  60.7 4.2 %all-to-all-start.2 = ((bf16[8,4,128,128]{3,2,1,0:T(8,128)(2,1)}), bf16[8,4,128,128]{3,2,1,0:T(8,128)(2,1)}, u32[]{:S(2)}, u32[]{:S(2)}) async-start(bf16[8,4,128,128]{3,2,1,0:T(8,128)(2,1)} %bitcast.88), calls=%async_computation.2 | async-start | bytes 2097152 | tf_op jit(solution)/shard_map/all_to_all | solution.py:66
  64.9 2.2 reshape.127
  67.1 7.1 %scatter_custom_fusion.2 = bf16[4096,128]{1,0:T(8,128)(2,1)} fusion(s32[2048]{0:T(1024)S(1)} %reshape.113, bf16[2048,128]{1,0:T(8,128)(2,1)} %reshape.127, bf16[]{:T(256)} %constant.63.clone.1), kind=kCustom, calls=%fused_computation.24 | custom fusion | bytes 1049088
  74.2 16.1 %all-to-all-done.2 = bf16[8,4,128,128]{3,2,1,0:T(8,128)(2,1)} async-done(((bf16[8,4,128,128]{3,2,1,0:T(8,128)(2,1)}), bf16[8,4,128,128]{3,2,1,0:T(8,128)(2,1)}, u32[]{:S(2)}, u32[]{:S(2)}) %all-to-all-start.2) | async-done | bytes 1048608 | tf_op jit(solution)/shard_map/all_to_all | solution.py:66
  90.3 4.4 %all-to-all-start.3 = ((bf16[8,4,128,128]{3,2,1,0:T(8,128)(2,1)}), bf16[8,4,128,128]{3,2,1,0:T(8,128)(2,1)}, u32[]{:S(2)}, u32[]{:S(2)}) async-start(bf16[8,4,128,128]{3,2,1,0:T(8,128)(2,1)} %bitcast.89), calls=%async_computation.3 | async-start | bytes 2097152 | tf_op jit(solution)/shard_map/all_to_all | solution.py:67
  94.8 25.2 %all-to-all-done.3 = bf16[8,4,128,128]{3,2,1,0:T(8,128)(2,1)} async-done(((bf16[8,4,128,128]{3,2,1,0:T(8,128)(2,1)}), bf16[8,4,128,128]{3,2,1,0:T(8,128)(2,1)}, u32[]{:S(2)}, u32[]{:S(2)}) %all-to-all-start.3) | async-done | bytes 1048608 | tf_op jit(solution)/shard_map/all_to_all | solution.py:67
  120.0 34.3 %while.10 = (s32[]{:T(128)}, bf16[4,8,128,128]{3,2,0,1:T(8,128)(2,1)}, s32[4]{0:T(128)S(1)}, bf16[8,4,128,128]{3,2,1,0:T(8,128)(2,1)S(1)}, bf16[8,4,32]{2,1,0:T(...) while((s32[]{:T(128)}, ...), condition=%wide.region_8.9_spmd, body=%wide.region_5.8_spmd.sunk | while | flops 17237316 | bytes 13532631 | solution.py:80
  122.5 1.1 constant_dynamic-slice_fusion.8
  124.2 1.6 fusion.32
  131.1 1.1 constant_dynamic-slice_fusion.8
  132.8 1.6 fusion.32
  139.7 1.1 constant_dynamic-slice_fusion.8
  141.4 1.6 fusion.32
  148.3 1.1 constant_dynamic-slice_fusion.8
  150.0 1.6 fusion.32
  154.3 4.2 %all-to-all-start.4 = ((bf16[4,8,128,128]{3,2,0,1:T(8,128)(2,1)}), bf16[4,8,128,128]{3,2,0,1:T(8,128)(2,1)}, u32[]{:S(2)}, u32[]{:S(2)}) async-start(bf16[4,8,128,128]{3,2,0,1:T(8,128)(2,1)} %get-tuple-element.42), calls=%async_computation.4 | async-start | bytes 2097152 | tf_op jit(solution)/shard_map/all_to_all | solution.py:81
  158.9 25.0 %all-to-all-done.4 = bf16[4,8,128,128]{3,2,0,1:T(8,128)(2,1)} async-done(((bf16[4,8,128,128]{3,2,0,1:T(8,128)(2,1)}), bf16[4,8,128,128]{3,2,0,1:T(8,128)(2,1)}, u32[]{:S(2)}, u32[]{:S(2)}) %all-to-all-start.4) | async-done | bytes 1048608 | tf_op jit(solution)/shard_map/all_to_all | solution.py:81
  183.9 1.3 copy.34
  185.2 22.8 %gather_fusion = bf16[2048,128]{1,0:T(8,128)(2,1)} fusion(bf16[4,8,128,128]{3,2,1,0:T(8,128)(2,1)S(1)} %copy.34, s32[2048]{0:T(1024)S(1)} %reshape.107), kind=kCustom, calls=%fused_computation | custom fusion | bytes 1073152 | tf_op jit(solution)/shard_map/gather | solution.py:82
  208.0 1.4 reshape.93
  209.4 3.2 %fusion.17 = f32[512,2048]{1,0:T(8,128)} fusion(bf16[512,512]{1,0:T(8,128)(2,1)S(1)} %reshape.93, bf16[512,2048]{1,0:T(8,128)(2,1)S(1)} %copy-done), kind=kOutput, calls=%fused_computation.52 | convolution fusion | flops 1073741824 | bytes 6815744 | tf_op jit(solution)/shard_map/dot_general | solution.py:84
  212.6 43.5 %reduce-scatter.2.cloned.1.call-done = f32[512,512]{1,0:T(8,128)} async-done(((f32[512,2048]{1,0:T(8,128)}), f32[512,512]{1,0:T(8,128)}) %reduce-scatter.2.cloned.1.call-update) | async-done | bytes 1048592 | tf_op jit(solution)/shard_map/reduce_scatter | solution.py:85
  256.1 2.1 convert_element_type.41
  (93 shorter events, 20.3 us)
Async XLA Ops:
  6.5 202.9 %copy-start = (bf16[512,2048]{1,0:T(8,128)(2,1)S(1)}, bf16[512,2048]{1,0:T(8,128)(2,1)}, u32[]{:S(2)}) copy-start(bf16[512,2048]{1,0:T(8,128)(2,1)} %param.11) | copy-start | bytes 6291460
  8.4 20.8 %all-to-all-start.1 = ((bf16[8,4,32]{2,1,0:T(4,128)(2,1)}), bf16[8,4,32]{2,1,0:T(4,128)(2,1)S(1)}, u32[]{:S(2)}, u32[]{:S(2)}) async-start(bf16[8,4,32]{2,1,0:T(4,128)(2,1)} %copy.27), calls=%async_computation.1 | async-start | bytes 16384 | tf_op jit(solution)/shard_map/all_to_all | solution.py:69
  29.3 31.4 %all-to-all-start = ((bf16[8,4,128,128]{3,2,1,0:T(8,128)(2,1)}), bf16[8,4,128,128]{3,2,1,0:T(8,128)(2,1)S(1)}, u32[]{:S(2)}, u32[]{:S(2)}) async-start(bf16[8,4,128,128]{3,2,1,0:T(8,128)(2,1)} %bitcast.90), calls=%async_computation | async-start | bytes 2097152 | tf_op jit(solution)/shard_map/all_to_all | solution.py:68
  60.7 29.6 %all-to-all-start.2 = ((bf16[8,4,128,128]{3,2,1,0:T(8,128)(2,1)}), bf16[8,4,128,128]{3,2,1,0:T(8,128)(2,1)}, u32[]{:S(2)}, u32[]{:S(2)}) async-start(bf16[8,4,128,128]{3,2,1,0:T(8,128)(2,1)} %bitcast.88), calls=%async_computation.2 | async-start | bytes 2097152 | tf_op jit(solution)/shard_map/all_to_all | solution.py:66
  90.3 29.6 %all-to-all-start.3 = ((bf16[8,4,128,128]{3,2,1,0:T(8,128)(2,1)}), bf16[8,4,128,128]{3,2,1,0:T(8,128)(2,1)}, u32[]{:S(2)}, u32[]{:S(2)}) async-start(bf16[8,4,128,128]{3,2,1,0:T(8,128)(2,1)} %bitcast.89), calls=%async_computation.3 | async-start | bytes 2097152 | tf_op jit(solution)/shard_map/all_to_all | solution.py:67
  120.0 3.6 %copy-start.1 = (bf16[8,4,128,128]{3,2,1,0:T(8,128)(2,1)}, bf16[8,4,128,128]{3,2,1,0:T(8,128)(2,1)S(1)}, u32[]{:S(2)}) copy-start(bf16[8,4,128,128]{3,2,1,0:T(8,128)(2,1)S(1)} %get-tuple-element.164) | copy-start | bytes 3145732 | tf_op jit(solution)/shard_map/while
  125.8 1.2 copy-start.2
  128.6 3.6 %copy-start.1 = (bf16[8,4,128,128]{3,2,1,0:T(8,128)(2,1)}, bf16[8,4,128,128]{3,2,1,0:T(8,128)(2,1)S(1)}, u32[]{:S(2)}) copy-start(bf16[8,4,128,128]{3,2,1,0:T(8,128)(2,1)S(1)} %get-tuple-element.164) | copy-start | bytes 3145732 | tf_op jit(solution)/shard_map/while
  134.4 1.2 copy-start.2
  137.1 3.6 %copy-start.1 = (bf16[8,4,128,128]{3,2,1,0:T(8,128)(2,1)}, bf16[8,4,128,128]{3,2,1,0:T(8,128)(2,1)S(1)}, u32[]{:S(2)}) copy-start(bf16[8,4,128,128]{3,2,1,0:T(8,128)(2,1)S(1)} %get-tuple-element.164) | copy-start | bytes 3145732 | tf_op jit(solution)/shard_map/while
  143.0 1.2 copy-start.2
  145.7 3.6 %copy-start.1 = (bf16[8,4,128,128]{3,2,1,0:T(8,128)(2,1)}, bf16[8,4,128,128]{3,2,1,0:T(8,128)(2,1)S(1)}, u32[]{:S(2)}) copy-start(bf16[8,4,128,128]{3,2,1,0:T(8,128)(2,1)S(1)} %get-tuple-element.164) | copy-start | bytes 3145732 | tf_op jit(solution)/shard_map/while
  151.6 1.2 copy-start.2
  154.3 29.7 %all-to-all-start.4 = ((bf16[4,8,128,128]{3,2,0,1:T(8,128)(2,1)}), bf16[4,8,128,128]{3,2,0,1:T(8,128)(2,1)}, u32[]{:S(2)}, u32[]{:S(2)}) async-start(bf16[4,8,128,128]{3,2,0,1:T(8,128)(2,1)} %get-tuple-element.42), calls=%async_computation.4 | async-start | bytes 2097152 | tf_op jit(solution)/shard_map/all_to_all | solution.py:81
  158.5 97.6 %reduce-scatter.2.cloned.1.call-start = ((), (), s32[]{:S(2)}) async-start(), calls=%async_computation.6 | async-start | bytes 5242880 | tf_op jit(solution)/shard_map/reduce_scatter | solution.py:85
Sparse Core Ops, SparseCore 0:
  212.7 43.2 reduce-scatter.1
where the time goes:
time: 266 us; the launch traced here: 265 us
  waiting for transfers between devices  126 us (47%)
  local copies, waits for them, and re-layouts  68.6 us (26%)
  starting transfers between devices  26.2 us (10%)
  between operations  13.5 us (5%)
  matrix products  11.7 us (4%)
  other arithmetic  11.4 us (4%)
  loops' own time  7.73 us (3%)
    reduce_scatter x1, waiting for transfers between devices, local(): lax.psum_scatter(partial_sums, 'head', scatter_dimension=1, tiled=True)  43.5 us
    all_to_all x1, waiting for transfers between devices, local(): lax.all_to_all(place(keys), 'seq', split_axis=0, concat_axis=0, tiled=True)  25.2 us
    all_to_all x1, waiting for transfers between devices, local(): lax.all_to_all(results, 'seq', split_axis=1, concat_axis=1, tiled=True)  25 us
    gather x1, local copies, waits for them, and re-layouts, local(): gathered = returned[head_index, owner_index, within_owner]  22.8 us
    unnamed x7, local copies, waits for them, and re-layouts  21.5 us
    all_to_all x1, waiting for transfers between devices, local(): lax.all_to_all(place(queries), 'seq', split_axis=0, concat_axis=0, tiled=...  16.1 us
    all_to_all x1, waiting for transfers between devices, local(): lax.all_to_all(place(values), 'seq', split_axis=0, concat_axis=0, tiled=T...  16.1 us
    another operation x1, loops' own time, local(): results = lax.map(one_head, jnp.arange(query_in.shape[1], dtype=jnp.int32))  7.73 us
  transfers between devices with their start and end apart: 6, of which 5 were waited for; matrix products, arithmetic and copies ran while one was open for 12% of the time, Pallas kernels for 0%

commit v1 on v0

--- a/solution.py
+++ b/solution.py
@@ -3,6 +3,8 @@
 import jax
 import jax.numpy as jnp
 from jax import lax
+from jax.experimental import pallas as pl
+from jax.experimental.pallas import tpu as pltpu
 from jax.sharding import PartitionSpec as P
 
 CLUSTERS = 256
@@ -36,7 +38,7 @@
     return combined.astype(jnp.bfloat16).reshape(owners, local_slots, head_width)
 
 
-def local(queries, keys, values, cluster_ids, out_weight):
+def padded_plan(queries, keys, values, cluster_ids, out_weight):
     token_count = queries.shape[0]
     groups = cluster_ids.shape[0]
     head_width = queries.shape[1] // groups
@@ -86,6 +88,243 @@
     return summed.astype(jnp.bfloat16)
 
 
+ID_ROWS = 16
+MISMATCH = 262144.0
+
+
+def pack_kernel(place_ref, q_ref, k_ref, v_ref, ids_ref, *outs):
+    heads = ids_ref.shape[0]
+    rows, width = outs[0].shape
+    parts = rows // width
+    for offset in range(heads):
+        q_out, kv_out = outs[2 * offset], outs[2 * offset + 1]
+        head = lax.bitwise_xor(place_ref[0], offset)
+        columns = pl.ds(pl.multiple_of(head * width, width), width)
+        kv_out[pl.ds(0, rows), :] = k_ref[:, columns]
+        kv_out[pl.ds(rows, rows), :] = v_ref[:, columns]
+        q_out[...] = q_ref[:, columns]
+        ids = ids_ref[pl.ds(head, 1), :].astype(jnp.float32)
+        lines = [ids[:, part * width : (part + 1) * width] for part in range(parts)]
+        lines.append(jnp.zeros((ID_ROWS - parts, width), jnp.float32))
+        kv_out[pl.ds(2 * rows, ID_ROWS), :] = jnp.concatenate(lines, axis=0).astype(jnp.bfloat16)
+
+
+def pack(place, queries, keys, values, cluster_ids):
+    heads = cluster_ids.shape[0]
+    rows = queries.shape[0]
+    width = queries.shape[1] // heads
+    local_memory = pl.BlockSpec(memory_space=pltpu.VMEM)
+    pair = [
+        jax.ShapeDtypeStruct((rows, width), jnp.bfloat16),
+        jax.ShapeDtypeStruct((2 * rows + ID_ROWS, width), jnp.bfloat16),
+    ]
+    outs = pl.pallas_call(
+        pack_kernel,
+        out_shape=tuple(pair * heads),
+        in_specs=[pl.BlockSpec(memory_space=pltpu.SMEM)] + [local_memory] * 4,
+        out_specs=(local_memory,) * (2 * heads),
+        name="pack",
+    )(place, queries, keys, values, cluster_ids)
+    return outs[0::2], outs[1::2]
+
+
+def attend_kernel(scale, where_ref, *refs):
+    pieces = (len(refs) - 6) // 4
+    own_refs, far_refs, q_refs, out_refs = (refs[pieces * kind : pieces * (kind + 1)] for kind in range(4))
+    k_all, v_all, q_all, ids_all, out_all, sems = refs[4 * pieces :]
+    rows, width = q_refs[0].shape
+    parts = rows // width
+    tile = 256
+    started = []
+    slots = [lax.bitwise_xor(where_ref[0], offset) for offset in range(pieces)]
+    spans = [pl.ds(pl.multiple_of(slot * rows, rows), rows) for slot in slots]
+
+    def fetch(source, target):
+        copy = pltpu.make_async_copy(source, target, sems.at[len(started)])
+        copy.start()
+        started.append(copy)
+
+    for side, side_refs in enumerate((own_refs, far_refs)):
+        for ref, slot in zip(side_refs, slots):
+            fetch(ref.at[pl.ds(2 * rows, ID_ROWS)], ids_all.at[side, slot])
+    for ref, span in zip(q_refs, spans):
+        fetch(ref, q_all.at[span, pl.ds(0, width)])
+    for side, side_refs in enumerate((own_refs, far_refs)):
+        for ref, span in zip(side_refs, spans):
+            fetch(ref.at[pl.ds(0, rows)], k_all.at[side, span, pl.ds(0, width)])
+            fetch(ref.at[pl.ds(rows, rows)], v_all.at[side, span, pl.ds(0, width)])
+    v_all[:, :, width:] = jnp.ones((2, pieces * rows, width), jnp.bfloat16)
+    for copy in started[: 2 * pieces]:
+        copy.wait()
+    lane = lax.broadcasted_iota(jnp.int32, (width, width), 1)
+    shift = jnp.minimum(lane // 2, 8)
+    odd = lane % 2
+    live = lane < 16
+    for side in range(2):
+        for piece in range(pieces):
+            ids = ids_all[side, piece].astype(jnp.float32)
+            for part in range(parts):
+                line = jnp.broadcast_to(ids[part : part + 1], (width, width)).T.astype(jnp.int32)
+                flag = lax.bitwise_xor(lax.bitwise_and(lax.shift_right_logical(line, shift), 1), odd)
+                here = pl.ds(piece * rows + part * width, width)
+                mark = jnp.where(live, flag.astype(jnp.float32), 0.0)
+                k_all[side, here, width:] = mark.astype(jnp.bfloat16)
+                if side == 0:
+                    other = jnp.where(live, (flag.astype(jnp.float32) - 1.0) * MISMATCH, 0.0)
+                    q_all[here, width:] = other.astype(jnp.bfloat16)
+    for copy in started[2 * pieces :]:
+        copy.wait()
+
+    later = where_ref[1]
+    far_bias = jnp.where(later > 0, 0.0, -MISMATCH * 4.0).astype(jnp.float32)
+    factor = scale * math.log2(math.e)
+    contract = (((1,), (1,)), ((), ()))
+    for piece in range(pieces):
+        span = (piece + 1) * rows
+        for step in range(rows // tile):
+            q = q_all[pl.ds(piece * rows + step * tile, tile), :]
+            own = lax.dot_general(q, k_all[0, pl.ds(0, span), :], contract, preferred_element_type=jnp.float32)
+            far = lax.dot_general(q, k_all[1, pl.ds(0, span), :], contract, preferred_element_type=jnp.float32)
+            before = piece * rows
+            row = lax.broadcasted_iota(jnp.int32, (tile, rows), 0) + step * tile
+            column = lax.broadcasted_iota(jnp.int32, (tile, rows), 1)
+            diagonal = jnp.where(column <= row, own[:, before:], -MISMATCH * 4.0)
+            last = far[:, before:] + far_bias
+            if piece:
+                own = jnp.concatenate([own[:, :before], diagonal], axis=1)
+                far = jnp.concatenate([far[:, :before], last], axis=1)
+            else:
+                own, far = diagonal, last
+            top = jnp.maximum(own[:, :width], far[:, :width])
+            for start in range(width, span, width):
+                top = jnp.maximum(top, own[:, start : start + width])
+                top = jnp.maximum(top, far[:, start : start + width])
+            top = jnp.max(top, axis=1, keepdims=True) * factor
+            own = jnp.exp2(own * factor - top).astype(jnp.bfloat16)
+            far = jnp.exp2(far * factor - top).astype(jnp.bfloat16)
+            total = jnp.dot(own, v_all[0, pl.ds(0, span), :], preferred_element_type=jnp.float32)
+            total = total + jnp.dot(far, v_all[1, pl.ds(0, span), :], preferred_element_type=jnp.float32)
+            result = total[:, :width] / total[:, width:]
+            out_all[piece, pl.ds(step * tile, tile), :] = result.astype(jnp.bfloat16)
+    started.clear()
+    for ref, slot in zip(out_refs, slots):
+        fetch(out_all.at[slot], ref)
+    for copy in started:
+        copy.wait()
+
+
+def attend(where, kv_own, kv_far, q):
+    pieces = len(q)
+    rows, width = q[0].shape
+    anywhere = pl.BlockSpec(memory_space=pl.ANY)
+    return pl.pallas_call(
+        lambda *refs: attend_kernel(1.0 / math.sqrt(width), *refs),
+        out_shape=(jax.ShapeDtypeStruct((rows, width), jnp.bfloat16),) * pieces,
+        in_specs=[pl.BlockSpec(memory_space=pltpu.SMEM)] + [anywhere] * (3 * pieces),
+        out_specs=(anywhere,) * pieces,
+        scratch_shapes=[
+            pltpu.VMEM((2, pieces * rows, 2 * width), jnp.bfloat16),
+            pltpu.VMEM((2, pieces * rows, 2 * width), jnp.bfloat16),
+            pltpu.VMEM((pieces * rows, 2 * width), jnp.bfloat16),
+            pltpu.VMEM((2, pieces, ID_ROWS, width), jnp.bfloat16),
+            pltpu.VMEM((pieces, rows, width), jnp.bfloat16),
+            pltpu.SemaphoreType.DMA((7 * pieces,)),
+        ],
+        compiler_params=pltpu.CompilerParams(vmem_limit_bytes=48 * 1024 * 1024),
+        name="attend",
+    )(where, *kv_own, *kv_far, *q)
+
+
+def project_kernel(where_ref, *refs):
+    pieces = (len(refs) - 8) // 4
+    a_refs, w_refs = refs[: 4 * pieces], refs[4 * pieces : 4 * pieces + 4]
+    out_ref, a_all, w_all, sems = refs[4 * pieces + 4 :]
+    rows, width = a_refs[0].shape
+    place, here = where_ref[0], where_ref[2]
+    started = []
+
+    def fetch(source, target):
+        copy = pltpu.make_async_copy(source, target, sems.at[len(started)])
+        copy.start()
+        started.append(copy)
+
+    for far in range(4):
+        group = lax.bitwise_xor(here, far)
+        fetch(w_refs[far], w_all.at[group])
+        for offset in range(pieces):
+            head = lax.bitwise_xor(place, offset)
+            columns = pl.ds(pl.multiple_of(head * width, width), width)
+            fetch(a_refs[far * pieces + offset], a_all.at[group, :, columns])
+    for copy in started:
+        copy.wait()
+    total = jnp.dot(a_all[0], w_all[0], preferred_element_type=jnp.float32)
+    for group in range(1, 4):
+        total = total + jnp.dot(a_all[group], w_all[group], preferred_element_type=jnp.float32)
+    out_ref[...] = total.astype(jnp.bfloat16)
+
+
+def project(where, blocks, weights):
+    pieces = len(blocks[0])
+    rows, width = blocks[0][0].shape
+    anywhere = pl.BlockSpec(memory_space=pl.ANY)
+    return pl.pallas_call(
+        project_kernel,
+        out_shape=jax.ShapeDtypeStruct((rows, weights[0].shape[1]), jnp.bfloat16),
+        in_specs=[pl.BlockSpec(memory_space=pltpu.SMEM)] + [anywhere] * (4 * pieces + 4),
+        out_specs=pl.BlockSpec(memory_space=pltpu.VMEM),
+        scratch_shapes=[
+            pltpu.VMEM((4, rows, pieces * width), jnp.bfloat16),
+            pltpu.VMEM((4,) + weights[0].shape, jnp.bfloat16),
+            pltpu.SemaphoreType.DMA((4 + 4 * pieces,)),
+        ],
+        compiler_params=pltpu.CompilerParams(vmem_limit_bytes=32 * 1024 * 1024),
+        name="project",
+    )(where, *[piece for block in blocks for piece in block], *weights)
+
+
+def head_plan(queries, keys, values, cluster_ids, out_weight):
+    heads = cluster_ids.shape[0]
+    seq = lax.axis_index("seq").astype(jnp.int32)
+    here = lax.axis_index("head").astype(jnp.int32)
+    where = jnp.stack([seq // 2, seq % 2, here])
+
+    def swap(array, axis, bits):
+        size = lax.axis_size(axis)
+        return lax.ppermute(array, axis, [(place, place ^ bits) for place in range(size)])
+
+    def after(array, *others):
+        return lax.optimization_barrier((array,) + others)[0]
+
+    q, kv = pack(where, queries, keys, values, cluster_ids)
+    kv_own, kv_far, q_own = [kv[0]] + [None] * 3, [None] * 4, [q[0]] + [None] * 3
+    for offset in (2, 3, 1):
+        kv_own[offset] = swap(kv[offset], "seq", 2 * offset)
+    kv_far[0] = swap(kv[0], "seq", 1)
+    columns = out_weight.shape[1] // 4
+    weights = []
+    late_weight = after(out_weight, kv[1])
+    for far in range(4):
+        block = lax.dynamic_slice_in_dim(late_weight, (here ^ far) * columns, columns, 1)
+        weights.append(swap(block, "head", far) if far else block)
+    for offset in (1, 2, 3):
+        kv_far[offset] = swap(kv_own[offset], "seq", 1)
+    for offset in (2, 3, 1):
+        q_own[offset] = swap(after(q[offset], kv_own[2], kv_own[3]), "seq", 2 * offset)
+    attended = list(attend(where, kv_own, kv_far, q_own))
+    for offset in range(1, heads):
+        attended[offset] = swap(attended[offset], "seq", 2 * offset)
+    across = [swap(piece, "head", 2) for piece in attended]
+    blocks = [attended, [swap(piece, "head", 1) for piece in attended], across, [swap(piece, "head", 1) for piece in across]]
+    return project(where, blocks, weights)
+
+
+def local(queries, keys, values, cluster_ids, out_weight):
+    groups = cluster_ids.shape[0]
+    if lax.axis_size("seq") == 2 * groups and lax.axis_size("head") == 4:
+        return head_plan(queries, keys, values, cluster_ids, out_weight)
+    return padded_plan(queries, keys, values, cluster_ids, out_weight)
+
+
 def solution(mesh):
     placed = (
         P("seq", "head"),

time: 266 us -> 98.4 us (0.37)
  waiting for transfers between devices: 126 us -> 41.8 us
  local copies, waits for them, and re-layouts: 68.6 us -> 1.68 us
  Pallas kernels: 0 us -> 17.7 us
  between operations: 13.5 us -> 0.09 us
  matrix products: 11.7 us -> 0 us
  other arithmetic: 11.4 us -> 0.59 us
  starting transfers between devices: 26.2 us -> 36.4 us
  loops' own time: 7.73 us -> 0 us
    all_to_all x5 -> x0, waiting for transfers between devices: 82.4 us -> none  [the longest x1 25.2 us: local(): lax.all_to_all(place(keys), 'seq', split_axis=0, concat_axis=0, tiled=True)]
    reduce_scatter x1 -> x0, waiting for transfers between devices: 43.5 us -> none  [local(): lax.psum_scatter(partial_sums, 'head', scatter_dimension=1, tiled=True)]
    ppermute x0 -> x28, waiting for transfers between devices: none -> 41.8 us  [swap(): lax.ppermute(array, axis, [(place, place ^ bits) for place in range(size)])]
    ppermute x0 -> x28, starting transfers between devices: none -> 36.4 us  [swap(): lax.ppermute(array, axis, [(place, place ^ bits) for place in range(size)])]
    all_to_all x5 -> x0, starting transfers between devices: 26.1 us -> none  [the longest x1 7.25 us: local(): lax.all_to_all(filled, 'seq', split_axis=0, concat_axis=0, tiled=True)]
    gather x1 -> x0, local copies, waits for them, and re-layouts: 22.8 us -> none  [local(): gathered = returned[head_index, owner_index, within_owner]]
    unnamed x7 -> x8, local copies, waits for them, and re-layouts: 21.5 us -> 0.02 us
    pallas_call x0 -> x3, Pallas kernels: none -> 17.7 us  [the longest x1 11.7 us: attend(): pl.pallas_call(lambda *refs: attend_kernel(1.0 / math.sqrt(width), *refs)...]
  transfers between devices with their start and end apart: 6 -> 28, of which waited for: 5 -> 9; matrix products, arithmetic and copies ran while one was open for 12% -> 2% of each run, Pallas kernels for 0% -> 12%
where the time goes in v1:
time: 98.4 us; the launch traced here: 98.3 us
  waiting for transfers between devices  41.8 us (42%)
  starting transfers between devices  36.4 us (37%)
  Pallas kernels  17.7 us (18%)
  local copies, waits for them, and re-layouts  1.68 us (2%)
    ppermute x28, waiting for transfers between devices, swap(): lax.ppermute(array, axis, [(place, place ^ bits) for place in range(size)])  41.8 us
    ppermute x28, starting transfers between devices, swap(): lax.ppermute(array, axis, [(place, place ^ bits) for place in range(size)])  36.4 us
    pallas_call x1, Pallas kernels, attend(): pl.pallas_call(lambda *refs: attend_kernel(1.0 / math.sqrt(width), *refs)...  11.7 us
    pallas_call x1, Pallas kernels, project(): pl.pallas_call(project_kernel, out_shape=jax.ShapeDtypeStruct((rows, weig...  3.33 us
    pallas_call x1, Pallas kernels, pack(): pl.pallas_call(pack_kernel, out_shape=tuple(pair * heads), in_specs=[pl.B...  2.71 us
  transfers between devices with their start and end apart: 28, of which 9 were waited for; matrix products, arithmetic and copies ran while one was open for 2% of the time, Pallas kernels for 12%

profile of v1, /device:TPU:0, one launch (start us, length us, event | category | flops | bytes accessed | tf_op | source)
XLA Modules:
  0.0 98.3 jit_solution(804304929680028911)
XLA Ops:
  0.0 0.6 pad_add_fusion.place_ref.refs_0_.where_ref
  0.6 2.7 %pack.1 = (bf16[512,128]{1,0:T(8,128)(2,1)}, bf16[1040,128]{1,0:T(8,128)(2,1)}, bf16[512,128]{1,0:T(8,128)(2,1)}, bf16[1040,128]{1,0:T(8,128)(2,1)}, bf16[512,12...) custom-call(s32[3]{0:T(128)} %pad_add_fusion.place_ref.refs_0_.where_ref, ...), custom_call_target="tpu_custom_call" | custom-call | tf_op jit(solution)/shard_map/pack/pallas_call | solution.py:121
  3.3 4.0 %collective-permute-start.1 = (bf16[1040,128]{1,0:T(8,128)(2,1)}, bf16[1040,128]{1,0:T(8,128)(2,1)S(1)}, u32[]{:S(2)}, u32[]{:S(2)}) collective-permute-start(bf16[1040,128]{1,0:T(8,128)(2,1)} %get-tuple-element.23), channel_id=1, source_target_pairs={{0,16},{4,20},{8,24},{12,28},{16,0},{20,4},{24,8},{28,12},{1,17},{... | collective-permute-start | bytes 798728 | tf_op jit(solution)/shard_map/ppermute | solution.py:293
  7.3 1.3 %collective-permute-start.2 = (bf16[1040,128]{1,0:T(8,128)(2,1)}, bf16[1040,128]{1,0:T(8,128)(2,1)S(1)}, u32[]{:S(2)}, u32[]{:S(2)}) collective-permute-start(bf16[1040,128]{1,0:T(8,128)(2,1)} %get-tuple-element.24), channel_id=1, source_target_pairs={{0,24},{4,28},{8,16},{12,20},{16,8},{20,12},{24,0},{28,4},{1,25},{... | collective-permute-start | bytes 798728 | tf_op jit(solution)/shard_map/ppermute | solution.py:293
  8.7 1.5 %collective-permute-start.3 = (bf16[1040,128]{1,0:T(8,128)(2,1)}, bf16[1040,128]{1,0:T(8,128)(2,1)S(1)}, u32[]{:S(2)}, u32[]{:S(2)}) collective-permute-start(bf16[1040,128]{1,0:T(8,128)(2,1)} %get-tuple-element.21.refs_1_), channel_id=1, source_target_pairs={{0,4},{4,0},{8,12},{12,8},{16,20},{20,16},{24,28},{28,24},{1,5},{5... | collective-permute-start | bytes 798728 | tf_op jit(solution)/shard_map/ppermute | solution.py:293
  10.4 15.8 %collective-permute-done.1.refs_3_ = bf16[1040,128]{1,0:T(8,128)(2,1)S(1)} collective-permute-done((bf16[1040,128]{1,0:T(8,128)(2,1)}, bf16[1040,128]{1,0:T(8,128)(2,1)S(1)}, u32[]{:S(2)}, u32[]{:S(2)}) %collective-permute-start.1) | collective-permute-done | bytes 266272 | tf_op jit(solution)/shard_map/ppermute | solution.py:293
  26.3 5.8 %collective-permute-start.7 = (bf16[512,128]{1,0:T(8,128)(2,1)}, bf16[512,128]{1,0:T(8,128)(2,1)S(1)}, u32[]{:S(2)}, u32[]{:S(2)}) collective-permute-start(bf16[512,128]{1,0:T(8,128)(2,1)} %get-tuple-element.27), channel_id=1, source_target_pairs={{0,8},{4,12},{8,0},{12,4},{16,24},{20,28},{24,16},{28,20},{1,9},{5... | collective-permute-start | bytes 393224 | tf_op jit(solution)/shard_map/ppermute | solution.py:293
  32.0 1.9 %collective-permute-start.8 = (bf16[512,128]{1,0:T(8,128)(2,1)}, bf16[512,128]{1,0:T(8,128)(2,1)S(1)}, u32[]{:S(2)}, u32[]{:S(2)}) collective-permute-start(bf16[512,128]{1,0:T(8,128)(2,1)} %get-tuple-element.29), channel_id=1, source_target_pairs={{0,16},{4,20},{8,24},{12,28},{16,0},{20,4},{24,8},{28,12},{1,17},{... | collective-permute-start | bytes 393224 | tf_op jit(solution)/shard_map/ppermute | solution.py:293
  33.9 1.5 %collective-permute-start.5 = (bf16[1040,128]{1,0:T(8,128)(2,1)S(1)}, bf16[1040,128]{1,0:T(8,128)(2,1)S(1)}, u32[]{:S(2)}, u32[]{:S(2)}) collective-permute-start(bf16[1040,128]{1,0:T(8,128)(2,1)S(1)} %collective-permute-done.1.refs_3_), channel_id=1, source_target_pairs={{0,4},{4,0},{8,12},{12,8},{16,20},{20,16},{24,28},{28,24},{1,5},{5... | collective-permute-start | bytes 798728 | tf_op jit(solution)/shard_map/ppermute | solution.py:293
  35.4 1.7 %constant_dynamic-slice_fusion = (bf16[512,512]{1,0:T(8,128)(2,1)S(1)}, bf16[512,512]{1,0:T(8,128)(2,1)S(1)}, bf16[512,512]{1,0:T(8,128)(2,1)S(1)}, bf16[512,512]{1,0:T(8,128)(2,1)S(1)}) fusion(bf16[512,2048]{1,0:T(8,128)(2,1)} %param.9, s32[]{:T(128)S(6)} %select_n.28, s32[]{:T(128)S(6)} %select_n.27, s32[]{:T(128)S(6)} %select_n.26, s32[]{:T(128)S(6)} %select_n.25), kind=kLoop, calls=%fused_computation | loop fusion | bytes 4194320 | tf_op jit(solution)/shard_map/dynamic_slice | solution.py:307
  37.1 0.6 collective-permute-start.27
  37.7 1.0 %collective-permute-start.26 = (bf16[512,512]{1,0:T(8,128)(2,1)S(1)}, bf16[512,512]{1,0:T(8,128)(2,1)S(1)}, u32[]{:S(2)}, u32[]{:S(2)}) collective-permute-start(bf16[512,512]{1,0:T(8,128)(2,1)S(1)} %get-tuple-element.38), channel_id=1, source_target_pairs={{0,2},{1,3},{2,0},{3,1},{4,6},{5,7},{6,4},{7,5},{8,10},{9,11},{10,... | collective-permute-start | bytes 1572872 | tf_op jit(solution)/shard_map/ppermute | solution.py:293
  39.0 5.2 %collective-permute-start.9 = (bf16[512,128]{1,0:T(8,128)(2,1)S(1)}, bf16[512,128]{1,0:T(8,128)(2,1)S(1)}, u32[]{:S(2)}, u32[]{:S(2)}) collective-permute-start(bf16[512,128]{1,0:T(8,128)(2,1)S(1)} %copy-done.3), channel_id=1, source_target_pairs={{0,24},{4,28},{8,16},{12,20},{16,8},{20,12},{24,0},{28,4},{1,25},{... | collective-permute-start | bytes 393224 | tf_op jit(solution)/shard_map/ppermute | solution.py:293
  44.2 3.2 %collective-permute-done.9.refs_12_ = bf16[512,128]{1,0:T(8,128)(2,1)S(1)} collective-permute-done((bf16[512,128]{1,0:T(8,128)(2,1)S(1)}, bf16[512,128]{1,0:T(8,128)(2,1)S(1)}, u32[]{:S(2)}, u32[]{:S(2)}) %collective-permute-start.9) | collective-permute-done | bytes 131104 | tf_op jit(solution)/shard_map/ppermute | solution.py:293
  47.5 1.5 %collective-permute-start.6 = (bf16[1040,128]{1,0:T(8,128)(2,1)S(1)}, bf16[1040,128]{1,0:T(8,128)(2,1)S(1)}, u32[]{:S(2)}, u32[]{:S(2)}) collective-permute-start(bf16[1040,128]{1,0:T(8,128)(2,1)S(1)} %collective-permute-done.2.refs_4_), channel_id=1, source_target_pairs={{0,4},{4,0},{8,12},{12,8},{16,20},{20,16},{24,28},{28,24},{1,5},{5... | collective-permute-start | bytes 798728 | tf_op jit(solution)/shard_map/ppermute | solution.py:293
  49.0 0.5 collective-permute-start.4
  49.5 7.3 %collective-permute-done.6.refs_8_ = bf16[1040,128]{1,0:T(8,128)(2,1)S(1)} collective-permute-done((bf16[1040,128]{1,0:T(8,128)(2,1)S(1)}, bf16[1040,128]{1,0:T(8,128)(2,1)S(1)}, u32[]{:S(2)}, u32[]{:S(2)}) %collective-permute-start.6) | collective-permute-done | bytes 266272 | tf_op jit(solution)/shard_map/ppermute | solution.py:293
  56.8 3.5 %collective-permute-done.4.refs_6_ = bf16[1040,128]{1,0:T(8,128)(2,1)S(1)} collective-permute-done((bf16[1040,128]{1,0:T(8,128)(2,1)S(1)}, bf16[1040,128]{1,0:T(8,128)(2,1)S(1)}, u32[]{:S(2)}, u32[]{:S(2)}) %collective-permute-start.4) | collective-permute-done | bytes 266272 | tf_op jit(solution)/shard_map/ppermute | solution.py:293
  60.3 11.7 %attend.1 = (bf16[512,128]{1,0:T(8,128)(2,1)S(1)}, bf16[512,128]{1,0:T(8,128)(2,1)S(1)}, bf16[512,128]{1,0:T(8,128)(2,1)S(1)}, bf16[512,128]{1,0:T(8,128)(2,1)S(1)}) custom-call(s32[3]{0:T(128)S(1)} %copy-done.2, bf16[1040,128]{1,0:T(8,128)(2,1)S(1)} %copy-done, bf16[1040,128]{1,0:T(8,128)(2,1)S(1)} %collective-permute-done.refs_2_, ...), custom_call_target="tpu_custom_call" | custom-call | tf_op jit(solution)/shard_map/attend/pallas_call | solution.py:220
  72.0 2.3 %collective-permute-start.10 = (bf16[512,128]{1,0:T(8,128)(2,1)S(1)}, bf16[512,128]{1,0:T(8,128)(2,1)S(1)}, u32[]{:S(2)}, u32[]{:S(2)}) collective-permute-start(bf16[512,128]{1,0:T(8,128)(2,1)S(1)} %get-tuple-element.33), channel_id=1, source_target_pairs={{0,8},{4,12},{8,0},{12,4},{16,24},{20,28},{24,16},{28,20},{1,9},{5... | collective-permute-start | bytes 393224 | tf_op jit(solution)/shard_map/ppermute | solution.py:293
  74.3 1.4 %collective-permute-start.11 = (bf16[512,128]{1,0:T(8,128)(2,1)S(1)}, bf16[512,128]{1,0:T(8,128)(2,1)S(1)}, u32[]{:S(2)}, u32[]{:S(2)}) collective-permute-start(bf16[512,128]{1,0:T(8,128)(2,1)S(1)} %get-tuple-element.34), channel_id=1, source_target_pairs={{0,16},{4,20},{8,24},{12,28},{16,0},{20,4},{24,8},{28,12},{1,17},{... | collective-permute-start | bytes 393224 | tf_op jit(solution)/shard_map/ppermute | solution.py:293
  75.6 1.1 %collective-permute-start.12 = (bf16[512,128]{1,0:T(8,128)(2,1)S(1)}, bf16[512,128]{1,0:T(8,128)(2,1)S(1)}, u32[]{:S(2)}, u32[]{:S(2)}) collective-permute-start(bf16[512,128]{1,0:T(8,128)(2,1)S(1)} %get-tuple-element.35), channel_id=1, source_target_pairs={{0,24},{4,28},{8,16},{12,20},{16,8},{20,12},{24,0},{28,4},{1,25},{... | collective-permute-start | bytes 393224 | tf_op jit(solution)/shard_map/ppermute | solution.py:293
  76.7 1.5 %collective-permute-start.17 = (bf16[512,128]{1,0:T(8,128)(2,1)S(1)}, bf16[512,128]{1,0:T(8,128)(2,1)S(1)}, u32[]{:S(2)}, u32[]{:S(2)}) collective-permute-start(bf16[512,128]{1,0:T(8,128)(2,1)S(1)} %get-tuple-element.32.refs_0_), channel_id=1, source_target_pairs={{0,2},{1,3},{2,0},{3,1},{4,6},{5,7},{6,4},{7,5},{8,10},{9,11},{10,... | collective-permute-start | bytes 393224 | tf_op jit(solution)/shard_map/ppermute | solution.py:293
  78.2 1.7 %collective-permute-done.10.refs_1_ = bf16[512,128]{1,0:T(8,128)(2,1)S(1)} collective-permute-done((bf16[512,128]{1,0:T(8,128)(2,1)S(1)}, bf16[512,128]{1,0:T(8,128)(2,1)S(1)}, u32[]{:S(2)}, u32[]{:S(2)}) %collective-permute-start.10) | collective-permute-done | bytes 131104 | tf_op jit(solution)/shard_map/ppermute | solution.py:293
  80.0 1.5 %collective-permute-start.18 = (bf16[512,128]{1,0:T(8,128)(2,1)S(1)}, bf16[512,128]{1,0:T(8,128)(2,1)S(1)}, u32[]{:S(2)}, u32[]{:S(2)}) collective-permute-start(bf16[512,128]{1,0:T(8,128)(2,1)S(1)} %collective-permute-done.10.refs_1_), channel_id=1, source_target_pairs={{0,2},{1,3},{2,0},{3,1},{4,6},{5,7},{6,4},{7,5},{8,10},{9,11},{10,... | collective-permute-start | bytes 393224 | tf_op jit(solution)/shard_map/ppermute | solution.py:293
  81.5 3.4 %collective-permute-done.11.refs_2_ = bf16[512,128]{1,0:T(8,128)(2,1)S(1)} collective-permute-done((bf16[512,128]{1,0:T(8,128)(2,1)S(1)}, bf16[512,128]{1,0:T(8,128)(2,1)S(1)}, u32[]{:S(2)}, u32[]{:S(2)}) %collective-permute-start.11) | collective-permute-done | bytes 131104 | tf_op jit(solution)/shard_map/ppermute | solution.py:293
  84.9 1.5 %collective-permute-start.19 = (bf16[512,128]{1,0:T(8,128)(2,1)S(1)}, bf16[512,128]{1,0:T(8,128)(2,1)S(1)}, u32[]{:S(2)}, u32[]{:S(2)}) collective-permute-start(bf16[512,128]{1,0:T(8,128)(2,1)S(1)} %collective-permute-done.11.refs_2_), channel_id=1, source_target_pairs={{0,2},{1,3},{2,0},{3,1},{4,6},{5,7},{6,4},{7,5},{8,10},{9,11},{10,... | collective-permute-start | bytes 393224 | tf_op jit(solution)/shard_map/ppermute | solution.py:293
  86.6 0.5 collective-permute-start.20
  87.7 3.5 %collective-permute-done.19.refs_10_ = bf16[512,128]{1,0:T(8,128)(2,1)S(1)} collective-permute-done((bf16[512,128]{1,0:T(8,128)(2,1)S(1)}, bf16[512,128]{1,0:T(8,128)(2,1)S(1)}, u32[]{:S(2)}, u32[]{:S(2)}) %collective-permute-start.19) | collective-permute-done | bytes 131104 | tf_op jit(solution)/shard_map/ppermute | solution.py:293
  91.7 1.9 %collective-permute-done.20.refs_11_ = bf16[512,128]{1,0:T(8,128)(2,1)S(1)} collective-permute-done((bf16[512,128]{1,0:T(8,128)(2,1)S(1)}, bf16[512,128]{1,0:T(8,128)(2,1)S(1)}, u32[]{:S(2)}, u32[]{:S(2)}) %collective-permute-start.20) | collective-permute-done | bytes 131104 | tf_op jit(solution)/shard_map/ppermute | solution.py:293
  93.6 1.3 %collective-permute-done.24.refs_15_ = bf16[512,128]{1,0:T(8,128)(2,1)S(1)} collective-permute-done((bf16[512,128]{1,0:T(8,128)(2,1)S(1)}, bf16[512,128]{1,0:T(8,128)(2,1)S(1)}, u32[]{:S(2)}, u32[]{:S(2)}) %collective-permute-start.24) | collective-permute-done | bytes 131104 | tf_op jit(solution)/shard_map/ppermute | solution.py:293
  95.0 3.3 %project.1 = bf16[512,512]{1,0:T(8,128)(2,1)} custom-call(s32[3]{0:T(128)S(1)} %copy-done.2, bf16[512,128]{1,0:T(8,128)(2,1)S(1)} %get-tuple-element.32.refs_0_, bf16[512,128]{1,0:T(8,128)(2,1)S(1)} %collective-permute-done.10.refs_1_, bf16[512,128]{1,0:T(8,128)(2,1)S(1)} %collective-permute-done.11.refs_2_, ...), custom_call_target="tpu_custom_call" | custom-call | tf_op jit(solution)/shard_map/project/pallas_call | solution.py:270
  (37 shorter events, 1.8 us)
Async XLA Ops:
  3.3 22.9 %collective-permute-start.1 = (bf16[1040,128]{1,0:T(8,128)(2,1)}, bf16[1040,128]{1,0:T(8,128)(2,1)S(1)}, u32[]{:S(2)}, u32[]{:S(2)}) collective-permute-start(bf16[1040,128]{1,0:T(8,128)(2,1)} %get-tuple-element.23), channel_id=1, source_target_pairs={{0,16},{4,20},{8,24},{12,28},{16,0},{20,4},{24,8},{28,12},{1,17},{... | collective-permute-start | bytes 798728 | tf_op jit(solution)/shard_map/ppermute | solution.py:293
  7.3 18.9 %collective-permute-start.2 = (bf16[1040,128]{1,0:T(8,128)(2,1)}, bf16[1040,128]{1,0:T(8,128)(2,1)S(1)}, u32[]{:S(2)}, u32[]{:S(2)}) collective-permute-start(bf16[1040,128]{1,0:T(8,128)(2,1)} %get-tuple-element.24), channel_id=1, source_target_pairs={{0,24},{4,28},{8,16},{12,20},{16,8},{20,12},{24,0},{28,4},{1,25},{... | collective-permute-start | bytes 798728 | tf_op jit(solution)/shard_map/ppermute | solution.py:293
  8.7 28.4 %collective-permute-start.3 = (bf16[1040,128]{1,0:T(8,128)(2,1)}, bf16[1040,128]{1,0:T(8,128)(2,1)S(1)}, u32[]{:S(2)}, u32[]{:S(2)}) collective-permute-start(bf16[1040,128]{1,0:T(8,128)(2,1)} %get-tuple-element.21.refs_1_), channel_id=1, source_target_pairs={{0,4},{4,0},{8,12},{12,8},{16,20},{20,16},{24,28},{28,24},{1,5},{5... | collective-permute-start | bytes 798728 | tf_op jit(solution)/shard_map/ppermute | solution.py:293
  10.2 27.5 %collective-permute-start = (bf16[1040,128]{1,0:T(8,128)(2,1)}, bf16[1040,128]{1,0:T(8,128)(2,1)S(1)}, u32[]{:S(2)}, u32[]{:S(2)}) collective-permute-start(bf16[1040,128]{1,0:T(8,128)(2,1)} %get-tuple-element.22), channel_id=1, source_target_pairs={{0,8},{4,12},{8,0},{12,4},{16,24},{20,28},{24,16},{28,20},{1,9},{5... | collective-permute-start | bytes 798728 | tf_op jit(solution)/shard_map/ppermute | solution.py:293
  26.2 12.8 %copy-start.3 = (bf16[512,128]{1,0:T(8,128)(2,1)S(1)}, bf16[512,128]{1,0:T(8,128)(2,1)}, u32[]{:S(2)}) copy-start(bf16[512,128]{1,0:T(8,128)(2,1)} %get-tuple-element.31) | copy-start | bytes 393220
  26.2 34.1 %copy-start = (bf16[1040,128]{1,0:T(8,128)(2,1)S(1)}, bf16[1040,128]{1,0:T(8,128)(2,1)}, u32[]{:S(2)}) copy-start(bf16[1040,128]{1,0:T(8,128)(2,1)} %get-tuple-element.21.refs_1_) | copy-start | bytes 798724
  26.2 34.1 %copy-start.1 = (bf16[512,128]{1,0:T(8,128)(2,1)S(1)}, bf16[512,128]{1,0:T(8,128)(2,1)}, u32[]{:S(2)}) copy-start(bf16[512,128]{1,0:T(8,128)(2,1)} %get-tuple-element.25.refs_9_) | copy-start | bytes 393220
  26.2 34.1 %copy-start.2 = (s32[3]{0:T(128)S(1)}, s32[3]{0:T(128)}, u32[]{:S(2)}) copy-start(s32[3]{0:T(128)} %pad_add_fusion.place_ref.refs_0_.where_ref) | copy-start | bytes 40
  26.3 12.5 %collective-permute-start.7 = (bf16[512,128]{1,0:T(8,128)(2,1)}, bf16[512,128]{1,0:T(8,128)(2,1)S(1)}, u32[]{:S(2)}, u32[]{:S(2)}) collective-permute-start(bf16[512,128]{1,0:T(8,128)(2,1)} %get-tuple-element.27), channel_id=1, source_target_pairs={{0,8},{4,12},{8,0},{12,4},{16,24},{20,28},{24,16},{28,20},{1,9},{5... | collective-permute-start | bytes 393224 | tf_op jit(solution)/shard_map/ppermute | solution.py:293
  32.0 7.0 %collective-permute-start.8 = (bf16[512,128]{1,0:T(8,128)(2,1)}, bf16[512,128]{1,0:T(8,128)(2,1)S(1)}, u32[]{:S(2)}, u32[]{:S(2)}) collective-permute-start(bf16[512,128]{1,0:T(8,128)(2,1)} %get-tuple-element.29), channel_id=1, source_target_pairs={{0,16},{4,20},{8,24},{12,28},{16,0},{20,4},{24,8},{28,12},{1,17},{... | collective-permute-start | bytes 393224 | tf_op jit(solution)/shard_map/ppermute | solution.py:293
  33.9 15.1 %collective-permute-start.5 = (bf16[1040,128]{1,0:T(8,128)(2,1)S(1)}, bf16[1040,128]{1,0:T(8,128)(2,1)S(1)}, u32[]{:S(2)}, u32[]{:S(2)}) collective-permute-start(bf16[1040,128]{1,0:T(8,128)(2,1)S(1)} %collective-permute-done.1.refs_3_), channel_id=1, source_target_pairs={{0,4},{4,0},{8,12},{12,8},{16,20},{20,16},{24,28},{28,24},{1,5},{5... | collective-permute-start | bytes 798728 | tf_op jit(solution)/shard_map/ppermute | solution.py:293
  37.1 38.6 %collective-permute-start.27 = (bf16[512,512]{1,0:T(8,128)(2,1)S(1)}, bf16[512,512]{1,0:T(8,128)(2,1)S(1)}, u32[]{:S(2)}, u32[]{:S(2)}) collective-permute-start(bf16[512,512]{1,0:T(8,128)(2,1)S(1)} %get-tuple-element.37), channel_id=1, source_target_pairs={{0,3},{1,2},{2,1},{3,0},{4,7},{5,6},{6,5},{7,4},{8,11},{9,10},{10,... | collective-permute-start | bytes 1572872 | tf_op jit(solution)/shard_map/ppermute | solution.py:293
  37.7 39.0 %collective-permute-start.26 = (bf16[512,512]{1,0:T(8,128)(2,1)S(1)}, bf16[512,512]{1,0:T(8,128)(2,1)S(1)}, u32[]{:S(2)}, u32[]{:S(2)}) collective-permute-start(bf16[512,512]{1,0:T(8,128)(2,1)S(1)} %get-tuple-element.38), channel_id=1, source_target_pairs={{0,2},{1,3},{2,0},{3,1},{4,6},{5,7},{6,4},{7,5},{8,10},{9,11},{10,... | collective-permute-start | bytes 1572872 | tf_op jit(solution)/shard_map/ppermute | solution.py:293
  38.8 39.5 %collective-permute-start.25 = (bf16[512,512]{1,0:T(8,128)(2,1)S(1)}, bf16[512,512]{1,0:T(8,128)(2,1)S(1)}, u32[]{:S(2)}, u32[]{:S(2)}) collective-permute-start(bf16[512,512]{1,0:T(8,128)(2,1)S(1)} %get-tuple-element.39), channel_id=1, source_target_pairs={{0,1},{1,0},{2,3},{3,2},{4,5},{5,4},{6,7},{7,6},{8,9},{9,8},{10,11... | collective-permute-start | bytes 1572872 | tf_op jit(solution)/shard_map/ppermute | solution.py:293
  39.0 8.4 %collective-permute-start.9 = (bf16[512,128]{1,0:T(8,128)(2,1)S(1)}, bf16[512,128]{1,0:T(8,128)(2,1)S(1)}, u32[]{:S(2)}, u32[]{:S(2)}) collective-permute-start(bf16[512,128]{1,0:T(8,128)(2,1)S(1)} %copy-done.3), channel_id=1, source_target_pairs={{0,24},{4,28},{8,16},{12,20},{16,8},{20,12},{24,0},{28,4},{1,25},{... | collective-permute-start | bytes 393224 | tf_op jit(solution)/shard_map/ppermute | solution.py:293
  47.5 9.3 %collective-permute-start.6 = (bf16[1040,128]{1,0:T(8,128)(2,1)S(1)}, bf16[1040,128]{1,0:T(8,128)(2,1)S(1)}, u32[]{:S(2)}, u32[]{:S(2)}) collective-permute-start(bf16[1040,128]{1,0:T(8,128)(2,1)S(1)} %collective-permute-done.2.refs_4_), channel_id=1, source_target_pairs={{0,4},{4,0},{8,12},{12,8},{16,20},{20,16},{24,28},{28,24},{1,5},{5... | collective-permute-start | bytes 798728 | tf_op jit(solution)/shard_map/ppermute | solution.py:293
  49.0 11.3 %collective-permute-start.4 = (bf16[1040,128]{1,0:T(8,128)(2,1)S(1)}, bf16[1040,128]{1,0:T(8,128)(2,1)S(1)}, u32[]{:S(2)}, u32[]{:S(2)}) collective-permute-start(bf16[1040,128]{1,0:T(8,128)(2,1)S(1)} %collective-permute-done.refs_2_), channel_id=1, source_target_pairs={{0,4},{4,0},{8,12},{12,8},{16,20},{20,16},{24,28},{28,24},{1,5},{5... | collective-permute-start | bytes 798728 | tf_op jit(solution)/shard_map/ppermute | solution.py:293
  72.0 8.0 %collective-permute-start.10 = (bf16[512,128]{1,0:T(8,128)(2,1)S(1)}, bf16[512,128]{1,0:T(8,128)(2,1)S(1)}, u32[]{:S(2)}, u32[]{:S(2)}) collective-permute-start(bf16[512,128]{1,0:T(8,128)(2,1)S(1)} %get-tuple-element.33), channel_id=1, source_target_pairs={{0,8},{4,12},{8,0},{12,4},{16,24},{20,28},{24,16},{28,20},{1,9},{5... | collective-permute-start | bytes 393224 | tf_op jit(solution)/shard_map/ppermute | solution.py:293
  74.3 10.6 %collective-permute-start.11 = (bf16[512,128]{1,0:T(8,128)(2,1)S(1)}, bf16[512,128]{1,0:T(8,128)(2,1)S(1)}, u32[]{:S(2)}, u32[]{:S(2)}) collective-permute-start(bf16[512,128]{1,0:T(8,128)(2,1)S(1)} %get-tuple-element.34), channel_id=1, source_target_pairs={{0,16},{4,20},{8,24},{12,28},{16,0},{20,4},{24,8},{28,12},{1,17},{... | collective-permute-start | bytes 393224 | tf_op jit(solution)/shard_map/ppermute | solution.py:293
  75.6 9.2 %collective-permute-start.12 = (bf16[512,128]{1,0:T(8,128)(2,1)S(1)}, bf16[512,128]{1,0:T(8,128)(2,1)S(1)}, u32[]{:S(2)}, u32[]{:S(2)}) collective-permute-start(bf16[512,128]{1,0:T(8,128)(2,1)S(1)} %get-tuple-element.35), channel_id=1, source_target_pairs={{0,24},{4,28},{8,16},{12,20},{16,8},{20,12},{24,0},{28,4},{1,25},{... | collective-permute-start | bytes 393224 | tf_op jit(solution)/shard_map/ppermute | solution.py:293
  76.7 9.7 %collective-permute-start.17 = (bf16[512,128]{1,0:T(8,128)(2,1)S(1)}, bf16[512,128]{1,0:T(8,128)(2,1)S(1)}, u32[]{:S(2)}, u32[]{:S(2)}) collective-permute-start(bf16[512,128]{1,0:T(8,128)(2,1)S(1)} %get-tuple-element.32.refs_0_), channel_id=1, source_target_pairs={{0,2},{1,3},{2,0},{3,1},{4,6},{5,7},{6,4},{7,5},{8,10},{9,11},{10,... | collective-permute-start | bytes 393224 | tf_op jit(solution)/shard_map/ppermute | solution.py:293
  78.2 8.4 %collective-permute-start.13 = (bf16[512,128]{1,0:T(8,128)(2,1)S(1)}, bf16[512,128]{1,0:T(8,128)(2,1)S(1)}, u32[]{:S(2)}, u32[]{:S(2)}) collective-permute-start(bf16[512,128]{1,0:T(8,128)(2,1)S(1)} %get-tuple-element.32.refs_0_), channel_id=1, source_target_pairs={{0,1},{1,0},{2,3},{3,2},{4,5},{5,4},{6,7},{7,6},{8,9},{9,8},{10,11... | collective-permute-start | bytes 393224 | tf_op jit(solution)/shard_map/ppermute | solution.py:293
  80.0 7.2 %collective-permute-start.18 = (bf16[512,128]{1,0:T(8,128)(2,1)S(1)}, bf16[512,128]{1,0:T(8,128)(2,1)S(1)}, u32[]{:S(2)}, u32[]{:S(2)}) collective-permute-start(bf16[512,128]{1,0:T(8,128)(2,1)S(1)} %collective-permute-done.10.refs_1_), channel_id=1, source_target_pairs={{0,2},{1,3},{2,0},{3,1},{4,6},{5,7},{6,4},{7,5},{8,10},{9,11},{10,... | collective-permute-start | bytes 393224 | tf_op jit(solution)/shard_map/ppermute | solution.py:293
  84.9 2.3 %collective-permute-start.14 = (bf16[512,128]{1,0:T(8,128)(2,1)S(1)}, bf16[512,128]{1,0:T(8,128)(2,1)S(1)}, u32[]{:S(2)}, u32[]{:S(2)}) collective-permute-start(bf16[512,128]{1,0:T(8,128)(2,1)S(1)} %collective-permute-done.10.refs_1_), channel_id=1, source_target_pairs={{0,1},{1,0},{2,3},{3,2},{4,5},{5,4},{6,7},{7,6},{8,9},{9,8},{10,11... | collective-permute-start | bytes 393224 | tf_op jit(solution)/shard_map/ppermute | solution.py:293
  84.9 6.3 %collective-permute-start.19 = (bf16[512,128]{1,0:T(8,128)(2,1)S(1)}, bf16[512,128]{1,0:T(8,128)(2,1)S(1)}, u32[]{:S(2)}, u32[]{:S(2)}) collective-permute-start(bf16[512,128]{1,0:T(8,128)(2,1)S(1)} %collective-permute-done.11.refs_2_), channel_id=1, source_target_pairs={{0,2},{1,3},{2,0},{3,1},{4,6},{5,7},{6,4},{7,5},{8,10},{9,11},{10,... | collective-permute-start | bytes 393224 | tf_op jit(solution)/shard_map/ppermute | solution.py:293
  86.4 4.8 %collective-permute-start.15 = (bf16[512,128]{1,0:T(8,128)(2,1)S(1)}, bf16[512,128]{1,0:T(8,128)(2,1)S(1)}, u32[]{:S(2)}, u32[]{:S(2)}) collective-permute-start(bf16[512,128]{1,0:T(8,128)(2,1)S(1)} %collective-permute-done.11.refs_2_), channel_id=1, source_target_pairs={{0,1},{1,0},{2,3},{3,2},{4,5},{5,4},{6,7},{7,6},{8,9},{9,8},{10,11... | collective-permute-start | bytes 393224 | tf_op jit(solution)/shard_map/ppermute | solution.py:293
  86.6 7.0 %collective-permute-start.20 = (bf16[512,128]{1,0:T(8,128)(2,1)S(1)}, bf16[512,128]{1,0:T(8,128)(2,1)S(1)}, u32[]{:S(2)}, u32[]{:S(2)}) collective-permute-start(bf16[512,128]{1,0:T(8,128)(2,1)S(1)} %collective-permute-done.12.refs_3_), channel_id=1, source_target_pairs={{0,2},{1,3},{2,0},{3,1},{4,6},{5,7},{6,4},{7,5},{8,10},{9,11},{10,... | collective-permute-start | bytes 393224 | tf_op jit(solution)/shard_map/ppermute | solution.py:293
  87.2 6.5 %collective-permute-start.16 = (bf16[512,128]{1,0:T(8,128)(2,1)S(1)}, bf16[512,128]{1,0:T(8,128)(2,1)S(1)}, u32[]{:S(2)}, u32[]{:S(2)}) collective-permute-start(bf16[512,128]{1,0:T(8,128)(2,1)S(1)} %collective-permute-done.12.refs_3_), channel_id=1, source_target_pairs={{0,1},{1,0},{2,3},{3,2},{4,5},{5,4},{6,7},{7,6},{8,9},{9,8},{10,11... | collective-permute-start | bytes 393224 | tf_op jit(solution)/shard_map/ppermute | solution.py:293
  87.2 6.5 %collective-permute-start.21 = (bf16[512,128]{1,0:T(8,128)(2,1)S(1)}, bf16[512,128]{1,0:T(8,128)(2,1)S(1)}, u32[]{:S(2)}, u32[]{:S(2)}) collective-permute-start(bf16[512,128]{1,0:T(8,128)(2,1)S(1)} %collective-permute-done.17.refs_8_), channel_id=1, source_target_pairs={{0,1},{1,0},{2,3},{3,2},{4,5},{5,4},{6,7},{7,6},{8,9},{9,8},{10,11... | collective-permute-start | bytes 393224 | tf_op jit(solution)/shard_map/ppermute | solution.py:293
  91.2 2.4 %collective-permute-start.22 = (bf16[512,128]{1,0:T(8,128)(2,1)S(1)}, bf16[512,128]{1,0:T(8,128)(2,1)S(1)}, u32[]{:S(2)}, u32[]{:S(2)}) collective-permute-start(bf16[512,128]{1,0:T(8,128)(2,1)S(1)} %collective-permute-done.18.refs_9_), channel_id=1, source_target_pairs={{0,1},{1,0},{2,3},{3,2},{4,5},{5,4},{6,7},{7,6},{8,9},{9,8},{10,11... | collective-permute-start | bytes 393224 | tf_op jit(solution)/shard_map/ppermute | solution.py:293
  91.2 2.4 %collective-permute-start.23 = (bf16[512,128]{1,0:T(8,128)(2,1)S(1)}, bf16[512,128]{1,0:T(8,128)(2,1)S(1)}, u32[]{:S(2)}, u32[]{:S(2)}) collective-permute-start(bf16[512,128]{1,0:T(8,128)(2,1)S(1)} %collective-permute-done.19.refs_10_), channel_id=1, source_target_pairs={{0,1},{1,0},{2,3},{3,2},{4,5},{5,4},{6,7},{7,6},{8,9},{9,8},{10,11... | collective-permute-start | bytes 393224 | tf_op jit(solution)/shard_map/ppermute | solution.py:293
  93.6 1.3 %collective-permute-start.24 = (bf16[512,128]{1,0:T(8,128)(2,1)S(1)}, bf16[512,128]{1,0:T(8,128)(2,1)S(1)}, u32[]{:S(2)}, u32[]{:S(2)}) collective-permute-start(bf16[512,128]{1,0:T(8,128)(2,1)S(1)} %collective-permute-done.20.refs_11_), channel_id=1, source_target_pairs={{0,1},{1,0},{2,3},{3,2},{4,5},{5,4},{6,7},{7,6},{8,9},{9,8},{10,11... | collective-permute-start | bytes 393224 | tf_op jit(solution)/shard_map/ppermute | solution.py:293

commit v2 on v1

--- a/solution.py
+++ b/solution.py
@@ -297,9 +297,10 @@
 
     q, kv = pack(where, queries, keys, values, cluster_ids)
     kv_own, kv_far, q_own = [kv[0]] + [None] * 3, [None] * 4, [q[0]] + [None] * 3
-    for offset in (2, 3, 1):
-        kv_own[offset] = swap(kv[offset], "seq", 2 * offset)
+    kv_own[2] = swap(kv[2], "seq", 4)
+    kv_own[1] = swap(kv[1], "seq", 2)
     kv_far[0] = swap(kv[0], "seq", 1)
+    kv_own[3] = swap(after(kv[3], kv_own[1]), "seq", 6)
     columns = out_weight.shape[1] // 4
     weights = []
     late_weight = after(out_weight, kv[1])
@@ -308,8 +309,9 @@
         weights.append(swap(block, "head", far) if far else block)
     for offset in (1, 2, 3):
         kv_far[offset] = swap(kv_own[offset], "seq", 1)
-    for offset in (2, 3, 1):
-        q_own[offset] = swap(after(q[offset], kv_own[2], kv_own[3]), "seq", 2 * offset)
+    q_own[2] = swap(after(q[2], kv_own[2]), "seq", 4)
+    for offset in (3, 1):
+        q_own[offset] = swap(after(q[offset], kv_own[3]), "seq", 2 * offset)
     attended = list(attend(where, kv_own, kv_far, q_own))
     for offset in range(1, heads):
         attended[offset] = swap(attended[offset], "seq", 2 * offset)

time: 98.4 us -> 88.9 us (0.903)
  starting transfers between devices: 36.4 us -> 30.6 us
  waiting for transfers between devices: 41.8 us -> 37.9 us
    ppermute x28, starting transfers between devices: 36.4 us -> 30.6 us  [swap(): lax.ppermute(array, axis, [(place, place ^ bits) for place in range(size)])]
    ppermute x28, waiting for transfers between devices: 41.8 us -> 37.9 us  [swap(): lax.ppermute(array, axis, [(place, place ^ bits) for place in range(size)])]
  transfers between devices with their start and end apart: 28 -> 28, of which waited for: 9 -> 9; matrix products, arithmetic and copies ran while one was open for 2% -> 2% of each run, Pallas kernels for 12% -> 13%
where the time goes in v2:
time: 88.9 us; the launch traced here: 88.7 us
  waiting for transfers between devices  37.9 us (43%)
  starting transfers between devices  30.6 us (34%)
  Pallas kernels  17.7 us (20%)
  local copies, waits for them, and re-layouts  1.69 us (2%)
    ppermute x28, waiting for transfers between devices, swap(): lax.ppermute(array, axis, [(place, place ^ bits) for place in range(size)])  37.9 us
    ppermute x28, starting transfers between devices, swap(): lax.ppermute(array, axis, [(place, place ^ bits) for place in range(size)])  30.6 us
    pallas_call x1, Pallas kernels, attend(): pl.pallas_call(lambda *refs: attend_kernel(1.0 / math.sqrt(width), *refs)...  11.7 us
    pallas_call x1, Pallas kernels, project(): pl.pallas_call(project_kernel, out_shape=jax.ShapeDtypeStruct((rows, weig...  3.33 us
    pallas_call x1, Pallas kernels, pack(): pl.pallas_call(pack_kernel, out_shape=tuple(pair * heads), in_specs=[pl.B...  2.73 us
  transfers between devices with their start and end apart: 28, of which 9 were waited for; matrix products, arithmetic and copies ran while one was open for 2% of the time, Pallas kernels for 13%

profile of v2, /device:TPU:0, one launch (start us, length us, event | category | flops | bytes accessed | tf_op | source)
XLA Modules:
  0.0 88.7 jit_solution(1104857664316354976)
XLA Ops:
  0.0 0.7 pad_add_fusion.place_ref.refs_0_.where_ref
  0.7 2.7 %pack.1 = (bf16[512,128]{1,0:T(8,128)(2,1)}, bf16[1040,128]{1,0:T(8,128)(2,1)}, bf16[512,128]{1,0:T(8,128)(2,1)}, bf16[1040,128]{1,0:T(8,128)(2,1)}, bf16[512,12...) custom-call(s32[3]{0:T(128)} %pad_add_fusion.place_ref.refs_0_.where_ref, ...), custom_call_target="tpu_custom_call" | custom-call | tf_op jit(solution)/shard_map/pack/pallas_call | solution.py:121
  3.4 4.0 %collective-permute-start.1 = (bf16[1040,128]{1,0:T(8,128)(2,1)}, bf16[1040,128]{1,0:T(8,128)(2,1)S(1)}, u32[]{:S(2)}, u32[]{:S(2)}) collective-permute-start(bf16[1040,128]{1,0:T(8,128)(2,1)} %get-tuple-element.24), channel_id=1, source_target_pairs={{0,16},{4,20},{8,24},{12,28},{16,0},{20,4},{24,8},{28,12},{1,17},{... | collective-permute-start | bytes 798728 | tf_op jit(solution)/shard_map/ppermute | solution.py:293
  7.4 1.6 %collective-permute-start = (bf16[1040,128]{1,0:T(8,128)(2,1)}, bf16[1040,128]{1,0:T(8,128)(2,1)S(1)}, u32[]{:S(2)}, u32[]{:S(2)}) collective-permute-start(bf16[1040,128]{1,0:T(8,128)(2,1)} %get-tuple-element.23), channel_id=1, source_target_pairs={{0,8},{4,12},{8,0},{12,4},{16,24},{20,28},{24,16},{28,20},{1,9},{5... | collective-permute-start | bytes 798728 | tf_op jit(solution)/shard_map/ppermute | solution.py:293
  9.0 1.5 %collective-permute-start.3 = (bf16[1040,128]{1,0:T(8,128)(2,1)}, bf16[1040,128]{1,0:T(8,128)(2,1)S(1)}, u32[]{:S(2)}, u32[]{:S(2)}) collective-permute-start(bf16[1040,128]{1,0:T(8,128)(2,1)} %get-tuple-element.22.refs_1_), channel_id=1, source_target_pairs={{0,4},{4,0},{8,12},{12,8},{16,20},{20,16},{24,28},{28,24},{1,5},{5... | collective-permute-start | bytes 798728 | tf_op jit(solution)/shard_map/ppermute | solution.py:293
  10.5 9.3 %collective-permute-done.1.refs_3_ = bf16[1040,128]{1,0:T(8,128)(2,1)S(1)} collective-permute-done((bf16[1040,128]{1,0:T(8,128)(2,1)}, bf16[1040,128]{1,0:T(8,128)(2,1)S(1)}, u32[]{:S(2)}, u32[]{:S(2)}) %collective-permute-start.1) | collective-permute-done | bytes 266272 | tf_op jit(solution)/shard_map/ppermute | solution.py:293
  19.8 1.5 %collective-permute-start.5 = (bf16[1040,128]{1,0:T(8,128)(2,1)S(1)}, bf16[1040,128]{1,0:T(8,128)(2,1)S(1)}, u32[]{:S(2)}, u32[]{:S(2)}) collective-permute-start(bf16[1040,128]{1,0:T(8,128)(2,1)S(1)} %collective-permute-done.1.refs_3_), channel_id=1, source_target_pairs={{0,4},{4,0},{8,12},{12,8},{16,20},{20,16},{24,28},{28,24},{1,5},{5... | collective-permute-start | bytes 798728 | tf_op jit(solution)/shard_map/ppermute | solution.py:293
  21.4 3.4 %collective-permute-start.2 = (bf16[1040,128]{1,0:T(8,128)(2,1)}, bf16[1040,128]{1,0:T(8,128)(2,1)S(1)}, u32[]{:S(2)}, u32[]{:S(2)}) collective-permute-start(bf16[1040,128]{1,0:T(8,128)(2,1)} %get-tuple-element.26), channel_id=1, source_target_pairs={{0,24},{4,28},{8,16},{12,20},{16,8},{20,12},{24,0},{28,4},{1,25},{... | collective-permute-start | bytes 798728 | tf_op jit(solution)/shard_map/ppermute | solution.py:293
  24.9 0.5 collective-permute-start.4
  25.4 1.7 %constant_dynamic-slice_fusion = (bf16[512,512]{1,0:T(8,128)(2,1)S(1)}, bf16[512,512]{1,0:T(8,128)(2,1)S(1)}, bf16[512,512]{1,0:T(8,128)(2,1)S(1)}, bf16[512,512]{1,0:T(8,128)(2,1)S(1)}) fusion(bf16[512,2048]{1,0:T(8,128)(2,1)} %param.9, s32[]{:T(128)S(6)} %select_n.28, s32[]{:T(128)S(6)} %select_n.27, s32[]{:T(128)S(6)} %select_n.26, s32[]{:T(128)S(6)} %select_n.25), kind=kLoop, calls=%fused_computation | loop fusion | bytes 4194320 | tf_op jit(solution)/shard_map/dynamic_slice | solution.py:308
  27.5 9.3 %collective-permute-done.8.refs_11_ = bf16[512,128]{1,0:T(8,128)(2,1)S(1)} collective-permute-done((bf16[512,128]{1,0:T(8,128)(2,1)}, bf16[512,128]{1,0:T(8,128)(2,1)S(1)}, u32[]{:S(2)}, u32[]{:S(2)}) %collective-permute-start.8) | collective-permute-done | bytes 131104 | tf_op jit(solution)/shard_map/ppermute | solution.py:293
  36.8 1.5 %collective-permute-start.26 = (bf16[512,512]{1,0:T(8,128)(2,1)S(1)}, bf16[512,512]{1,0:T(8,128)(2,1)S(1)}, u32[]{:S(2)}, u32[]{:S(2)}) collective-permute-start(bf16[512,512]{1,0:T(8,128)(2,1)S(1)} %get-tuple-element.40), channel_id=1, source_target_pairs={{0,2},{1,3},{2,0},{3,1},{4,6},{5,7},{6,4},{7,5},{8,10},{9,11},{10,... | collective-permute-start | bytes 1572872 | tf_op jit(solution)/shard_map/ppermute | solution.py:293
  38.3 0.6 collective-permute-start.6
  38.9 3.4 %collective-permute-start.7 = (bf16[512,128]{1,0:T(8,128)(2,1)S(1)}, bf16[512,128]{1,0:T(8,128)(2,1)S(1)}, u32[]{:S(2)}, u32[]{:S(2)}) collective-permute-start(bf16[512,128]{1,0:T(8,128)(2,1)S(1)} %copy-done.4), channel_id=1, source_target_pairs={{0,8},{4,12},{8,0},{12,4},{16,24},{20,28},{24,16},{28,20},{1,9},{5... | collective-permute-start | bytes 393224 | tf_op jit(solution)/shard_map/ppermute | solution.py:293
  42.3 2.9 %collective-permute-done.7.refs_10_ = bf16[512,128]{1,0:T(8,128)(2,1)S(1)} collective-permute-done((bf16[512,128]{1,0:T(8,128)(2,1)S(1)}, bf16[512,128]{1,0:T(8,128)(2,1)S(1)}, u32[]{:S(2)}, u32[]{:S(2)}) %collective-permute-start.7) | collective-permute-done | bytes 131104 | tf_op jit(solution)/shard_map/ppermute | solution.py:293
  45.2 1.3 %collective-permute-start.9 = (bf16[512,128]{1,0:T(8,128)(2,1)S(1)}, bf16[512,128]{1,0:T(8,128)(2,1)S(1)}, u32[]{:S(2)}, u32[]{:S(2)}) collective-permute-start(bf16[512,128]{1,0:T(8,128)(2,1)S(1)} %copy-done.3), channel_id=1, source_target_pairs={{0,24},{4,28},{8,16},{12,20},{16,8},{20,12},{24,0},{28,4},{1,25},{... | collective-permute-start | bytes 393224 | tf_op jit(solution)/shard_map/ppermute | solution.py:293
  46.6 5.5 %collective-permute-done.9.refs_12_ = bf16[512,128]{1,0:T(8,128)(2,1)S(1)} collective-permute-done((bf16[512,128]{1,0:T(8,128)(2,1)S(1)}, bf16[512,128]{1,0:T(8,128)(2,1)S(1)}, u32[]{:S(2)}, u32[]{:S(2)}) %collective-permute-start.9) | collective-permute-done | bytes 131104 | tf_op jit(solution)/shard_map/ppermute | solution.py:293
  52.1 11.7 %attend.1 = (bf16[512,128]{1,0:T(8,128)(2,1)S(1)}, bf16[512,128]{1,0:T(8,128)(2,1)S(1)}, bf16[512,128]{1,0:T(8,128)(2,1)S(1)}, bf16[512,128]{1,0:T(8,128)(2,1)S(1)}) custom-call(s32[3]{0:T(128)S(1)} %copy-done.2, bf16[1040,128]{1,0:T(8,128)(2,1)S(1)} %copy-done, bf16[1040,128]{1,0:T(8,128)(2,1)S(1)} %collective-permute-done.refs_2_, ...), custom_call_target="tpu_custom_call" | custom-call | tf_op jit(solution)/shard_map/attend/pallas_call | solution.py:220
  63.8 1.6 %collective-permute-start.10 = (bf16[512,128]{1,0:T(8,128)(2,1)S(1)}, bf16[512,128]{1,0:T(8,128)(2,1)S(1)}, u32[]{:S(2)}, u32[]{:S(2)}) collective-permute-start(bf16[512,128]{1,0:T(8,128)(2,1)S(1)} %get-tuple-element.35), channel_id=1, source_target_pairs={{0,8},{4,12},{8,0},{12,4},{16,24},{20,28},{24,16},{28,20},{1,9},{5... | collective-permute-start | bytes 393224 | tf_op jit(solution)/shard_map/ppermute | solution.py:293
  65.8 2.5 %collective-permute-start.12 = (bf16[512,128]{1,0:T(8,128)(2,1)S(1)}, bf16[512,128]{1,0:T(8,128)(2,1)S(1)}, u32[]{:S(2)}, u32[]{:S(2)}) collective-permute-start(bf16[512,128]{1,0:T(8,128)(2,1)S(1)} %get-tuple-element.37), channel_id=1, source_target_pairs={{0,24},{4,28},{8,16},{12,20},{16,8},{20,12},{24,0},{28,4},{1,25},{... | collective-permute-start | bytes 393224 | tf_op jit(solution)/shard_map/ppermute | solution.py:293
  68.3 1.5 %collective-permute-start.17 = (bf16[512,128]{1,0:T(8,128)(2,1)S(1)}, bf16[512,128]{1,0:T(8,128)(2,1)S(1)}, u32[]{:S(2)}, u32[]{:S(2)}) collective-permute-start(bf16[512,128]{1,0:T(8,128)(2,1)S(1)} %get-tuple-element.34.refs_0_), channel_id=1, source_target_pairs={{0,2},{1,3},{2,0},{3,1},{4,6},{5,7},{6,4},{7,5},{8,10},{9,11},{10,... | collective-permute-start | bytes 393224 | tf_op jit(solution)/shard_map/ppermute | solution.py:293
  69.8 1.4 %collective-permute-done.10.refs_1_ = bf16[512,128]{1,0:T(8,128)(2,1)S(1)} collective-permute-done((bf16[512,128]{1,0:T(8,128)(2,1)S(1)}, bf16[512,128]{1,0:T(8,128)(2,1)S(1)}, u32[]{:S(2)}, u32[]{:S(2)}) %collective-permute-start.10) | collective-permute-done | bytes 131104 | tf_op jit(solution)/shard_map/ppermute | solution.py:293
  71.1 1.6 %collective-permute-start.18 = (bf16[512,128]{1,0:T(8,128)(2,1)S(1)}, bf16[512,128]{1,0:T(8,128)(2,1)S(1)}, u32[]{:S(2)}, u32[]{:S(2)}) collective-permute-start(bf16[512,128]{1,0:T(8,128)(2,1)S(1)} %collective-permute-done.10.refs_1_), channel_id=1, source_target_pairs={{0,2},{1,3},{2,0},{3,1},{4,6},{5,7},{6,4},{7,5},{8,10},{9,11},{10,... | collective-permute-start | bytes 393224 | tf_op jit(solution)/shard_map/ppermute | solution.py:293
  72.7 2.6 %collective-permute-done.11.refs_2_ = bf16[512,128]{1,0:T(8,128)(2,1)S(1)} collective-permute-done((bf16[512,128]{1,0:T(8,128)(2,1)S(1)}, bf16[512,128]{1,0:T(8,128)(2,1)S(1)}, u32[]{:S(2)}, u32[]{:S(2)}) %collective-permute-start.11) | collective-permute-done | bytes 131104 | tf_op jit(solution)/shard_map/ppermute | solution.py:293
  75.3 1.5 %collective-permute-start.19 = (bf16[512,128]{1,0:T(8,128)(2,1)S(1)}, bf16[512,128]{1,0:T(8,128)(2,1)S(1)}, u32[]{:S(2)}, u32[]{:S(2)}) collective-permute-start(bf16[512,128]{1,0:T(8,128)(2,1)S(1)} %collective-permute-done.11.refs_2_), channel_id=1, source_target_pairs={{0,2},{1,3},{2,0},{3,1},{4,6},{5,7},{6,4},{7,5},{8,10},{9,11},{10,... | collective-permute-start | bytes 393224 | tf_op jit(solution)/shard_map/ppermute | solution.py:293
  77.1 0.5 collective-permute-start.20
  77.6 0.5 collective-permute-start.21
  78.1 3.5 %collective-permute-done.19.refs_10_ = bf16[512,128]{1,0:T(8,128)(2,1)S(1)} collective-permute-done((bf16[512,128]{1,0:T(8,128)(2,1)S(1)}, bf16[512,128]{1,0:T(8,128)(2,1)S(1)}, u32[]{:S(2)}, u32[]{:S(2)}) %collective-permute-start.19) | collective-permute-done | bytes 131104 | tf_op jit(solution)/shard_map/ppermute | solution.py:293
  81.6 0.5 collective-permute-start.23
  82.1 1.9 %collective-permute-done.20.refs_11_ = bf16[512,128]{1,0:T(8,128)(2,1)S(1)} collective-permute-done((bf16[512,128]{1,0:T(8,128)(2,1)S(1)}, bf16[512,128]{1,0:T(8,128)(2,1)S(1)}, u32[]{:S(2)}, u32[]{:S(2)}) %collective-permute-start.20) | collective-permute-done | bytes 131104 | tf_op jit(solution)/shard_map/ppermute | solution.py:293
  84.1 1.3 %collective-permute-done.24.refs_15_ = bf16[512,128]{1,0:T(8,128)(2,1)S(1)} collective-permute-done((bf16[512,128]{1,0:T(8,128)(2,1)S(1)}, bf16[512,128]{1,0:T(8,128)(2,1)S(1)}, u32[]{:S(2)}, u32[]{:S(2)}) %collective-permute-start.24) | collective-permute-done | bytes 131104 | tf_op jit(solution)/shard_map/ppermute | solution.py:293
  85.4 3.3 %project.1 = bf16[512,512]{1,0:T(8,128)(2,1)} custom-call(s32[3]{0:T(128)S(1)} %copy-done.2, bf16[512,128]{1,0:T(8,128)(2,1)S(1)} %get-tuple-element.34.refs_0_, bf16[512,128]{1,0:T(8,128)(2,1)S(1)} %collective-permute-done.10.refs_1_, bf16[512,128]{1,0:T(8,128)(2,1)S(1)} %collective-permute-done.11.refs_2_, ...), custom_call_target="tpu_custom_call" | custom-call | tf_op jit(solution)/shard_map/project/pallas_call | solution.py:270
  (39 shorter events, 1.1 us)
Async XLA Ops:
  3.4 16.5 %collective-permute-start.1 = (bf16[1040,128]{1,0:T(8,128)(2,1)}, bf16[1040,128]{1,0:T(8,128)(2,1)S(1)}, u32[]{:S(2)}, u32[]{:S(2)}) collective-permute-start(bf16[1040,128]{1,0:T(8,128)(2,1)} %get-tuple-element.24), channel_id=1, source_target_pairs={{0,16},{4,20},{8,24},{12,28},{16,0},{20,4},{24,8},{28,12},{1,17},{... | collective-permute-start | bytes 798728 | tf_op jit(solution)/shard_map/ppermute | solution.py:293
  7.4 14.0 %collective-permute-start = (bf16[1040,128]{1,0:T(8,128)(2,1)}, bf16[1040,128]{1,0:T(8,128)(2,1)S(1)}, u32[]{:S(2)}, u32[]{:S(2)}) collective-permute-start(bf16[1040,128]{1,0:T(8,128)(2,1)} %get-tuple-element.23), channel_id=1, source_target_pairs={{0,8},{4,12},{8,0},{12,4},{16,24},{20,28},{24,16},{28,20},{1,9},{5... | collective-permute-start | bytes 798728 | tf_op jit(solution)/shard_map/ppermute | solution.py:293
  9.0 18.1 %collective-permute-start.3 = (bf16[1040,128]{1,0:T(8,128)(2,1)}, bf16[1040,128]{1,0:T(8,128)(2,1)S(1)}, u32[]{:S(2)}, u32[]{:S(2)}) collective-permute-start(bf16[1040,128]{1,0:T(8,128)(2,1)} %get-tuple-element.22.refs_1_), channel_id=1, source_target_pairs={{0,4},{4,0},{8,12},{12,8},{16,20},{20,16},{24,28},{28,24},{1,5},{5... | collective-permute-start | bytes 798728 | tf_op jit(solution)/shard_map/ppermute | solution.py:293
  19.8 18.5 %collective-permute-start.5 = (bf16[1040,128]{1,0:T(8,128)(2,1)S(1)}, bf16[1040,128]{1,0:T(8,128)(2,1)S(1)}, u32[]{:S(2)}, u32[]{:S(2)}) collective-permute-start(bf16[1040,128]{1,0:T(8,128)(2,1)S(1)} %collective-permute-done.1.refs_3_), channel_id=1, source_target_pairs={{0,4},{4,0},{8,12},{12,8},{16,20},{20,16},{24,28},{28,24},{1,5},{5... | collective-permute-start | bytes 798728 | tf_op jit(solution)/shard_map/ppermute | solution.py:293
  21.4 15.4 %collective-permute-start.8 = (bf16[512,128]{1,0:T(8,128)(2,1)}, bf16[512,128]{1,0:T(8,128)(2,1)S(1)}, u32[]{:S(2)}, u32[]{:S(2)}) collective-permute-start(bf16[512,128]{1,0:T(8,128)(2,1)} %get-tuple-element.31), channel_id=1, source_target_pairs={{0,16},{4,20},{8,24},{12,28},{16,0},{20,4},{24,8},{28,12},{1,17},{... | collective-permute-start | bytes 393224 | tf_op jit(solution)/shard_map/ppermute | solution.py:293
  21.4 23.8 %copy-start.3 = (bf16[512,128]{1,0:T(8,128)(2,1)S(1)}, bf16[512,128]{1,0:T(8,128)(2,1)}, u32[]{:S(2)}) copy-start(bf16[512,128]{1,0:T(8,128)(2,1)} %get-tuple-element.33) | copy-start | bytes 393220
  21.4 30.7 %copy-start = (bf16[1040,128]{1,0:T(8,128)(2,1)S(1)}, bf16[1040,128]{1,0:T(8,128)(2,1)}, u32[]{:S(2)}) copy-start(bf16[1040,128]{1,0:T(8,128)(2,1)} %get-tuple-element.22.refs_1_) | copy-start | bytes 798724
  21.4 30.7 %copy-start.1 = (bf16[512,128]{1,0:T(8,128)(2,1)S(1)}, bf16[512,128]{1,0:T(8,128)(2,1)}, u32[]{:S(2)}) copy-start(bf16[512,128]{1,0:T(8,128)(2,1)} %get-tuple-element.27.refs_9_) | copy-start | bytes 393220
  21.4 30.7 %copy-start.2 = (s32[3]{0:T(128)S(1)}, s32[3]{0:T(128)}, u32[]{:S(2)}) copy-start(s32[3]{0:T(128)} %pad_add_fusion.place_ref.refs_0_.where_ref) | copy-start | bytes 40
  21.4 16.9 %collective-permute-start.2 = (bf16[1040,128]{1,0:T(8,128)(2,1)}, bf16[1040,128]{1,0:T(8,128)(2,1)S(1)}, u32[]{:S(2)}, u32[]{:S(2)}) collective-permute-start(bf16[1040,128]{1,0:T(8,128)(2,1)} %get-tuple-element.26), channel_id=1, source_target_pairs={{0,24},{4,28},{8,16},{12,20},{16,8},{20,12},{24,0},{28,4},{1,25},{... | collective-permute-start | bytes 798728 | tf_op jit(solution)/shard_map/ppermute | solution.py:293
  24.9 14.0 %collective-permute-start.4 = (bf16[1040,128]{1,0:T(8,128)(2,1)S(1)}, bf16[1040,128]{1,0:T(8,128)(2,1)S(1)}, u32[]{:S(2)}, u32[]{:S(2)}) collective-permute-start(bf16[1040,128]{1,0:T(8,128)(2,1)S(1)} %collective-permute-done.refs_2_), channel_id=1, source_target_pairs={{0,4},{4,0},{8,12},{12,8},{16,20},{20,16},{24,28},{28,24},{1,5},{5... | collective-permute-start | bytes 798728 | tf_op jit(solution)/shard_map/ppermute | solution.py:293
  27.1 38.7 %collective-permute-start.27 = (bf16[512,512]{1,0:T(8,128)(2,1)S(1)}, bf16[512,512]{1,0:T(8,128)(2,1)S(1)}, u32[]{:S(2)}, u32[]{:S(2)}) collective-permute-start(bf16[512,512]{1,0:T(8,128)(2,1)S(1)} %get-tuple-element.39), channel_id=1, source_target_pairs={{0,3},{1,2},{2,1},{3,0},{4,7},{5,6},{6,5},{7,4},{8,11},{9,10},{10,... | collective-permute-start | bytes 1572872 | tf_op jit(solution)/shard_map/ppermute | solution.py:293
  36.8 31.5 %collective-permute-start.26 = (bf16[512,512]{1,0:T(8,128)(2,1)S(1)}, bf16[512,512]{1,0:T(8,128)(2,1)S(1)}, u32[]{:S(2)}, u32[]{:S(2)}) collective-permute-start(bf16[512,512]{1,0:T(8,128)(2,1)S(1)} %get-tuple-element.40), channel_id=1, source_target_pairs={{0,2},{1,3},{2,0},{3,1},{4,6},{5,7},{6,4},{7,5},{8,10},{9,11},{10,... | collective-permute-start | bytes 1572872 | tf_op jit(solution)/shard_map/ppermute | solution.py:293
  38.3 31.5 %collective-permute-start.25 = (bf16[512,512]{1,0:T(8,128)(2,1)S(1)}, bf16[512,512]{1,0:T(8,128)(2,1)S(1)}, u32[]{:S(2)}, u32[]{:S(2)}) collective-permute-start(bf16[512,512]{1,0:T(8,128)(2,1)S(1)} %get-tuple-element.41), channel_id=1, source_target_pairs={{0,1},{1,0},{2,3},{3,2},{4,5},{5,4},{6,7},{7,6},{8,9},{9,8},{10,11... | collective-permute-start | bytes 1572872 | tf_op jit(solution)/shard_map/ppermute | solution.py:293
  38.3 13.8 %collective-permute-start.6 = (bf16[1040,128]{1,0:T(8,128)(2,1)S(1)}, bf16[1040,128]{1,0:T(8,128)(2,1)S(1)}, u32[]{:S(2)}, u32[]{:S(2)}) collective-permute-start(bf16[1040,128]{1,0:T(8,128)(2,1)S(1)} %collective-permute-done.2.refs_4_), channel_id=1, source_target_pairs={{0,4},{4,0},{8,12},{12,8},{16,20},{20,16},{24,28},{28,24},{1,5},{5... | collective-permute-start | bytes 798728 | tf_op jit(solution)/shard_map/ppermute | solution.py:293
  38.9 6.3 %collective-permute-start.7 = (bf16[512,128]{1,0:T(8,128)(2,1)S(1)}, bf16[512,128]{1,0:T(8,128)(2,1)S(1)}, u32[]{:S(2)}, u32[]{:S(2)}) collective-permute-start(bf16[512,128]{1,0:T(8,128)(2,1)S(1)} %copy-done.4), channel_id=1, source_target_pairs={{0,8},{4,12},{8,0},{12,4},{16,24},{20,28},{24,16},{28,20},{1,9},{5... | collective-permute-start | bytes 393224 | tf_op jit(solution)/shard_map/ppermute | solution.py:293
  45.2 6.9 %collective-permute-start.9 = (bf16[512,128]{1,0:T(8,128)(2,1)S(1)}, bf16[512,128]{1,0:T(8,128)(2,1)S(1)}, u32[]{:S(2)}, u32[]{:S(2)}) collective-permute-start(bf16[512,128]{1,0:T(8,128)(2,1)S(1)} %copy-done.3), channel_id=1, source_target_pairs={{0,24},{4,28},{8,16},{12,20},{16,8},{20,12},{24,0},{28,4},{1,25},{... | collective-permute-start | bytes 393224 | tf_op jit(solution)/shard_map/ppermute | solution.py:293
  63.8 7.3 %collective-permute-start.10 = (bf16[512,128]{1,0:T(8,128)(2,1)S(1)}, bf16[512,128]{1,0:T(8,128)(2,1)S(1)}, u32[]{:S(2)}, u32[]{:S(2)}) collective-permute-start(bf16[512,128]{1,0:T(8,128)(2,1)S(1)} %get-tuple-element.35), channel_id=1, source_target_pairs={{0,8},{4,12},{8,0},{12,4},{16,24},{20,28},{24,16},{28,20},{1,9},{5... | collective-permute-start | bytes 393224 | tf_op jit(solution)/shard_map/ppermute | solution.py:293
  65.4 9.9 %collective-permute-start.11 = (bf16[512,128]{1,0:T(8,128)(2,1)S(1)}, bf16[512,128]{1,0:T(8,128)(2,1)S(1)}, u32[]{:S(2)}, u32[]{:S(2)}) collective-permute-start(bf16[512,128]{1,0:T(8,128)(2,1)S(1)} %get-tuple-element.36), channel_id=1, source_target_pairs={{0,16},{4,20},{8,24},{12,28},{16,0},{20,4},{24,8},{28,12},{1,17},{... | collective-permute-start | bytes 393224 | tf_op jit(solution)/shard_map/ppermute | solution.py:293
  65.8 9.5 %collective-permute-start.12 = (bf16[512,128]{1,0:T(8,128)(2,1)S(1)}, bf16[512,128]{1,0:T(8,128)(2,1)S(1)}, u32[]{:S(2)}, u32[]{:S(2)}) collective-permute-start(bf16[512,128]{1,0:T(8,128)(2,1)S(1)} %get-tuple-element.37), channel_id=1, source_target_pairs={{0,24},{4,28},{8,16},{12,20},{16,8},{20,12},{24,0},{28,4},{1,25},{... | collective-permute-start | bytes 393224 | tf_op jit(solution)/shard_map/ppermute | solution.py:293
  68.3 8.6 %collective-permute-start.17 = (bf16[512,128]{1,0:T(8,128)(2,1)S(1)}, bf16[512,128]{1,0:T(8,128)(2,1)S(1)}, u32[]{:S(2)}, u32[]{:S(2)}) collective-permute-start(bf16[512,128]{1,0:T(8,128)(2,1)S(1)} %get-tuple-element.34.refs_0_), channel_id=1, source_target_pairs={{0,2},{1,3},{2,0},{3,1},{4,6},{5,7},{6,4},{7,5},{8,10},{9,11},{10,... | collective-permute-start | bytes 393224 | tf_op jit(solution)/shard_map/ppermute | solution.py:293
  69.8 7.3 %collective-permute-start.13 = (bf16[512,128]{1,0:T(8,128)(2,1)S(1)}, bf16[512,128]{1,0:T(8,128)(2,1)S(1)}, u32[]{:S(2)}, u32[]{:S(2)}) collective-permute-start(bf16[512,128]{1,0:T(8,128)(2,1)S(1)} %get-tuple-element.34.refs_0_), channel_id=1, source_target_pairs={{0,1},{1,0},{2,3},{3,2},{4,5},{5,4},{6,7},{7,6},{8,9},{9,8},{10,11... | collective-permute-start | bytes 393224 | tf_op jit(solution)/shard_map/ppermute | solution.py:293
  71.1 6.4 %collective-permute-start.18 = (bf16[512,128]{1,0:T(8,128)(2,1)S(1)}, bf16[512,128]{1,0:T(8,128)(2,1)S(1)}, u32[]{:S(2)}, u32[]{:S(2)}) collective-permute-start(bf16[512,128]{1,0:T(8,128)(2,1)S(1)} %collective-permute-done.10.refs_1_), channel_id=1, source_target_pairs={{0,2},{1,3},{2,0},{3,1},{4,6},{5,7},{6,4},{7,5},{8,10},{9,11},{10,... | collective-permute-start | bytes 393224 | tf_op jit(solution)/shard_map/ppermute | solution.py:293
  75.3 2.3 %collective-permute-start.14 = (bf16[512,128]{1,0:T(8,128)(2,1)S(1)}, bf16[512,128]{1,0:T(8,128)(2,1)S(1)}, u32[]{:S(2)}, u32[]{:S(2)}) collective-permute-start(bf16[512,128]{1,0:T(8,128)(2,1)S(1)} %collective-permute-done.10.refs_1_), channel_id=1, source_target_pairs={{0,1},{1,0},{2,3},{3,2},{4,5},{5,4},{6,7},{7,6},{8,9},{9,8},{10,11... | collective-permute-start | bytes 393224 | tf_op jit(solution)/shard_map/ppermute | solution.py:293
  75.3 6.3 %collective-permute-start.19 = (bf16[512,128]{1,0:T(8,128)(2,1)S(1)}, bf16[512,128]{1,0:T(8,128)(2,1)S(1)}, u32[]{:S(2)}, u32[]{:S(2)}) collective-permute-start(bf16[512,128]{1,0:T(8,128)(2,1)S(1)} %collective-permute-done.11.refs_2_), channel_id=1, source_target_pairs={{0,2},{1,3},{2,0},{3,1},{4,6},{5,7},{6,4},{7,5},{8,10},{9,11},{10,... | collective-permute-start | bytes 393224 | tf_op jit(solution)/shard_map/ppermute | solution.py:293
  76.8 4.8 %collective-permute-start.15 = (bf16[512,128]{1,0:T(8,128)(2,1)S(1)}, bf16[512,128]{1,0:T(8,128)(2,1)S(1)}, u32[]{:S(2)}, u32[]{:S(2)}) collective-permute-start(bf16[512,128]{1,0:T(8,128)(2,1)S(1)} %collective-permute-done.11.refs_2_), channel_id=1, source_target_pairs={{0,1},{1,0},{2,3},{3,2},{4,5},{5,4},{6,7},{7,6},{8,9},{9,8},{10,11... | collective-permute-start | bytes 393224 | tf_op jit(solution)/shard_map/ppermute | solution.py:293
  77.1 7.0 %collective-permute-start.20 = (bf16[512,128]{1,0:T(8,128)(2,1)S(1)}, bf16[512,128]{1,0:T(8,128)(2,1)S(1)}, u32[]{:S(2)}, u32[]{:S(2)}) collective-permute-start(bf16[512,128]{1,0:T(8,128)(2,1)S(1)} %collective-permute-done.12.refs_3_), channel_id=1, source_target_pairs={{0,2},{1,3},{2,0},{3,1},{4,6},{5,7},{6,4},{7,5},{8,10},{9,11},{10,... | collective-permute-start | bytes 393224 | tf_op jit(solution)/shard_map/ppermute | solution.py:293
  77.6 6.5 %collective-permute-start.16 = (bf16[512,128]{1,0:T(8,128)(2,1)S(1)}, bf16[512,128]{1,0:T(8,128)(2,1)S(1)}, u32[]{:S(2)}, u32[]{:S(2)}) collective-permute-start(bf16[512,128]{1,0:T(8,128)(2,1)S(1)} %collective-permute-done.12.refs_3_), channel_id=1, source_target_pairs={{0,1},{1,0},{2,3},{3,2},{4,5},{5,4},{6,7},{7,6},{8,9},{9,8},{10,11... | collective-permute-start | bytes 393224 | tf_op jit(solution)/shard_map/ppermute | solution.py:293
  77.6 6.5 %collective-permute-start.21 = (bf16[512,128]{1,0:T(8,128)(2,1)S(1)}, bf16[512,128]{1,0:T(8,128)(2,1)S(1)}, u32[]{:S(2)}, u32[]{:S(2)}) collective-permute-start(bf16[512,128]{1,0:T(8,128)(2,1)S(1)} %collective-permute-done.17.refs_8_), channel_id=1, source_target_pairs={{0,1},{1,0},{2,3},{3,2},{4,5},{5,4},{6,7},{7,6},{8,9},{9,8},{10,11... | collective-permute-start | bytes 393224 | tf_op jit(solution)/shard_map/ppermute | solution.py:293
  81.6 2.4 %collective-permute-start.22 = (bf16[512,128]{1,0:T(8,128)(2,1)S(1)}, bf16[512,128]{1,0:T(8,128)(2,1)S(1)}, u32[]{:S(2)}, u32[]{:S(2)}) collective-permute-start(bf16[512,128]{1,0:T(8,128)(2,1)S(1)} %collective-permute-done.18.refs_9_), channel_id=1, source_target_pairs={{0,1},{1,0},{2,3},{3,2},{4,5},{5,4},{6,7},{7,6},{8,9},{9,8},{10,11... | collective-permute-start | bytes 393224 | tf_op jit(solution)/shard_map/ppermute | solution.py:293
  81.6 2.4 %collective-permute-start.23 = (bf16[512,128]{1,0:T(8,128)(2,1)S(1)}, bf16[512,128]{1,0:T(8,128)(2,1)S(1)}, u32[]{:S(2)}, u32[]{:S(2)}) collective-permute-start(bf16[512,128]{1,0:T(8,128)(2,1)S(1)} %collective-permute-done.19.refs_10_), channel_id=1, source_target_pairs={{0,1},{1,0},{2,3},{3,2},{4,5},{5,4},{6,7},{7,6},{8,9},{9,8},{10,11... | collective-permute-start | bytes 393224 | tf_op jit(solution)/shard_map/ppermute | solution.py:293
  84.0 1.3 %collective-permute-start.24 = (bf16[512,128]{1,0:T(8,128)(2,1)S(1)}, bf16[512,128]{1,0:T(8,128)(2,1)S(1)}, u32[]{:S(2)}, u32[]{:S(2)}) collective-permute-start(bf16[512,128]{1,0:T(8,128)(2,1)S(1)} %collective-permute-done.20.refs_11_), channel_id=1, source_target_pairs={{0,1},{1,0},{2,3},{3,2},{4,5},{5,4},{6,7},{7,6},{8,9},{9,8},{10,11... | collective-permute-start | bytes 393224 | tf_op jit(solution)/shard_map/ppermute | solution.py:293
  (1 other events, 17.5 us)

commit v3 on v2

--- a/solution.py
+++ b/solution.py
@@ -235,51 +235,78 @@
     )(where, *kv_own, *kv_far, *q)
 
 
-def project_kernel(where_ref, *refs):
-    pieces = (len(refs) - 8) // 4
-    a_refs, w_refs = refs[: 4 * pieces], refs[4 * pieces : 4 * pieces + 4]
-    out_ref, a_all, w_all, sems = refs[4 * pieces + 4 :]
-    rows, width = a_refs[0].shape
-    place, here = where_ref[0], where_ref[2]
-    started = []
-
-    def fetch(source, target):
-        copy = pltpu.make_async_copy(source, target, sems.at[len(started)])
+def gather_rows(place, pieces, w_source, a_all, w_all, sems):
+    rows, width = pieces[0].shape
+    copies = [pltpu.make_async_copy(w_source, w_all, sems.at[len(pieces)])]
+    for offset, ref in enumerate(pieces):
+        head = lax.bitwise_xor(place, offset)
+        columns = pl.ds(pl.multiple_of(head * width, width), width)
+        copies.append(pltpu.make_async_copy(ref, a_all.at[:, columns], sems.at[offset]))
+    for copy in copies:
         copy.start()
-        started.append(copy)
-
-    for far in range(4):
-        group = lax.bitwise_xor(here, far)
-        fetch(w_refs[far], w_all.at[group])
-        for offset in range(pieces):
-            head = lax.bitwise_xor(place, offset)
-            columns = pl.ds(pl.multiple_of(head * width, width), width)
-            fetch(a_refs[far * pieces + offset], a_all.at[group, :, columns])
-    for copy in started:
+    for copy in copies:
         copy.wait()
-    total = jnp.dot(a_all[0], w_all[0], preferred_element_type=jnp.float32)
-    for group in range(1, 4):
-        total = total + jnp.dot(a_all[group], w_all[group], preferred_element_type=jnp.float32)
-    out_ref[...] = total.astype(jnp.bfloat16)
-
-
-def project(where, blocks, weights):
-    pieces = len(blocks[0])
-    rows, width = blocks[0][0].shape
+
+
+def near_kernel(where_ref, w_ref, *refs):
+    out_ref, a_all, w_all, sems = refs[-4:]
+    half = w_all.shape[1]
+    columns = pl.ds(pl.multiple_of(where_ref[2] // 2 * half, half), half)
+    gather_rows(where_ref[0], refs[:-4], w_ref.at[:, columns], a_all, w_all, sems)
+    out_ref[...] = jnp.dot(a_all[...], w_all[...], preferred_element_type=jnp.float32)
+
+
+def far_kernel(where_ref, w_ref, near_ref, *refs):
+    mine_ref, other_ref, a_all, w_all, total, sems = refs[-6:]
+    gather_rows(where_ref[0], refs[:-6], w_ref, a_all, w_all, sems)
+    total[...] = near_ref[...] + jnp.dot(a_all[...], w_all[...], preferred_element_type=jnp.float32)
+    width = mine_ref.shape[1]
+    core = where_ref[2] % 2
+    mine_ref[...] = total[:, pl.ds(pl.multiple_of(core * width, width), width)]
+    other_ref[...] = total[:, pl.ds(pl.multiple_of((1 - core) * width, width), width)].astype(jnp.bfloat16)
+
+
+def near_sums(where, out_weight, pieces):
+    rows, width = pieces[0].shape
+    depth, half = out_weight.shape[0], out_weight.shape[1] // 2
     anywhere = pl.BlockSpec(memory_space=pl.ANY)
     return pl.pallas_call(
-        project_kernel,
-        out_shape=jax.ShapeDtypeStruct((rows, weights[0].shape[1]), jnp.bfloat16),
-        in_specs=[pl.BlockSpec(memory_space=pltpu.SMEM)] + [anywhere] * (4 * pieces + 4),
+        near_kernel,
+        out_shape=jax.ShapeDtypeStruct((rows, half), jnp.float32),
+        in_specs=[pl.BlockSpec(memory_space=pltpu.SMEM)] + [anywhere] * (1 + len(pieces)),
         out_specs=pl.BlockSpec(memory_space=pltpu.VMEM),
         scratch_shapes=[
-            pltpu.VMEM((4, rows, pieces * width), jnp.bfloat16),
-            pltpu.VMEM((4,) + weights[0].shape, jnp.bfloat16),
-            pltpu.SemaphoreType.DMA((4 + 4 * pieces,)),
+            pltpu.VMEM((rows, depth), jnp.bfloat16),
+            pltpu.VMEM((depth, half), jnp.bfloat16),
+            pltpu.SemaphoreType.DMA((1 + len(pieces),)),
         ],
-        compiler_params=pltpu.CompilerParams(vmem_limit_bytes=32 * 1024 * 1024),
-        name="project",
-    )(where, *[piece for block in blocks for piece in block], *weights)
+        compiler_params=pltpu.CompilerParams(vmem_limit_bytes=24 * 1024 * 1024),
+        name="near_sums",
+    )(where, out_weight, *pieces)
+
+
+def far_sums(where, weights, near, pieces):
+    rows, width = pieces[0].shape
+    depth, half = weights.shape
+    anywhere = pl.BlockSpec(memory_space=pl.ANY)
+    local_memory = pl.BlockSpec(memory_space=pltpu.VMEM)
+    return pl.pallas_call(
+        far_kernel,
+        out_shape=(
+            jax.ShapeDtypeStruct((rows, half // 2), jnp.float32),
+            jax.ShapeDtypeStruct((rows, half // 2), jnp.bfloat16),
+        ),
+        in_specs=[pl.BlockSpec(memory_space=pltpu.SMEM), anywhere, local_memory] + [anywhere] * len(pieces),
+        out_specs=(local_memory, local_memory),
+        scratch_shapes=[
+            pltpu.VMEM((rows, depth), jnp.bfloat16),
+            pltpu.VMEM((depth, half), jnp.bfloat16),
+            pltpu.VMEM((rows, half), jnp.float32),
+            pltpu.SemaphoreType.DMA((1 + len(pieces),)),
+        ],
+        compiler_params=pltpu.CompilerParams(vmem_limit_bytes=24 * 1024 * 1024),
+        name="far_sums",
+    )(where, weights, near, *pieces)
 
 
 def head_plan(queries, keys, values, cluster_ids, out_weight):
@@ -301,12 +328,9 @@
     kv_own[1] = swap(kv[1], "seq", 2)
     kv_far[0] = swap(kv[0], "seq", 1)
     kv_own[3] = swap(after(kv[3], kv_own[1]), "seq", 6)
-    columns = out_weight.shape[1] // 4
-    weights = []
-    late_weight = after(out_weight, kv[1])
-    for far in range(4):
-        block = lax.dynamic_slice_in_dim(late_weight, (here ^ far) * columns, columns, 1)
-        weights.append(swap(block, "head", far) if far else block)
+    half = out_weight.shape[1] // 2
+    weights = lax.dynamic_slice_in_dim(after(out_weight, kv[1]), (1 - here // 2) * half, half, 1)
+    weights = swap(weights, "head", 2)
     for offset in (1, 2, 3):
         kv_far[offset] = swap(kv_own[offset], "seq", 1)
     q_own[2] = swap(after(q[2], kv_own[2]), "seq", 4)
@@ -316,8 +340,9 @@
     for offset in range(1, heads):
         attended[offset] = swap(attended[offset], "seq", 2 * offset)
     across = [swap(piece, "head", 2) for piece in attended]
-    blocks = [attended, [swap(piece, "head", 1) for piece in attended], across, [swap(piece, "head", 1) for piece in across]]
-    return project(where, blocks, weights)
+    near = near_sums(where, out_weight, attended)
+    mine, other = far_sums(where, weights, near, across)
+    return (mine + swap(other, "head", 1).astype(jnp.float32)).astype(jnp.bfloat16)
 
 
 def local(queries, keys, values, cluster_ids, out_weight):

time: 88.9 us -> 84.4 us (0.949)
  waiting for transfers between devices: 37.9 us -> 34.7 us
  starting transfers between devices: 30.6 us -> 28.5 us
  other arithmetic: 0.65 us -> 1.66 us
    ppermute x28 -> x19, waiting for transfers between devices: 37.9 us -> 34.7 us  [swap(): lax.ppermute(array, axis, [(place, place ^ bits) for place in range(size)])]
    ppermute x28 -> x19, starting transfers between devices: 30.6 us -> 28.5 us  [swap(): lax.ppermute(array, axis, [(place, place ^ bits) for place in range(size)])]
    convert_element_type x0 -> x1, other arithmetic: none -> 0.99 us  [head_plan(): (mine + swap(other, 'head', 1).astype(jnp.float32)).astype(jnp.bfloat16)]
    pallas_call x1 -> x2, Pallas kernels: 3.33 us -> 3.28 us  [the longest x1 1.73 us: far_sums(): pl.pallas_call(far_kernel, out_shape=(jax.ShapeDtypeStruct((rows, half //...]
  transfers between devices with their start and end apart: 28 -> 19, of which waited for: 9 -> 10; matrix products, arithmetic and copies ran while one was open for 2% -> 2% of each run, Pallas kernels for 13% -> 16%
where the time goes in v3:
time: 84.4 us; the launch traced here: 84.2 us
  waiting for transfers between devices  34.7 us (41%)
  starting transfers between devices  28.5 us (34%)
  Pallas kernels  17.7 us (21%)
  other arithmetic  1.66 us (2%)
  local copies, waits for them, and re-layouts  1.48 us (2%)
    ppermute x19, waiting for transfers between devices, swap(): lax.ppermute(array, axis, [(place, place ^ bits) for place in range(size)])  34.7 us
    ppermute x19, starting transfers between devices, swap(): lax.ppermute(array, axis, [(place, place ^ bits) for place in range(size)])  28.5 us
    pallas_call x1, Pallas kernels, attend(): pl.pallas_call(lambda *refs: attend_kernel(1.0 / math.sqrt(width), *refs)...  11.7 us
    pallas_call x1, Pallas kernels, pack(): pl.pallas_call(pack_kernel, out_shape=tuple(pair * heads), in_specs=[pl.B...  2.73 us
    pallas_call x1, Pallas kernels, far_sums(): pl.pallas_call(far_kernel, out_shape=(jax.ShapeDtypeStruct((rows, half //...  1.73 us
  transfers between devices with their start and end apart: 19, of which 10 were waited for; matrix products, arithmetic and copies ran while one was open for 2% of the time, Pallas kernels for 16%

profile of v3, /device:TPU:0, one launch (start us, length us, event | category | flops | bytes accessed | tf_op | source)
XLA Modules:
  0.0 84.2 jit_solution(13905724358745716576)
XLA Ops:
  0.0 0.7 pad_add_fusion.place_ref.refs_0_.where_ref
  0.7 2.7 %pack.1 = (bf16[512,128]{1,0:T(8,128)(2,1)}, bf16[1040,128]{1,0:T(8,128)(2,1)}, bf16[512,128]{1,0:T(8,128)(2,1)}, bf16[1040,128]{1,0:T(8,128)(2,1)}, bf16[512,12...) custom-call(s32[3]{0:T(128)} %pad_add_fusion.place_ref.refs_0_.where_ref, ...), custom_call_target="tpu_custom_call" | custom-call | tf_op jit(solution)/shard_map/pack/pallas_call | solution.py:121
  3.5 3.1 %collective-permute-start.1 = (bf16[1040,128]{1,0:T(8,128)(2,1)}, bf16[1040,128]{1,0:T(8,128)(2,1)S(1)}, u32[]{:S(2)}, u32[]{:S(2)}) collective-permute-start(bf16[1040,128]{1,0:T(8,128)(2,1)} %get-tuple-element.24), channel_id=1, source_target_pairs={{0,8},{4,12},{8,0},{12,4},{16,24},{20,28},{24,16},{28,20},{1,9},{5... | collective-permute-start | bytes 798728 | tf_op jit(solution)/shard_map/ppermute | solution.py:320
  6.5 1.4 %constant_dynamic-slice_fusion = bf16[512,1024]{1,0:T(8,128)(2,1)S(1)} fusion(bf16[512,2048]{1,0:T(8,128)(2,1)} %w_ref.1, s32[]{:T(128)S(6)} %select_n.20), kind=kLoop, calls=%fused_computation.2 | loop fusion | bytes 2097156 | tf_op jit(solution)/shard_map/dynamic_slice | solution.py:332
  8.0 1.6 %collective-permute-start = (bf16[512,1024]{1,0:T(8,128)(2,1)S(1)}, bf16[512,1024]{1,0:T(8,128)(2,1)S(1)}, u32[]{:S(2)}, u32[]{:S(2)}) collective-permute-start(bf16[512,1024]{1,0:T(8,128)(2,1)S(1)} %constant_dynamic-slice_fusion), channel_id=1, source_target_pairs={{0,2},{1,3},{2,0},{3,1},{4,6},{5,7},{6,4},{7,5},{8,10},{9,11},{10,... | collective-permute-start | bytes 3145736 | tf_op jit(solution)/shard_map/ppermute | solution.py:320
  9.6 2.6 %collective-permute-start.2 = (bf16[1040,128]{1,0:T(8,128)(2,1)S(1)}, bf16[1040,128]{1,0:T(8,128)(2,1)S(1)}, u32[]{:S(2)}, u32[]{:S(2)}) collective-permute-start(bf16[1040,128]{1,0:T(8,128)(2,1)S(1)} %copy-done.5), channel_id=1, source_target_pairs={{0,16},{4,20},{8,24},{12,28},{16,0},{20,4},{24,8},{28,12},{1,17},{... | collective-permute-start | bytes 798728 | tf_op jit(solution)/shard_map/ppermute | solution.py:320
  12.2 3.5 %collective-permute-done.1.refs_2_ = bf16[1040,128]{1,0:T(8,128)(2,1)S(1)} collective-permute-done((bf16[1040,128]{1,0:T(8,128)(2,1)}, bf16[1040,128]{1,0:T(8,128)(2,1)S(1)}, u32[]{:S(2)}, u32[]{:S(2)}) %collective-permute-start.1) | collective-permute-done | bytes 266272 | tf_op jit(solution)/shard_map/ppermute | solution.py:320
  15.7 3.1 %collective-permute-start.3 = (bf16[1040,128]{1,0:T(8,128)(2,1)S(1)}, bf16[1040,128]{1,0:T(8,128)(2,1)S(1)}, u32[]{:S(2)}, u32[]{:S(2)}) collective-permute-start(bf16[1040,128]{1,0:T(8,128)(2,1)S(1)} %copy-done.4), channel_id=1, source_target_pairs={{0,24},{4,28},{8,16},{12,20},{16,8},{20,12},{24,0},{28,4},{1,25},{... | collective-permute-start | bytes 798728 | tf_op jit(solution)/shard_map/ppermute | solution.py:320
  18.8 1.5 %collective-permute-start.4 = (bf16[1040,128]{1,0:T(8,128)(2,1)S(1)}, bf16[1040,128]{1,0:T(8,128)(2,1)S(1)}, u32[]{:S(2)}, u32[]{:S(2)}) collective-permute-start(bf16[1040,128]{1,0:T(8,128)(2,1)S(1)} %copy-done.1), channel_id=1, source_target_pairs={{0,4},{4,0},{8,12},{12,8},{16,20},{20,16},{24,28},{28,24},{1,5},{5... | collective-permute-start | bytes 798728 | tf_op jit(solution)/shard_map/ppermute | solution.py:320
  20.3 10.9 %collective-permute-done.2.refs_3_ = bf16[1040,128]{1,0:T(8,128)(2,1)S(1)} collective-permute-done((bf16[1040,128]{1,0:T(8,128)(2,1)S(1)}, bf16[1040,128]{1,0:T(8,128)(2,1)S(1)}, u32[]{:S(2)}, u32[]{:S(2)}) %collective-permute-start.2) | collective-permute-done | bytes 266272 | tf_op jit(solution)/shard_map/ppermute | solution.py:320
  31.2 1.5 %collective-permute-start.6 = (bf16[1040,128]{1,0:T(8,128)(2,1)S(1)}, bf16[1040,128]{1,0:T(8,128)(2,1)S(1)}, u32[]{:S(2)}, u32[]{:S(2)}) collective-permute-start(bf16[1040,128]{1,0:T(8,128)(2,1)S(1)} %collective-permute-done.2.refs_3_), channel_id=1, source_target_pairs={{0,4},{4,0},{8,12},{12,8},{16,20},{20,16},{24,28},{28,24},{1,5},{5... | collective-permute-start | bytes 798728 | tf_op jit(solution)/shard_map/ppermute | solution.py:320
  32.7 0.5 collective-permute-start.5
  33.3 1.5 %collective-permute-start.7 = (bf16[1040,128]{1,0:T(8,128)(2,1)S(1)}, bf16[1040,128]{1,0:T(8,128)(2,1)S(1)}, u32[]{:S(2)}, u32[]{:S(2)}) collective-permute-start(bf16[1040,128]{1,0:T(8,128)(2,1)S(1)} %collective-permute-done.3.refs_4_), channel_id=1, source_target_pairs={{0,4},{4,0},{8,12},{12,8},{16,20},{20,16},{24,28},{28,24},{1,5},{5... | collective-permute-start | bytes 798728 | tf_op jit(solution)/shard_map/ppermute | solution.py:320
  34.8 3.5 %collective-permute-start.9 = (bf16[512,128]{1,0:T(8,128)(2,1)S(1)}, bf16[512,128]{1,0:T(8,128)(2,1)S(1)}, u32[]{:S(2)}, u32[]{:S(2)}) collective-permute-start(bf16[512,128]{1,0:T(8,128)(2,1)S(1)} %copy-done.8), channel_id=1, source_target_pairs={{0,16},{4,20},{8,24},{12,28},{16,0},{20,4},{24,8},{28,12},{1,17},{... | collective-permute-start | bytes 393224 | tf_op jit(solution)/shard_map/ppermute | solution.py:320
  38.3 4.9 %collective-permute-done.9.refs_11_ = bf16[512,128]{1,0:T(8,128)(2,1)S(1)} collective-permute-done((bf16[512,128]{1,0:T(8,128)(2,1)S(1)}, bf16[512,128]{1,0:T(8,128)(2,1)S(1)}, u32[]{:S(2)}, u32[]{:S(2)}) %collective-permute-start.9) | collective-permute-done | bytes 131104 | tf_op jit(solution)/shard_map/ppermute | solution.py:320
  43.3 2.5 %collective-permute-start.10 = (bf16[512,128]{1,0:T(8,128)(2,1)S(1)}, bf16[512,128]{1,0:T(8,128)(2,1)S(1)}, u32[]{:S(2)}, u32[]{:S(2)}) collective-permute-start(bf16[512,128]{1,0:T(8,128)(2,1)S(1)} %copy-done.6), channel_id=1, source_target_pairs={{0,24},{4,28},{8,16},{12,20},{16,8},{20,12},{24,0},{28,4},{1,25},{... | collective-permute-start | bytes 393224 | tf_op jit(solution)/shard_map/ppermute | solution.py:320
  45.7 2.6 %collective-permute-done.8.refs_10_ = bf16[512,128]{1,0:T(8,128)(2,1)S(1)} collective-permute-done((bf16[512,128]{1,0:T(8,128)(2,1)S(1)}, bf16[512,128]{1,0:T(8,128)(2,1)S(1)}, u32[]{:S(2)}, u32[]{:S(2)}) %collective-permute-start.8) | collective-permute-done | bytes 131104 | tf_op jit(solution)/shard_map/ppermute | solution.py:320
  48.4 1.8 %collective-permute-done.10.refs_12_ = bf16[512,128]{1,0:T(8,128)(2,1)S(1)} collective-permute-done((bf16[512,128]{1,0:T(8,128)(2,1)S(1)}, bf16[512,128]{1,0:T(8,128)(2,1)S(1)}, u32[]{:S(2)}, u32[]{:S(2)}) %collective-permute-start.10) | collective-permute-done | bytes 131104 | tf_op jit(solution)/shard_map/ppermute | solution.py:320
  50.2 11.7 %attend.1 = (bf16[512,128]{1,0:T(8,128)(2,1)S(1)}, bf16[512,128]{1,0:T(8,128)(2,1)S(1)}, bf16[512,128]{1,0:T(8,128)(2,1)S(1)}, bf16[512,128]{1,0:T(8,128)(2,1)S(1)}) custom-call(s32[3]{0:T(128)S(1)} %copy-done.3, bf16[1040,128]{1,0:T(8,128)(2,1)S(1)} %copy-done.1, bf16[1040,128]{1,0:T(8,128)(2,1)S(1)} %collective-permute-done.1.refs_2_, ...), custom_call_target="tpu_custom_call" | custom-call | tf_op jit(solution)/shard_map/attend/pallas_call | solution.py:220
  61.9 1.5 %collective-permute-start.11 = (bf16[512,128]{1,0:T(8,128)(2,1)S(1)}, bf16[512,128]{1,0:T(8,128)(2,1)S(1)}, u32[]{:S(2)}, u32[]{:S(2)}) collective-permute-start(bf16[512,128]{1,0:T(8,128)(2,1)S(1)} %get-tuple-element.38), channel_id=1, source_target_pairs={{0,8},{4,12},{8,0},{12,4},{16,24},{20,28},{24,16},{28,20},{1,9},{5... | collective-permute-start | bytes 393224 | tf_op jit(solution)/shard_map/ppermute | solution.py:320
  63.4 1.6 %collective-permute-start.12 = (bf16[512,128]{1,0:T(8,128)(2,1)S(1)}, bf16[512,128]{1,0:T(8,128)(2,1)S(1)}, u32[]{:S(2)}, u32[]{:S(2)}) collective-permute-start(bf16[512,128]{1,0:T(8,128)(2,1)S(1)} %get-tuple-element.39), channel_id=1, source_target_pairs={{0,16},{4,20},{8,24},{12,28},{16,0},{20,4},{24,8},{28,12},{1,17},{... | collective-permute-start | bytes 393224 | tf_op jit(solution)/shard_map/ppermute | solution.py:320
  64.9 1.4 %collective-permute-start.13 = (bf16[512,128]{1,0:T(8,128)(2,1)S(1)}, bf16[512,128]{1,0:T(8,128)(2,1)S(1)}, u32[]{:S(2)}, u32[]{:S(2)}) collective-permute-start(bf16[512,128]{1,0:T(8,128)(2,1)S(1)} %get-tuple-element.40), channel_id=1, source_target_pairs={{0,24},{4,28},{8,16},{12,20},{16,8},{20,12},{24,0},{28,4},{1,25},{... | collective-permute-start | bytes 393224 | tf_op jit(solution)/shard_map/ppermute | solution.py:320
  66.3 0.5 collective-permute-start.14
  66.8 2.4 %collective-permute-done.11.refs_1_ = bf16[512,128]{1,0:T(8,128)(2,1)S(1)} collective-permute-done((bf16[512,128]{1,0:T(8,128)(2,1)S(1)}, bf16[512,128]{1,0:T(8,128)(2,1)S(1)}, u32[]{:S(2)}, u32[]{:S(2)}) %collective-permute-start.11) | collective-permute-done | bytes 131104 | tf_op jit(solution)/shard_map/ppermute | solution.py:320
  69.2 3.9 %collective-permute-done.12.refs_2_ = bf16[512,128]{1,0:T(8,128)(2,1)S(1)} collective-permute-done((bf16[512,128]{1,0:T(8,128)(2,1)S(1)}, bf16[512,128]{1,0:T(8,128)(2,1)S(1)}, u32[]{:S(2)}, u32[]{:S(2)}) %collective-permute-start.12) | collective-permute-done | bytes 131104 | tf_op jit(solution)/shard_map/ppermute | solution.py:320
  73.1 2.0 %collective-permute-start.17 = (bf16[512,128]{1,0:T(8,128)(2,1)S(1)}, bf16[512,128]{1,0:T(8,128)(2,1)S(1)}, u32[]{:S(2)}, u32[]{:S(2)}) collective-permute-start(bf16[512,128]{1,0:T(8,128)(2,1)S(1)} %collective-permute-done.13.refs_3_), channel_id=1, source_target_pairs={{0,2},{1,3},{2,0},{3,1},{4,6},{5,7},{6,4},{7,5},{8,10},{9,11},{10,... | collective-permute-start | bytes 393224 | tf_op jit(solution)/shard_map/ppermute | solution.py:320
  75.1 1.5 %near_sums.1.near_ref = f32[512,1024]{1,0:T(8,128)S(1)} custom-call(s32[3]{0:T(128)S(1)} %copy-done.3, bf16[512,2048]{1,0:T(8,128)(2,1)S(1)} %copy-done, bf16[512,128]{1,0:T(8,128)(2,1)S(1)} %get-tuple-element.37.refs_0_, bf16[512,128]{1,0:T(8,128)(2,1)S(1)} %collective-permute-done.11.refs_1_, bf16[512,128]{1,0:T(8,128)(2,1)S(1)} %collective-permute-done.12.refs_2_, ...), custom_call_target="tpu_custom_call" | custom-call | tf_op jit(solution)/shard_map/near_sums/pallas_call | solution.py:273
  76.7 1.3 %collective-permute-done.16.refs_2_ = bf16[512,128]{1,0:T(8,128)(2,1)S(1)} collective-permute-done((bf16[512,128]{1,0:T(8,128)(2,1)S(1)}, bf16[512,128]{1,0:T(8,128)(2,1)S(1)}, u32[]{:S(2)}, u32[]{:S(2)}) %collective-permute-start.16) | collective-permute-done | bytes 131104 | tf_op jit(solution)/shard_map/ppermute | solution.py:320
  78.1 1.4 %collective-permute-done.17.refs_3_ = bf16[512,128]{1,0:T(8,128)(2,1)S(1)} collective-permute-done((bf16[512,128]{1,0:T(8,128)(2,1)S(1)}, bf16[512,128]{1,0:T(8,128)(2,1)S(1)}, u32[]{:S(2)}, u32[]{:S(2)}) %collective-permute-start.17) | collective-permute-done | bytes 131104 | tf_op jit(solution)/shard_map/ppermute | solution.py:320
  79.5 1.7 %far_sums.1 = (f32[512,512]{1,0:T(8,128)S(1)}, bf16[512,512]{1,0:T(8,128)(2,1)S(1)}) custom-call(s32[3]{0:T(128)S(1)} %copy-done.3, bf16[512,1024]{1,0:T(8,128)(2,1)S(1)} %collective-permute-done.w_ref, f32[512,1024]{1,0:T(8,128)S(1)} %near_sums.1.near_ref, bf16[512,128]{1,0:T(8,128)(2,1)S(1)} %collective-permute-done.14.refs_0_, ...), custom_call_target="tpu_custom_call" | custom-call | tf_op jit(solution)/shard_map/far_sums/pallas_call | solution.py:293
  81.3 1.9 %collective-permute-done.18 = bf16[512,512]{1,0:T(8,128)(2,1)S(1)} collective-permute-done((bf16[512,512]{1,0:T(8,128)(2,1)S(1)}, bf16[512,512]{1,0:T(8,128)(2,1)S(1)}, u32[]{:S(2)}, u32[]{:S(2)}) %collective-permute-start.18) | collective-permute-done | bytes 524320 | tf_op jit(solution)/shard_map/ppermute | solution.py:320
  83.2 1.0 %add_convert_fusion = bf16[512,512]{1,0:T(8,128)(2,1)} fusion(f32[512,512]{1,0:T(8,128)S(1)} %get-tuple-element.41, bf16[512,512]{1,0:T(8,128)(2,1)S(1)} %collective-permute-done.18), kind=kLoop, calls=%fused_computation | loop fusion | flops 786432 | bytes 2097152 | tf_op jit(solution)/shard_map/convert_element_type | solution.py:345
  (31 shorter events, 0.2 us)
Async XLA Ops:
  0.7 49.5 %copy-start.3 = (s32[3]{0:T(128)S(1)}, s32[3]{0:T(128)}, u32[]{:S(2)}) copy-start(s32[3]{0:T(128)} %pad_add_fusion.place_ref.refs_0_.where_ref) | copy-start | bytes 40
  3.4 6.2 %copy-start.5 = (bf16[1040,128]{1,0:T(8,128)(2,1)S(1)}, bf16[1040,128]{1,0:T(8,128)(2,1)}, u32[]{:S(2)}) copy-start(bf16[1040,128]{1,0:T(8,128)(2,1)} %get-tuple-element.27) | copy-start | bytes 798724
  3.4 12.3 %copy-start.4 = (bf16[1040,128]{1,0:T(8,128)(2,1)S(1)}, bf16[1040,128]{1,0:T(8,128)(2,1)}, u32[]{:S(2)}) copy-start(bf16[1040,128]{1,0:T(8,128)(2,1)} %get-tuple-element.29) | copy-start | bytes 798724
  3.4 15.4 %copy-start.1 = (bf16[1040,128]{1,0:T(8,128)(2,1)S(1)}, bf16[1040,128]{1,0:T(8,128)(2,1)}, u32[]{:S(2)}) copy-start(bf16[1040,128]{1,0:T(8,128)(2,1)} %get-tuple-element.26.refs_1_) | copy-start | bytes 798724
  3.4 31.3 %copy-start.8 = (bf16[512,128]{1,0:T(8,128)(2,1)S(1)}, bf16[512,128]{1,0:T(8,128)(2,1)}, u32[]{:S(2)}) copy-start(bf16[512,128]{1,0:T(8,128)(2,1)} %get-tuple-element.34) | copy-start | bytes 393220
  3.4 39.8 %copy-start.7 = (bf16[512,128]{1,0:T(8,128)(2,1)S(1)}, bf16[512,128]{1,0:T(8,128)(2,1)}, u32[]{:S(2)}) copy-start(bf16[512,128]{1,0:T(8,128)(2,1)} %get-tuple-element.32) | copy-start | bytes 393220
  3.4 39.8 %copy-start.6 = (bf16[512,128]{1,0:T(8,128)(2,1)S(1)}, bf16[512,128]{1,0:T(8,128)(2,1)}, u32[]{:S(2)}) copy-start(bf16[512,128]{1,0:T(8,128)(2,1)} %get-tuple-element.36) | copy-start | bytes 393220
  3.4 46.7 %copy-start.2 = (bf16[512,128]{1,0:T(8,128)(2,1)S(1)}, bf16[512,128]{1,0:T(8,128)(2,1)}, u32[]{:S(2)}) copy-start(bf16[512,128]{1,0:T(8,128)(2,1)} %get-tuple-element.30.refs_9_) | copy-start | bytes 393220
  3.5 12.2 %collective-permute-start.1 = (bf16[1040,128]{1,0:T(8,128)(2,1)}, bf16[1040,128]{1,0:T(8,128)(2,1)S(1)}, u32[]{:S(2)}, u32[]{:S(2)}) collective-permute-start(bf16[1040,128]{1,0:T(8,128)(2,1)} %get-tuple-element.24), channel_id=1, source_target_pairs={{0,8},{4,12},{8,0},{12,4},{16,24},{20,28},{24,16},{28,20},{1,9},{5... | collective-permute-start | bytes 798728 | tf_op jit(solution)/shard_map/ppermute | solution.py:320
  6.5 68.6 %copy-start = (bf16[512,2048]{1,0:T(8,128)(2,1)S(1)}, bf16[512,2048]{1,0:T(8,128)(2,1)}, u32[]{:S(2)}) copy-start(bf16[512,2048]{1,0:T(8,128)(2,1)} %w_ref.1) | copy-start | bytes 6291460
  8.0 68.7 %collective-permute-start = (bf16[512,1024]{1,0:T(8,128)(2,1)S(1)}, bf16[512,1024]{1,0:T(8,128)(2,1)S(1)}, u32[]{:S(2)}, u32[]{:S(2)}) collective-permute-start(bf16[512,1024]{1,0:T(8,128)(2,1)S(1)} %constant_dynamic-slice_fusion), channel_id=1, source_target_pairs={{0,2},{1,3},{2,0},{3,1},{4,6},{5,7},{6,4},{7,5},{8,10},{9,11},{10,... | collective-permute-start | bytes 3145736 | tf_op jit(solution)/shard_map/ppermute | solution.py:320
  9.6 21.6 %collective-permute-start.2 = (bf16[1040,128]{1,0:T(8,128)(2,1)S(1)}, bf16[1040,128]{1,0:T(8,128)(2,1)S(1)}, u32[]{:S(2)}, u32[]{:S(2)}) collective-permute-start(bf16[1040,128]{1,0:T(8,128)(2,1)S(1)} %copy-done.5), channel_id=1, source_target_pairs={{0,16},{4,20},{8,24},{12,28},{16,0},{20,4},{24,8},{28,12},{1,17},{... | collective-permute-start | bytes 798728 | tf_op jit(solution)/shard_map/ppermute | solution.py:320
  15.7 17.6 %collective-permute-start.3 = (bf16[1040,128]{1,0:T(8,128)(2,1)S(1)}, bf16[1040,128]{1,0:T(8,128)(2,1)S(1)}, u32[]{:S(2)}, u32[]{:S(2)}) collective-permute-start(bf16[1040,128]{1,0:T(8,128)(2,1)S(1)} %copy-done.4), channel_id=1, source_target_pairs={{0,24},{4,28},{8,16},{12,20},{16,8},{20,12},{24,0},{28,4},{1,25},{... | collective-permute-start | bytes 798728 | tf_op jit(solution)/shard_map/ppermute | solution.py:320
  18.8 15.9 %collective-permute-start.4 = (bf16[1040,128]{1,0:T(8,128)(2,1)S(1)}, bf16[1040,128]{1,0:T(8,128)(2,1)S(1)}, u32[]{:S(2)}, u32[]{:S(2)}) collective-permute-start(bf16[1040,128]{1,0:T(8,128)(2,1)S(1)} %copy-done.1), channel_id=1, source_target_pairs={{0,4},{4,0},{8,12},{12,8},{16,20},{20,16},{24,28},{28,24},{1,5},{5... | collective-permute-start | bytes 798728 | tf_op jit(solution)/shard_map/ppermute | solution.py:320
  31.2 12.0 %collective-permute-start.6 = (bf16[1040,128]{1,0:T(8,128)(2,1)S(1)}, bf16[1040,128]{1,0:T(8,128)(2,1)S(1)}, u32[]{:S(2)}, u32[]{:S(2)}) collective-permute-start(bf16[1040,128]{1,0:T(8,128)(2,1)S(1)} %collective-permute-done.2.refs_3_), channel_id=1, source_target_pairs={{0,4},{4,0},{8,12},{12,8},{16,20},{20,16},{24,28},{28,24},{1,5},{5... | collective-permute-start | bytes 798728 | tf_op jit(solution)/shard_map/ppermute | solution.py:320
  32.7 13.0 %collective-permute-start.5 = (bf16[1040,128]{1,0:T(8,128)(2,1)S(1)}, bf16[1040,128]{1,0:T(8,128)(2,1)S(1)}, u32[]{:S(2)}, u32[]{:S(2)}) collective-permute-start(bf16[1040,128]{1,0:T(8,128)(2,1)S(1)} %collective-permute-done.1.refs_2_), channel_id=1, source_target_pairs={{0,4},{4,0},{8,12},{12,8},{16,20},{20,16},{24,28},{28,24},{1,5},{5... | collective-permute-start | bytes 798728 | tf_op jit(solution)/shard_map/ppermute | solution.py:320
  33.3 16.9 %collective-permute-start.7 = (bf16[1040,128]{1,0:T(8,128)(2,1)S(1)}, bf16[1040,128]{1,0:T(8,128)(2,1)S(1)}, u32[]{:S(2)}, u32[]{:S(2)}) collective-permute-start(bf16[1040,128]{1,0:T(8,128)(2,1)S(1)} %collective-permute-done.3.refs_4_), channel_id=1, source_target_pairs={{0,4},{4,0},{8,12},{12,8},{16,20},{20,16},{24,28},{28,24},{1,5},{5... | collective-permute-start | bytes 798728 | tf_op jit(solution)/shard_map/ppermute | solution.py:320
  34.8 8.5 %collective-permute-start.9 = (bf16[512,128]{1,0:T(8,128)(2,1)S(1)}, bf16[512,128]{1,0:T(8,128)(2,1)S(1)}, u32[]{:S(2)}, u32[]{:S(2)}) collective-permute-start(bf16[512,128]{1,0:T(8,128)(2,1)S(1)} %copy-done.8), channel_id=1, source_target_pairs={{0,16},{4,20},{8,24},{12,28},{16,0},{20,4},{24,8},{28,12},{1,17},{... | collective-permute-start | bytes 393224 | tf_op jit(solution)/shard_map/ppermute | solution.py:320
  43.2 5.2 %collective-permute-start.8 = (bf16[512,128]{1,0:T(8,128)(2,1)S(1)}, bf16[512,128]{1,0:T(8,128)(2,1)S(1)}, u32[]{:S(2)}, u32[]{:S(2)}) collective-permute-start(bf16[512,128]{1,0:T(8,128)(2,1)S(1)} %copy-done.7), channel_id=1, source_target_pairs={{0,8},{4,12},{8,0},{12,4},{16,24},{20,28},{24,16},{28,20},{1,9},{5... | collective-permute-start | bytes 393224 | tf_op jit(solution)/shard_map/ppermute | solution.py:320
  43.3 6.9 %collective-permute-start.10 = (bf16[512,128]{1,0:T(8,128)(2,1)S(1)}, bf16[512,128]{1,0:T(8,128)(2,1)S(1)}, u32[]{:S(2)}, u32[]{:S(2)}) collective-permute-start(bf16[512,128]{1,0:T(8,128)(2,1)S(1)} %copy-done.6), channel_id=1, source_target_pairs={{0,24},{4,28},{8,16},{12,20},{16,8},{20,12},{24,0},{28,4},{1,25},{... | collective-permute-start | bytes 393224 | tf_op jit(solution)/shard_map/ppermute | solution.py:320
  61.9 7.4 %collective-permute-start.11 = (bf16[512,128]{1,0:T(8,128)(2,1)S(1)}, bf16[512,128]{1,0:T(8,128)(2,1)S(1)}, u32[]{:S(2)}, u32[]{:S(2)}) collective-permute-start(bf16[512,128]{1,0:T(8,128)(2,1)S(1)} %get-tuple-element.38), channel_id=1, source_target_pairs={{0,8},{4,12},{8,0},{12,4},{16,24},{20,28},{24,16},{28,20},{1,9},{5... | collective-permute-start | bytes 393224 | tf_op jit(solution)/shard_map/ppermute | solution.py:320
  63.4 9.7 %collective-permute-start.12 = (bf16[512,128]{1,0:T(8,128)(2,1)S(1)}, bf16[512,128]{1,0:T(8,128)(2,1)S(1)}, u32[]{:S(2)}, u32[]{:S(2)}) collective-permute-start(bf16[512,128]{1,0:T(8,128)(2,1)S(1)} %get-tuple-element.39), channel_id=1, source_target_pairs={{0,16},{4,20},{8,24},{12,28},{16,0},{20,4},{24,8},{28,12},{1,17},{... | collective-permute-start | bytes 393224 | tf_op jit(solution)/shard_map/ppermute | solution.py:320
  64.9 8.2 %collective-permute-start.13 = (bf16[512,128]{1,0:T(8,128)(2,1)S(1)}, bf16[512,128]{1,0:T(8,128)(2,1)S(1)}, u32[]{:S(2)}, u32[]{:S(2)}) collective-permute-start(bf16[512,128]{1,0:T(8,128)(2,1)S(1)} %get-tuple-element.40), channel_id=1, source_target_pairs={{0,24},{4,28},{8,16},{12,20},{16,8},{20,12},{24,0},{28,4},{1,25},{... | collective-permute-start | bytes 393224 | tf_op jit(solution)/shard_map/ppermute | solution.py:320
  66.3 10.4 %collective-permute-start.14 = (bf16[512,128]{1,0:T(8,128)(2,1)S(1)}, bf16[512,128]{1,0:T(8,128)(2,1)S(1)}, u32[]{:S(2)}, u32[]{:S(2)}) collective-permute-start(bf16[512,128]{1,0:T(8,128)(2,1)S(1)} %get-tuple-element.37.refs_0_), channel_id=1, source_target_pairs={{0,2},{1,3},{2,0},{3,1},{4,6},{5,7},{6,4},{7,5},{8,10},{9,11},{10,... | collective-permute-start | bytes 393224 | tf_op jit(solution)/shard_map/ppermute | solution.py:320
  69.2 7.5 %collective-permute-start.15 = (bf16[512,128]{1,0:T(8,128)(2,1)S(1)}, bf16[512,128]{1,0:T(8,128)(2,1)S(1)}, u32[]{:S(2)}, u32[]{:S(2)}) collective-permute-start(bf16[512,128]{1,0:T(8,128)(2,1)S(1)} %collective-permute-done.11.refs_1_), channel_id=1, source_target_pairs={{0,2},{1,3},{2,0},{3,1},{4,6},{5,7},{6,4},{7,5},{8,10},{9,11},{10,... | collective-permute-start | bytes 393224 | tf_op jit(solution)/shard_map/ppermute | solution.py:320
  73.1 5.0 %collective-permute-start.16 = (bf16[512,128]{1,0:T(8,128)(2,1)S(1)}, bf16[512,128]{1,0:T(8,128)(2,1)S(1)}, u32[]{:S(2)}, u32[]{:S(2)}) collective-permute-start(bf16[512,128]{1,0:T(8,128)(2,1)S(1)} %collective-permute-done.12.refs_2_), channel_id=1, source_target_pairs={{0,2},{1,3},{2,0},{3,1},{4,6},{5,7},{6,4},{7,5},{8,10},{9,11},{10,... | collective-permute-start | bytes 393224 | tf_op jit(solution)/shard_map/ppermute | solution.py:320
  73.1 6.4 %collective-permute-start.17 = (bf16[512,128]{1,0:T(8,128)(2,1)S(1)}, bf16[512,128]{1,0:T(8,128)(2,1)S(1)}, u32[]{:S(2)}, u32[]{:S(2)}) collective-permute-start(bf16[512,128]{1,0:T(8,128)(2,1)S(1)} %collective-permute-done.13.refs_3_), channel_id=1, source_target_pairs={{0,2},{1,3},{2,0},{3,1},{4,6},{5,7},{6,4},{7,5},{8,10},{9,11},{10,... | collective-permute-start | bytes 393224 | tf_op jit(solution)/shard_map/ppermute | solution.py:320
  81.2 2.0 %collective-permute-start.18 = (bf16[512,512]{1,0:T(8,128)(2,1)S(1)}, bf16[512,512]{1,0:T(8,128)(2,1)S(1)}, u32[]{:S(2)}, u32[]{:S(2)}) collective-permute-start(bf16[512,512]{1,0:T(8,128)(2,1)S(1)} %get-tuple-element.42), channel_id=1, source_target_pairs={{0,1},{1,0},{2,3},{3,2},{4,5},{5,4},{6,7},{7,6},{8,9},{9,8},{10,11... | collective-permute-start | bytes 1572872 | tf_op jit(solution)/shard_map/ppermute | solution.py:320

commit v4 on v3

--- a/solution.py
+++ b/solution.py
@@ -92,13 +92,19 @@
 MISMATCH = 262144.0
 
 
-def pack_kernel(place_ref, q_ref, k_ref, v_ref, ids_ref, *outs):
+def coordinates():
+    seq = lax.axis_index("seq").astype(jnp.int32)
+    return seq // 2, seq % 2, lax.axis_index("head").astype(jnp.int32)
+
+
+def pack_kernel(q_ref, k_ref, v_ref, ids_ref, *outs):
     heads = ids_ref.shape[0]
     rows, width = outs[0].shape
     parts = rows // width
+    place = coordinates()[0]
     for offset in range(heads):
         q_out, kv_out = outs[2 * offset], outs[2 * offset + 1]
-        head = lax.bitwise_xor(place_ref[0], offset)
+        head = lax.bitwise_xor(place, offset)
         columns = pl.ds(pl.multiple_of(head * width, width), width)
         kv_out[pl.ds(0, rows), :] = k_ref[:, columns]
         kv_out[pl.ds(rows, rows), :] = v_ref[:, columns]
@@ -109,7 +115,7 @@
         kv_out[pl.ds(2 * rows, ID_ROWS), :] = jnp.concatenate(lines, axis=0).astype(jnp.bfloat16)
 
 
-def pack(place, queries, keys, values, cluster_ids):
+def pack(queries, keys, values, cluster_ids):
     heads = cluster_ids.shape[0]
     rows = queries.shape[0]
     width = queries.shape[1] // heads
@@ -121,14 +127,16 @@
     outs = pl.pallas_call(
         pack_kernel,
         out_shape=tuple(pair * heads),
-        in_specs=[pl.BlockSpec(memory_space=pltpu.SMEM)] + [local_memory] * 4,
+        in_specs=[local_memory] * 4,
         out_specs=(local_memory,) * (2 * heads),
+        cost_estimate=pl.CostEstimate(flops=2700000000, bytes_accessed=8910000, transcendentals=0),
         name="pack",
-    )(place, queries, keys, values, cluster_ids)
+    )(queries, keys, values, cluster_ids)
     return outs[0::2], outs[1::2]
 
 
-def attend_kernel(scale, where_ref, *refs):
+def attend_kernel(scale, *refs):
+    place, later, _ = coordinates()
     pieces = (len(refs) - 6) // 4
     own_refs, far_refs, q_refs, out_refs = (refs[pieces * kind : pieces * (kind + 1)] for kind in range(4))
     k_all, v_all, q_all, ids_all, out_all, sems = refs[4 * pieces :]
@@ -136,7 +144,7 @@
     parts = rows // width
     tile = 256
     started = []
-    slots = [lax.bitwise_xor(where_ref[0], offset) for offset in range(pieces)]
+    slots = [lax.bitwise_xor(place, offset) for offset in range(pieces)]
     spans = [pl.ds(pl.multiple_of(slot * rows, rows), rows) for slot in slots]
 
     def fetch(source, target):
@@ -175,7 +183,6 @@
     for copy in started[2 * pieces :]:
         copy.wait()
 
-    later = where_ref[1]
     far_bias = jnp.where(later > 0, 0.0, -MISMATCH * 4.0).astype(jnp.float32)
     factor = scale * math.log2(math.e)
     contract = (((1,), (1,)), ((), ()))
@@ -213,14 +220,14 @@
         copy.wait()
 
 
-def attend(where, kv_own, kv_far, q):
+def attend(kv_own, kv_far, q):
     pieces = len(q)
     rows, width = q[0].shape
     anywhere = pl.BlockSpec(memory_space=pl.ANY)
     return pl.pallas_call(
         lambda *refs: attend_kernel(1.0 / math.sqrt(width), *refs),
         out_shape=(jax.ShapeDtypeStruct((rows, width), jnp.bfloat16),) * pieces,
-        in_specs=[pl.BlockSpec(memory_space=pltpu.SMEM)] + [anywhere] * (3 * pieces),
+        in_specs=[anywhere] * (3 * pieces),
         out_specs=(anywhere,) * pieces,
         scratch_shapes=[
             pltpu.VMEM((2, pieces * rows, 2 * width), jnp.bfloat16),
@@ -231,8 +238,9 @@
             pltpu.SemaphoreType.DMA((7 * pieces,)),
         ],
         compiler_params=pltpu.CompilerParams(vmem_limit_bytes=48 * 1024 * 1024),
+        cost_estimate=pl.CostEstimate(flops=11600000000, bytes_accessed=38280000, transcendentals=0),
         name="attend",
-    )(where, *kv_own, *kv_far, *q)
+    )(*kv_own, *kv_far, *q)
 
 
 def gather_rows(place, pieces, w_source, a_all, w_all, sems):
@@ -248,32 +256,34 @@
         copy.wait()
 
 
-def near_kernel(where_ref, w_ref, *refs):
+def near_kernel(w_ref, *refs):
     out_ref, a_all, w_all, sems = refs[-4:]
     half = w_all.shape[1]
-    columns = pl.ds(pl.multiple_of(where_ref[2] // 2 * half, half), half)
-    gather_rows(where_ref[0], refs[:-4], w_ref.at[:, columns], a_all, w_all, sems)
+    place, _, here = coordinates()
+    columns = pl.ds(pl.multiple_of(here // 2 * half, half), half)
+    gather_rows(place, refs[:-4], w_ref.at[:, columns], a_all, w_all, sems)
     out_ref[...] = jnp.dot(a_all[...], w_all[...], preferred_element_type=jnp.float32)
 
 
-def far_kernel(where_ref, w_ref, near_ref, *refs):
+def far_kernel(w_ref, near_ref, *refs):
+    place, _, here = coordinates()
     mine_ref, other_ref, a_all, w_all, total, sems = refs[-6:]
-    gather_rows(where_ref[0], refs[:-6], w_ref, a_all, w_all, sems)
+    gather_rows(place, refs[:-6], w_ref, a_all, w_all, sems)
     total[...] = near_ref[...] + jnp.dot(a_all[...], w_all[...], preferred_element_type=jnp.float32)
     width = mine_ref.shape[1]
-    core = where_ref[2] % 2
+    core = here % 2
     mine_ref[...] = total[:, pl.ds(pl.multiple_of(core * width, width), width)]
     other_ref[...] = total[:, pl.ds(pl.multiple_of((1 - core) * width, width), width)].astype(jnp.bfloat16)
 
 
-def near_sums(where, out_weight, pieces):
+def near_sums(out_weight, pieces):
     rows, width = pieces[0].shape
     depth, half = out_weight.shape[0], out_weight.shape[1] // 2
     anywhere = pl.BlockSpec(memory_space=pl.ANY)
     return pl.pallas_call(
         near_kernel,
         out_shape=jax.ShapeDtypeStruct((rows, half), jnp.float32),
-        in_specs=[pl.BlockSpec(memory_space=pltpu.SMEM)] + [anywhere] * (1 + len(pieces)),
+        in_specs=[anywhere] * (1 + len(pieces)),
         out_specs=pl.BlockSpec(memory_space=pltpu.VMEM),
         scratch_shapes=[
             pltpu.VMEM((rows, depth), jnp.bfloat16),
@@ -281,11 +291,12 @@
             pltpu.SemaphoreType.DMA((1 + len(pieces),)),
         ],
         compiler_params=pltpu.CompilerParams(vmem_limit_bytes=24 * 1024 * 1024),
+        cost_estimate=pl.CostEstimate(flops=1500000000, bytes_accessed=4950000, transcendentals=0),
         name="near_sums",
-    )(where, out_weight, *pieces)
-
-
-def far_sums(where, weights, near, pieces):
+    )(out_weight, *pieces)
+
+
+def far_sums(weights, near, pieces):
     rows, width = pieces[0].shape
     depth, half = weights.shape
     anywhere = pl.BlockSpec(memory_space=pl.ANY)
@@ -296,7 +307,7 @@
             jax.ShapeDtypeStruct((rows, half // 2), jnp.float32),
             jax.ShapeDtypeStruct((rows, half // 2), jnp.bfloat16),
         ),
-        in_specs=[pl.BlockSpec(memory_space=pltpu.SMEM), anywhere, local_memory] + [anywhere] * len(pieces),
+        in_specs=[anywhere, local_memory] + [anywhere] * len(pieces),
         out_specs=(local_memory, local_memory),
         scratch_shapes=[
             pltpu.VMEM((rows, depth), jnp.bfloat16),
@@ -305,15 +316,14 @@
             pltpu.SemaphoreType.DMA((1 + len(pieces),)),
         ],
         compiler_params=pltpu.CompilerParams(vmem_limit_bytes=24 * 1024 * 1024),
+        cost_estimate=pl.CostEstimate(flops=1800000000, bytes_accessed=5940000, transcendentals=0),
         name="far_sums",
-    )(where, weights, near, *pieces)
+    )(weights, near, *pieces)
 
 
 def head_plan(queries, keys, values, cluster_ids, out_weight):
     heads = cluster_ids.shape[0]
-    seq = lax.axis_index("seq").astype(jnp.int32)
     here = lax.axis_index("head").astype(jnp.int32)
-    where = jnp.stack([seq // 2, seq % 2, here])
 
     def swap(array, axis, bits):
         size = lax.axis_size(axis)
@@ -322,7 +332,7 @@
     def after(array, *others):
         return lax.optimization_barrier((array,) + others)[0]
 
-    q, kv = pack(where, queries, keys, values, cluster_ids)
+    q, kv = pack(queries, keys, values, cluster_ids)
     kv_own, kv_far, q_own = [kv[0]] + [None] * 3, [None] * 4, [q[0]] + [None] * 3
     kv_own[2] = swap(kv[2], "seq", 4)
     kv_own[1] = swap(kv[1], "seq", 2)
@@ -336,12 +346,12 @@
     q_own[2] = swap(after(q[2], kv_own[2]), "seq", 4)
     for offset in (3, 1):
         q_own[offset] = swap(after(q[offset], kv_own[3]), "seq", 2 * offset)
-    attended = list(attend(where, kv_own, kv_far, q_own))
+    attended = list(attend(kv_own, kv_far, q_own))
     for offset in range(1, heads):
         attended[offset] = swap(attended[offset], "seq", 2 * offset)
     across = [swap(piece, "head", 2) for piece in attended]
-    near = near_sums(where, out_weight, attended)
-    mine, other = far_sums(where, weights, near, across)
+    near = near_sums(out_weight, attended)
+    mine, other = far_sums(weights, near, across)
     return (mine + swap(other, "head", 1).astype(jnp.float32)).astype(jnp.bfloat16)
 
 

time: 84.4 us -> 80 us (0.948)
  waiting for transfers between devices: 34.7 us -> 28.1 us
  starting transfers between devices: 28.5 us -> 34.2 us
  local copies, waits for them, and re-layouts: 1.48 us -> 0.1 us
  Pallas kernels: 17.7 us -> 16.4 us
    ppermute x19, waiting for transfers between devices: 34.7 us -> 28.1 us  [swap(): lax.ppermute(array, axis, [(place, place ^ bits) for place in range(size)])]
    ppermute x19, starting transfers between devices: 28.5 us -> 34.2 us  [swap(): lax.ppermute(array, axis, [(place, place ^ bits) for place in range(size)])]
    dynamic_slice x1, local copies, waits for them, and re-layouts: 1.44 us -> 0.09 us  [head_plan(): lax.dynamic_slice_in_dim(after(out_weight, kv[1]), (1 - here // 2) * half...]
  transfers between devices with their start and end apart: 19 -> 19, of which waited for: 10 -> 9; matrix products, arithmetic and copies ran while one was open for 2% -> 0% of each run, Pallas kernels for 16% -> 15%
where the time goes in v4:
time: 80 us; the launch traced here: 79.9 us
  starting transfers between devices  34.2 us (43%)
  waiting for transfers between devices  28.1 us (35%)
  Pallas kernels  16.4 us (20%)
  other arithmetic  0.95 us (1%)
    ppermute x19, starting transfers between devices, swap(): lax.ppermute(array, axis, [(place, place ^ bits) for place in range(size)])  34.2 us
    ppermute x19, waiting for transfers between devices, swap(): lax.ppermute(array, axis, [(place, place ^ bits) for place in range(size)])  28.1 us
    pallas_call x1, Pallas kernels, attend(): pl.pallas_call(lambda *refs: attend_kernel(1.0 / math.sqrt(width), *refs)...  11.2 us
    pallas_call x1, Pallas kernels, pack(): pl.pallas_call(pack_kernel, out_shape=tuple(pair * heads), in_specs=[loca...  2.94 us
  transfers between devices with their start and end apart: 19, of which 9 were waited for; matrix products, arithmetic and copies ran while one was open for 0% of the time, Pallas kernels for 15%

profile of v4, /device:TPU:0, one launch (start us, length us, event | category | flops | bytes accessed | tf_op | source)
XLA Modules:
  0.0 79.9 jit_solution(8327630598991973406)
XLA Ops:
  0.0 2.9 %pack.1 = (bf16[512,128]{1,0:T(8,128)(2,1)}, bf16[1040,128]{1,0:T(8,128)(2,1)}, bf16[512,128]{1,0:T(8,128)(2,1)}, bf16[1040,128]{1,0:T(8,128)(2,1)}, bf16[512,12...) custom-call(bf16[512,512]{1,0:T(8,128)(2,1)} %q_ref.1, ...), custom_call_target="tpu_custom_call" | custom-call | flops 2700000000 | bytes 8910000 | tf_op jit(solution)/shard_map/pack/pallas_call | solution.py:127
  2.9 3.0 %collective-permute-start.1 = (bf16[1040,128]{1,0:T(8,128)(2,1)}, bf16[1040,128]{1,0:T(8,128)(2,1)S(1)}, u32[]{:S(2)}, u32[]{:S(2)}) collective-permute-start(bf16[1040,128]{1,0:T(8,128)(2,1)} %get-tuple-element.24), channel_id=1, source_target_pairs={{0,8},{4,12},{8,0},{12,4},{16,24},{20,28},{24,16},{28,20},{1,9},{5... | collective-permute-start | bytes 798728 | tf_op jit(solution)/shard_map/ppermute | solution.py:330
  6.0 2.6 %collective-permute-start.2 = (bf16[1040,128]{1,0:T(8,128)(2,1)}, bf16[1040,128]{1,0:T(8,128)(2,1)S(1)}, u32[]{:S(2)}, u32[]{:S(2)}) collective-permute-start(bf16[1040,128]{1,0:T(8,128)(2,1)} %get-tuple-element.27), channel_id=1, source_target_pairs={{0,16},{4,20},{8,24},{12,28},{16,0},{20,4},{24,8},{28,12},{1,17},{... | collective-permute-start | bytes 798728 | tf_op jit(solution)/shard_map/ppermute | solution.py:330
  8.6 9.6 %collective-permute-done.1.refs_1_ = bf16[1040,128]{1,0:T(8,128)(2,1)S(1)} collective-permute-done((bf16[1040,128]{1,0:T(8,128)(2,1)}, bf16[1040,128]{1,0:T(8,128)(2,1)S(1)}, u32[]{:S(2)}, u32[]{:S(2)}) %collective-permute-start.1) | collective-permute-done | bytes 266272 | tf_op jit(solution)/shard_map/ppermute | solution.py:330
  18.2 2.6 %collective-permute-start.3 = (bf16[1040,128]{1,0:T(8,128)(2,1)}, bf16[1040,128]{1,0:T(8,128)(2,1)S(1)}, u32[]{:S(2)}, u32[]{:S(2)}) collective-permute-start(bf16[1040,128]{1,0:T(8,128)(2,1)} %get-tuple-element.29), channel_id=1, source_target_pairs={{0,24},{4,28},{8,16},{12,20},{16,8},{20,12},{24,0},{28,4},{1,25},{... | collective-permute-start | bytes 798728 | tf_op jit(solution)/shard_map/ppermute | solution.py:330
  20.8 1.5 %collective-permute-start.4 = (bf16[1040,128]{1,0:T(8,128)(2,1)}, bf16[1040,128]{1,0:T(8,128)(2,1)S(1)}, u32[]{:S(2)}, u32[]{:S(2)}) collective-permute-start(bf16[1040,128]{1,0:T(8,128)(2,1)} %get-tuple-element.26.refs_0_), channel_id=1, source_target_pairs={{0,4},{4,0},{8,12},{12,8},{16,20},{20,16},{24,28},{28,24},{1,5},{5... | collective-permute-start | bytes 798728 | tf_op jit(solution)/shard_map/ppermute | solution.py:330
  22.3 0.5 collective-permute-start.6
  22.8 1.5 %collective-permute-start.5 = (bf16[1040,128]{1,0:T(8,128)(2,1)S(1)}, bf16[1040,128]{1,0:T(8,128)(2,1)}, u32[]{:S(2)}, u32[]{:S(2)}) collective-permute-start(bf16[1040,128]{1,0:T(8,128)(2,1)S(1)} %collective-permute-done.1.refs_1_), channel_id=1, source_target_pairs={{0,4},{4,0},{8,12},{12,8},{16,20},{20,16},{24,28},{28,24},{1,5},{5... | collective-permute-start | bytes 798728 | tf_op jit(solution)/shard_map/ppermute | solution.py:330
  24.3 4.9 %collective-permute-done.3.refs_3_ = bf16[1040,128]{1,0:T(8,128)(2,1)S(1)} collective-permute-done((bf16[1040,128]{1,0:T(8,128)(2,1)}, bf16[1040,128]{1,0:T(8,128)(2,1)S(1)}, u32[]{:S(2)}, u32[]{:S(2)}) %collective-permute-start.3) | collective-permute-done | bytes 266272 | tf_op jit(solution)/shard_map/ppermute | solution.py:330
  29.3 1.3 %collective-permute-start.7 = (bf16[1040,128]{1,0:T(8,128)(2,1)S(1)}, bf16[1040,128]{1,0:T(8,128)(2,1)}, u32[]{:S(2)}, u32[]{:S(2)}) collective-permute-start(bf16[1040,128]{1,0:T(8,128)(2,1)S(1)} %collective-permute-done.3.refs_3_), channel_id=1, source_target_pairs={{0,4},{4,0},{8,12},{12,8},{16,20},{20,16},{24,28},{28,24},{1,5},{5... | collective-permute-start | bytes 798728 | tf_op jit(solution)/shard_map/ppermute | solution.py:330
  30.6 6.9 %collective-permute-start.8 = (bf16[512,128]{1,0:T(8,128)(2,1)}, bf16[512,128]{1,0:T(8,128)(2,1)S(1)}, u32[]{:S(2)}, u32[]{:S(2)}) collective-permute-start(bf16[512,128]{1,0:T(8,128)(2,1)} %get-tuple-element.32), channel_id=1, source_target_pairs={{0,8},{4,12},{8,0},{12,4},{16,24},{20,28},{24,16},{28,20},{1,9},{5... | collective-permute-start | bytes 393224 | tf_op jit(solution)/shard_map/ppermute | solution.py:330
  37.5 0.3 collective-permute-done.9.refs_10_
  37.8 2.8 %collective-permute-start.10 = (bf16[512,128]{1,0:T(8,128)(2,1)}, bf16[512,128]{1,0:T(8,128)(2,1)S(1)}, u32[]{:S(2)}, u32[]{:S(2)}) collective-permute-start(bf16[512,128]{1,0:T(8,128)(2,1)} %get-tuple-element.36), channel_id=1, source_target_pairs={{0,24},{4,28},{8,16},{12,20},{16,8},{20,12},{24,0},{28,4},{1,25},{... | collective-permute-start | bytes 393224 | tf_op jit(solution)/shard_map/ppermute | solution.py:330
  40.6 0.1 constant_dynamic-slice_fusion
  40.7 1.6 %collective-permute-start = (bf16[512,1024]{1,0:T(8,128)(2,1)S(1)}, bf16[512,1024]{1,0:T(8,128)(2,1)S(1)}, u32[]{:S(2)}, u32[]{:S(2)}) collective-permute-start(bf16[512,1024]{1,0:T(8,128)(2,1)S(1)} %constant_dynamic-slice_fusion), channel_id=1, source_target_pairs={{0,2},{1,3},{2,0},{3,1},{4,6},{5,7},{6,4},{7,5},{8,10},{9,11},{10,... | collective-permute-start | bytes 3145736 | tf_op jit(solution)/shard_map/ppermute | solution.py:330
  42.3 4.1 %collective-permute-done.10.refs_11_ = bf16[512,128]{1,0:T(8,128)(2,1)S(1)} collective-permute-done((bf16[512,128]{1,0:T(8,128)(2,1)}, bf16[512,128]{1,0:T(8,128)(2,1)S(1)}, u32[]{:S(2)}, u32[]{:S(2)}) %collective-permute-start.10) | collective-permute-done | bytes 131104 | tf_op jit(solution)/shard_map/ppermute | solution.py:330
  46.4 11.2 %attend.1 = (bf16[512,128]{1,0:T(8,128)(2,1)S(1)}, bf16[512,128]{1,0:T(8,128)(2,1)S(1)}, bf16[512,128]{1,0:T(8,128)(2,1)S(1)}, bf16[512,128]{1,0:T(8,128)(2,1)S(1)}) custom-call(bf16[1040,128]{1,0:T(8,128)(2,1)S(1)} %copy-done.1, bf16[1040,128]{1,0:T(8,128)(2,1)S(1)} %collective-permute-done.1.refs_1_, bf16[1040,128]{1,0:T(8,128)(2,1)S(1)} %collective-permute-done.2.refs_2_, ...), custom_call_target="tpu_custom_call" | custom-call | flops 11600000000 | bytes 38280000 | tf_op jit(solution)/shard_map/attend/pallas_call | solution.py:227
  57.6 0.1 collective-permute-start.11
  57.7 1.8 %collective-permute-start.12 = (bf16[512,128]{1,0:T(8,128)(2,1)S(1)}, bf16[512,128]{1,0:T(8,128)(2,1)S(1)}, u32[]{:S(2)}, u32[]{:S(2)}) collective-permute-start(bf16[512,128]{1,0:T(8,128)(2,1)S(1)} %get-tuple-element.39), channel_id=1, source_target_pairs={{0,16},{4,20},{8,24},{12,28},{16,0},{20,4},{24,8},{28,12},{1,17},{... | collective-permute-start | bytes 393224 | tf_op jit(solution)/shard_map/ppermute | solution.py:330
  59.5 2.6 %collective-permute-start.13 = (bf16[512,128]{1,0:T(8,128)(2,1)S(1)}, bf16[512,128]{1,0:T(8,128)(2,1)S(1)}, u32[]{:S(2)}, u32[]{:S(2)}) collective-permute-start(bf16[512,128]{1,0:T(8,128)(2,1)S(1)} %get-tuple-element.40), channel_id=1, source_target_pairs={{0,24},{4,28},{8,16},{12,20},{16,8},{20,12},{24,0},{28,4},{1,25},{... | collective-permute-start | bytes 393224 | tf_op jit(solution)/shard_map/ppermute | solution.py:330
  62.1 1.3 %collective-permute-start.14 = (bf16[512,128]{1,0:T(8,128)(2,1)S(1)}, bf16[512,128]{1,0:T(8,128)(2,1)S(1)}, u32[]{:S(2)}, u32[]{:S(2)}) collective-permute-start(bf16[512,128]{1,0:T(8,128)(2,1)S(1)} %get-tuple-element.37.refs_0_), channel_id=1, source_target_pairs={{0,2},{1,3},{2,0},{3,1},{4,6},{5,7},{6,4},{7,5},{8,10},{9,11},{10,... | collective-permute-start | bytes 393224 | tf_op jit(solution)/shard_map/ppermute | solution.py:330
  63.4 0.6 collective-permute-done.11.refs_1_
  64.0 2.0 %collective-permute-start.15 = (bf16[512,128]{1,0:T(8,128)(2,1)S(1)}, bf16[512,128]{1,0:T(8,128)(2,1)S(1)}, u32[]{:S(2)}, u32[]{:S(2)}) collective-permute-start(bf16[512,128]{1,0:T(8,128)(2,1)S(1)} %collective-permute-done.11.refs_1_), channel_id=1, source_target_pairs={{0,2},{1,3},{2,0},{3,1},{4,6},{5,7},{6,4},{7,5},{8,10},{9,11},{10,... | collective-permute-start | bytes 393224 | tf_op jit(solution)/shard_map/ppermute | solution.py:330
  66.0 3.4 %collective-permute-done.12.refs_2_ = bf16[512,128]{1,0:T(8,128)(2,1)S(1)} collective-permute-done((bf16[512,128]{1,0:T(8,128)(2,1)S(1)}, bf16[512,128]{1,0:T(8,128)(2,1)S(1)}, u32[]{:S(2)}, u32[]{:S(2)}) %collective-permute-start.12) | collective-permute-done | bytes 131104 | tf_op jit(solution)/shard_map/ppermute | solution.py:330
  69.4 1.2 %collective-permute-start.16 = (bf16[512,128]{1,0:T(8,128)(2,1)S(1)}, bf16[512,128]{1,0:T(8,128)(2,1)S(1)}, u32[]{:S(2)}, u32[]{:S(2)}) collective-permute-start(bf16[512,128]{1,0:T(8,128)(2,1)S(1)} %collective-permute-done.12.refs_2_), channel_id=1, source_target_pairs={{0,2},{1,3},{2,0},{3,1},{4,6},{5,7},{6,4},{7,5},{8,10},{9,11},{10,... | collective-permute-start | bytes 393224 | tf_op jit(solution)/shard_map/ppermute | solution.py:330
  70.5 0.9 %collective-permute-start.17 = (bf16[512,128]{1,0:T(8,128)(2,1)S(1)}, bf16[512,128]{1,0:T(8,128)(2,1)S(1)}, u32[]{:S(2)}, u32[]{:S(2)}) collective-permute-start(bf16[512,128]{1,0:T(8,128)(2,1)S(1)} %collective-permute-done.13.refs_3_), channel_id=1, source_target_pairs={{0,2},{1,3},{2,0},{3,1},{4,6},{5,7},{6,4},{7,5},{8,10},{9,11},{10,... | collective-permute-start | bytes 393224 | tf_op jit(solution)/shard_map/ppermute | solution.py:330
  71.4 1.1 %near_sums.1.near_ref = f32[512,1024]{1,0:T(8,128)S(1)} custom-call(bf16[512,2048]{1,0:T(8,128)(2,1)S(1)} %copy-done, bf16[512,128]{1,0:T(8,128)(2,1)S(1)} %get-tuple-element.37.refs_0_, bf16[512,128]{1,0:T(8,128)(2,1)S(1)} %collective-permute-done.11.refs_1_, bf16[512,128]{1,0:T(8,128)(2,1)S(1)} %collective-permute-done.12.refs_2_, ...), custom_call_target="tpu_custom_call" | custom-call | flops 1500000000 | bytes 4950000 | tf_op jit(solution)/shard_map/near_sums/pallas_call | solution.py:283
  72.5 1.8 %collective-permute-done.16.refs_2_ = bf16[512,128]{1,0:T(8,128)(2,1)S(1)} collective-permute-done((bf16[512,128]{1,0:T(8,128)(2,1)S(1)}, bf16[512,128]{1,0:T(8,128)(2,1)S(1)}, u32[]{:S(2)}, u32[]{:S(2)}) %collective-permute-start.16) | collective-permute-done | bytes 131104 | tf_op jit(solution)/shard_map/ppermute | solution.py:330
  74.4 1.4 %collective-permute-done.17.refs_3_ = bf16[512,128]{1,0:T(8,128)(2,1)S(1)} collective-permute-done((bf16[512,128]{1,0:T(8,128)(2,1)S(1)}, bf16[512,128]{1,0:T(8,128)(2,1)S(1)}, u32[]{:S(2)}, u32[]{:S(2)}) %collective-permute-start.17) | collective-permute-done | bytes 131104 | tf_op jit(solution)/shard_map/ppermute | solution.py:330
  75.8 1.2 %far_sums.1 = (f32[512,512]{1,0:T(8,128)S(1)}, bf16[512,512]{1,0:T(8,128)(2,1)S(1)}) custom-call(bf16[512,1024]{1,0:T(8,128)(2,1)S(1)} %collective-permute-done.w_ref, f32[512,1024]{1,0:T(8,128)S(1)} %near_sums.1.near_ref, bf16[512,128]{1,0:T(8,128)(2,1)S(1)} %collective-permute-done.14.refs_0_, bf16[512,128]{1,0:T(8,128)(2,1)S(1)} %collective-permute-done.15.refs_1_, ...), custom_call_target="tpu_custom_call" | custom-call | flops 1800000000 | bytes 5940000 | tf_op jit(solution)/shard_map/far_sums/pallas_call | solution.py:304
  77.0 1.9 %collective-permute-done.18 = bf16[512,512]{1,0:T(8,128)(2,1)S(1)} collective-permute-done((bf16[512,512]{1,0:T(8,128)(2,1)S(1)}, bf16[512,512]{1,0:T(8,128)(2,1)S(1)}, u32[]{:S(2)}, u32[]{:S(2)}) %collective-permute-start.18) | collective-permute-done | bytes 524320 | tf_op jit(solution)/shard_map/ppermute | solution.py:330
  78.9 1.0 %add_convert_fusion = bf16[512,512]{1,0:T(8,128)(2,1)} fusion(f32[512,512]{1,0:T(8,128)S(1)} %get-tuple-element.41, bf16[512,512]{1,0:T(8,128)(2,1)S(1)} %collective-permute-done.18), kind=kLoop, calls=%fused_computation | loop fusion | flops 786432 | bytes 2097152 | tf_op jit(solution)/shard_map/convert_element_type | solution.py:355
  (18 shorter events, 0.1 us)
Async XLA Ops:
  0.0 40.6 %copy-start = (bf16[512,2048]{1,0:T(8,128)(2,1)S(1)}, bf16[512,2048]{1,0:T(8,128)(2,1)}, u32[]{:S(2)}) copy-start(bf16[512,2048]{1,0:T(8,128)(2,1)} %w_ref.1) | copy-start | bytes 6291460
  2.9 43.5 %copy-start.1 = (bf16[1040,128]{1,0:T(8,128)(2,1)S(1)}, bf16[1040,128]{1,0:T(8,128)(2,1)}, u32[]{:S(2)}) copy-start(bf16[1040,128]{1,0:T(8,128)(2,1)} %get-tuple-element.26.refs_0_) | copy-start | bytes 798724
  2.9 15.2 %collective-permute-start.1 = (bf16[1040,128]{1,0:T(8,128)(2,1)}, bf16[1040,128]{1,0:T(8,128)(2,1)S(1)}, u32[]{:S(2)}, u32[]{:S(2)}) collective-permute-start(bf16[1040,128]{1,0:T(8,128)(2,1)} %get-tuple-element.24), channel_id=1, source_target_pairs={{0,8},{4,12},{8,0},{12,4},{16,24},{20,28},{24,16},{28,20},{1,9},{5... | collective-permute-start | bytes 798728 | tf_op jit(solution)/shard_map/ppermute | solution.py:330
  6.0 16.3 %collective-permute-start.2 = (bf16[1040,128]{1,0:T(8,128)(2,1)}, bf16[1040,128]{1,0:T(8,128)(2,1)S(1)}, u32[]{:S(2)}, u32[]{:S(2)}) collective-permute-start(bf16[1040,128]{1,0:T(8,128)(2,1)} %get-tuple-element.27), channel_id=1, source_target_pairs={{0,16},{4,20},{8,24},{12,28},{16,0},{20,4},{24,8},{28,12},{1,17},{... | collective-permute-start | bytes 798728 | tf_op jit(solution)/shard_map/ppermute | solution.py:330
  18.2 11.1 %collective-permute-start.3 = (bf16[1040,128]{1,0:T(8,128)(2,1)}, bf16[1040,128]{1,0:T(8,128)(2,1)S(1)}, u32[]{:S(2)}, u32[]{:S(2)}) collective-permute-start(bf16[1040,128]{1,0:T(8,128)(2,1)} %get-tuple-element.29), channel_id=1, source_target_pairs={{0,24},{4,28},{8,16},{12,20},{16,8},{20,12},{24,0},{28,4},{1,25},{... | collective-permute-start | bytes 798728 | tf_op jit(solution)/shard_map/ppermute | solution.py:330
  20.8 9.8 %collective-permute-start.4 = (bf16[1040,128]{1,0:T(8,128)(2,1)}, bf16[1040,128]{1,0:T(8,128)(2,1)S(1)}, u32[]{:S(2)}, u32[]{:S(2)}) collective-permute-start(bf16[1040,128]{1,0:T(8,128)(2,1)} %get-tuple-element.26.refs_0_), channel_id=1, source_target_pairs={{0,4},{4,0},{8,12},{12,8},{16,20},{20,16},{24,28},{28,24},{1,5},{5... | collective-permute-start | bytes 798728 | tf_op jit(solution)/shard_map/ppermute | solution.py:330
  22.3 15.6 %collective-permute-start.9 = (bf16[512,128]{1,0:T(8,128)(2,1)}, bf16[512,128]{1,0:T(8,128)(2,1)}, u32[]{:S(2)}, u32[]{:S(2)}) collective-permute-start(bf16[512,128]{1,0:T(8,128)(2,1)} %get-tuple-element.34), channel_id=1, source_target_pairs={{0,16},{4,20},{8,24},{12,28},{16,0},{20,4},{24,8},{28,12},{1,17},{... | collective-permute-start | bytes 393224 | tf_op jit(solution)/shard_map/ppermute | solution.py:330
  22.3 18.4 %collective-permute-start.6 = (bf16[1040,128]{1,0:T(8,128)(2,1)S(1)}, bf16[1040,128]{1,0:T(8,128)(2,1)}, u32[]{:S(2)}, u32[]{:S(2)}) collective-permute-start(bf16[1040,128]{1,0:T(8,128)(2,1)S(1)} %collective-permute-done.2.refs_2_), channel_id=1, source_target_pairs={{0,4},{4,0},{8,12},{12,8},{16,20},{20,16},{24,28},{28,24},{1,5},{5... | collective-permute-start | bytes 798728 | tf_op jit(solution)/shard_map/ppermute | solution.py:330
  22.8 19.5 %collective-permute-start.5 = (bf16[1040,128]{1,0:T(8,128)(2,1)S(1)}, bf16[1040,128]{1,0:T(8,128)(2,1)}, u32[]{:S(2)}, u32[]{:S(2)}) collective-permute-start(bf16[1040,128]{1,0:T(8,128)(2,1)S(1)} %collective-permute-done.1.refs_1_), channel_id=1, source_target_pairs={{0,4},{4,0},{8,12},{12,8},{16,20},{20,16},{24,28},{28,24},{1,5},{5... | collective-permute-start | bytes 798728 | tf_op jit(solution)/shard_map/ppermute | solution.py:330
  29.3 17.2 %collective-permute-start.7 = (bf16[1040,128]{1,0:T(8,128)(2,1)S(1)}, bf16[1040,128]{1,0:T(8,128)(2,1)}, u32[]{:S(2)}, u32[]{:S(2)}) collective-permute-start(bf16[1040,128]{1,0:T(8,128)(2,1)S(1)} %collective-permute-done.3.refs_3_), channel_id=1, source_target_pairs={{0,4},{4,0},{8,12},{12,8},{16,20},{20,16},{24,28},{28,24},{1,5},{5... | collective-permute-start | bytes 798728 | tf_op jit(solution)/shard_map/ppermute | solution.py:330
  30.6 15.8 %copy-start.2 = (bf16[512,128]{1,0:T(8,128)(2,1)S(1)}, bf16[512,128]{1,0:T(8,128)(2,1)}, u32[]{:S(2)}) copy-start(bf16[512,128]{1,0:T(8,128)(2,1)} %get-tuple-element.30.refs_8_) | copy-start | bytes 393220
  30.6 11.7 %collective-permute-start.8 = (bf16[512,128]{1,0:T(8,128)(2,1)}, bf16[512,128]{1,0:T(8,128)(2,1)S(1)}, u32[]{:S(2)}, u32[]{:S(2)}) collective-permute-start(bf16[512,128]{1,0:T(8,128)(2,1)} %get-tuple-element.32), channel_id=1, source_target_pairs={{0,8},{4,12},{8,0},{12,4},{16,24},{20,28},{24,16},{28,20},{1,9},{5... | collective-permute-start | bytes 393224 | tf_op jit(solution)/shard_map/ppermute | solution.py:330
  37.8 8.6 %collective-permute-start.10 = (bf16[512,128]{1,0:T(8,128)(2,1)}, bf16[512,128]{1,0:T(8,128)(2,1)S(1)}, u32[]{:S(2)}, u32[]{:S(2)}) collective-permute-start(bf16[512,128]{1,0:T(8,128)(2,1)} %get-tuple-element.36), channel_id=1, source_target_pairs={{0,24},{4,28},{8,16},{12,20},{16,8},{20,12},{24,0},{28,4},{1,25},{... | collective-permute-start | bytes 393224 | tf_op jit(solution)/shard_map/ppermute | solution.py:330
  40.7 31.8 %collective-permute-start = (bf16[512,1024]{1,0:T(8,128)(2,1)S(1)}, bf16[512,1024]{1,0:T(8,128)(2,1)S(1)}, u32[]{:S(2)}, u32[]{:S(2)}) collective-permute-start(bf16[512,1024]{1,0:T(8,128)(2,1)S(1)} %constant_dynamic-slice_fusion), channel_id=1, source_target_pairs={{0,2},{1,3},{2,0},{3,1},{4,6},{5,7},{6,4},{7,5},{8,10},{9,11},{10,... | collective-permute-start | bytes 3145736 | tf_op jit(solution)/shard_map/ppermute | solution.py:330
  57.6 6.4 %collective-permute-start.11 = (bf16[512,128]{1,0:T(8,128)(2,1)S(1)}, bf16[512,128]{1,0:T(8,128)(2,1)S(1)}, u32[]{:S(2)}, u32[]{:S(2)}) collective-permute-start(bf16[512,128]{1,0:T(8,128)(2,1)S(1)} %get-tuple-element.38), channel_id=1, source_target_pairs={{0,8},{4,12},{8,0},{12,4},{16,24},{20,28},{24,16},{28,20},{1,9},{5... | collective-permute-start | bytes 393224 | tf_op jit(solution)/shard_map/ppermute | solution.py:330
  57.7 11.7 %collective-permute-start.12 = (bf16[512,128]{1,0:T(8,128)(2,1)S(1)}, bf16[512,128]{1,0:T(8,128)(2,1)S(1)}, u32[]{:S(2)}, u32[]{:S(2)}) collective-permute-start(bf16[512,128]{1,0:T(8,128)(2,1)S(1)} %get-tuple-element.39), channel_id=1, source_target_pairs={{0,16},{4,20},{8,24},{12,28},{16,0},{20,4},{24,8},{28,12},{1,17},{... | collective-permute-start | bytes 393224 | tf_op jit(solution)/shard_map/ppermute | solution.py:330
  59.5 11.0 %collective-permute-start.13 = (bf16[512,128]{1,0:T(8,128)(2,1)S(1)}, bf16[512,128]{1,0:T(8,128)(2,1)S(1)}, u32[]{:S(2)}, u32[]{:S(2)}) collective-permute-start(bf16[512,128]{1,0:T(8,128)(2,1)S(1)} %get-tuple-element.40), channel_id=1, source_target_pairs={{0,24},{4,28},{8,16},{12,20},{16,8},{20,12},{24,0},{28,4},{1,25},{... | collective-permute-start | bytes 393224 | tf_op jit(solution)/shard_map/ppermute | solution.py:330
  62.1 10.4 %collective-permute-start.14 = (bf16[512,128]{1,0:T(8,128)(2,1)S(1)}, bf16[512,128]{1,0:T(8,128)(2,1)S(1)}, u32[]{:S(2)}, u32[]{:S(2)}) collective-permute-start(bf16[512,128]{1,0:T(8,128)(2,1)S(1)} %get-tuple-element.37.refs_0_), channel_id=1, source_target_pairs={{0,2},{1,3},{2,0},{3,1},{4,6},{5,7},{6,4},{7,5},{8,10},{9,11},{10,... | collective-permute-start | bytes 393224 | tf_op jit(solution)/shard_map/ppermute | solution.py:330
  64.0 8.5 %collective-permute-start.15 = (bf16[512,128]{1,0:T(8,128)(2,1)S(1)}, bf16[512,128]{1,0:T(8,128)(2,1)S(1)}, u32[]{:S(2)}, u32[]{:S(2)}) collective-permute-start(bf16[512,128]{1,0:T(8,128)(2,1)S(1)} %collective-permute-done.11.refs_1_), channel_id=1, source_target_pairs={{0,2},{1,3},{2,0},{3,1},{4,6},{5,7},{6,4},{7,5},{8,10},{9,11},{10,... | collective-permute-start | bytes 393224 | tf_op jit(solution)/shard_map/ppermute | solution.py:330
  69.4 5.0 %collective-permute-start.16 = (bf16[512,128]{1,0:T(8,128)(2,1)S(1)}, bf16[512,128]{1,0:T(8,128)(2,1)S(1)}, u32[]{:S(2)}, u32[]{:S(2)}) collective-permute-start(bf16[512,128]{1,0:T(8,128)(2,1)S(1)} %collective-permute-done.12.refs_2_), channel_id=1, source_target_pairs={{0,2},{1,3},{2,0},{3,1},{4,6},{5,7},{6,4},{7,5},{8,10},{9,11},{10,... | collective-permute-start | bytes 393224 | tf_op jit(solution)/shard_map/ppermute | solution.py:330
  70.5 5.2 %collective-permute-start.17 = (bf16[512,128]{1,0:T(8,128)(2,1)S(1)}, bf16[512,128]{1,0:T(8,128)(2,1)S(1)}, u32[]{:S(2)}, u32[]{:S(2)}) collective-permute-start(bf16[512,128]{1,0:T(8,128)(2,1)S(1)} %collective-permute-done.13.refs_3_), channel_id=1, source_target_pairs={{0,2},{1,3},{2,0},{3,1},{4,6},{5,7},{6,4},{7,5},{8,10},{9,11},{10,... | collective-permute-start | bytes 393224 | tf_op jit(solution)/shard_map/ppermute | solution.py:330
  76.9 2.0 %collective-permute-start.18 = (bf16[512,512]{1,0:T(8,128)(2,1)S(1)}, bf16[512,512]{1,0:T(8,128)(2,1)S(1)}, u32[]{:S(2)}, u32[]{:S(2)}) collective-permute-start(bf16[512,512]{1,0:T(8,128)(2,1)S(1)} %get-tuple-element.42), channel_id=1, source_target_pairs={{0,1},{1,0},{2,3},{3,2},{4,5},{5,4},{6,7},{7,6},{8,9},{9,8},{10,11... | collective-permute-start | bytes 1572872 | tf_op jit(solution)/shard_map/ppermute | solution.py:330

commit v5 on v4

--- a/solution.py
+++ b/solution.py
@@ -143,33 +143,43 @@
     rows, width = q_refs[0].shape
     parts = rows // width
     tile = 256
-    started = []
     slots = [lax.bitwise_xor(place, offset) for offset in range(pieces)]
-    spans = [pl.ds(pl.multiple_of(slot * rows, rows), rows) for slot in slots]
-
-    def fetch(source, target):
-        copy = pltpu.make_async_copy(source, target, sems.at[len(started)])
-        copy.start()
-        started.append(copy)
-
-    for side, side_refs in enumerate((own_refs, far_refs)):
-        for ref, slot in zip(side_refs, slots):
-            fetch(ref.at[pl.ds(2 * rows, ID_ROWS)], ids_all.at[side, slot])
-    for ref, span in zip(q_refs, spans):
-        fetch(ref, q_all.at[span, pl.ds(0, width)])
-    for side, side_refs in enumerate((own_refs, far_refs)):
-        for ref, span in zip(side_refs, spans):
-            fetch(ref.at[pl.ds(0, rows)], k_all.at[side, span, pl.ds(0, width)])
-            fetch(ref.at[pl.ds(rows, rows)], v_all.at[side, span, pl.ds(0, width)])
+    sides = (own_refs, far_refs)
+
+    def copies_of(offset, slot):
+        span = pl.ds(slot * rows if isinstance(slot, int) else pl.multiple_of(slot * rows, rows), rows)
+        pairs = []
+        for side, side_refs in enumerate(sides):
+            ref = side_refs[offset]
+            pairs.append((ref.at[pl.ds(2 * rows, ID_ROWS)], ids_all.at[side, slot]))
+        pairs.append((q_refs[offset], q_all.at[span, pl.ds(0, width)]))
+        for side, side_refs in enumerate(sides):
+            ref = side_refs[offset]
+            pairs.append((ref.at[pl.ds(0, rows)], k_all.at[side, span, pl.ds(0, width)]))
+            pairs.append((ref.at[pl.ds(rows, rows)], v_all.at[side, span, pl.ds(0, width)]))
+        return [
+            pltpu.make_async_copy(source, target, sems.at[kind, slot]) for kind, (source, target) in enumerate(pairs)
+        ]
+
+    for offset, slot in enumerate(slots):
+        for copy in copies_of(offset, slot):
+            copy.start()
     v_all[:, :, width:] = jnp.ones((2, pieces * rows, width), jnp.bfloat16)
-    for copy in started[: 2 * pieces]:
-        copy.wait()
     lane = lax.broadcasted_iota(jnp.int32, (width, width), 1)
     shift = jnp.minimum(lane // 2, 8)
     odd = lane % 2
     live = lane < 16
-    for side in range(2):
-        for piece in range(pieces):
+    far_bias = jnp.where(later > 0, 0.0, -MISMATCH * 4.0).astype(jnp.float32)
+    factor = scale * math.log2(math.e)
+    contract = (((1,), (1,)), ((), ()))
+    row = lax.broadcasted_iota(jnp.int32, (tile, tile), 0)
+    column = lax.broadcasted_iota(jnp.int32, (tile, tile), 1)
+
+    def ready(piece):
+        waits = copies_of(0, piece)
+        for copy in waits[:2]:
+            copy.wait()
+        for side in range(2):
             ids = ids_all[side, piece].astype(jnp.float32)
             for part in range(parts):
                 line = jnp.broadcast_to(ids[part : part + 1], (width, width)).T.astype(jnp.int32)
@@ -180,43 +190,55 @@
                 if side == 0:
                     other = jnp.where(live, (flag.astype(jnp.float32) - 1.0) * MISMATCH, 0.0)
                     q_all[here, width:] = other.astype(jnp.bfloat16)
-    for copy in started[2 * pieces :]:
-        copy.wait()
-
-    far_bias = jnp.where(later > 0, 0.0, -MISMATCH * 4.0).astype(jnp.float32)
-    factor = scale * math.log2(math.e)
-    contract = (((1,), (1,)), ((), ()))
+        for copy in waits[2:]:
+            copy.wait()
+
+    def scores_of(piece, step):
+        edge = piece * rows + step * tile
+        q = q_all[pl.ds(edge, tile), :]
+        own = lax.dot_general(q, k_all[0, pl.ds(0, edge + tile), :], contract, preferred_element_type=jnp.float32)
+        far = lax.dot_general(
+            q, k_all[1, pl.ds(0, (piece + 1) * rows), :], contract, preferred_element_type=jnp.float32
+        )
+        return own, far
+
+    def finish(piece, step, own, far):
+        before = piece * rows
+        edge = before + step * tile
+        diagonal = jnp.where(column <= row, own[:, edge:], -MISMATCH * 4.0)
+        last = far[:, before:] + far_bias
+        own = jnp.concatenate([own[:, :edge], diagonal], axis=1) if edge else diagonal
+        far = jnp.concatenate([far[:, :before], last], axis=1) if before else last
+        top = own[:, :width]
+        for start in range(width, own.shape[1], width):
+            top = jnp.maximum(top, own[:, start : start + width])
+        for start in range(0, far.shape[1], width):
+            top = jnp.maximum(top, far[:, start : start + width])
+        top = jnp.max(top, axis=1, keepdims=True) * factor
+        own = jnp.exp2(own * factor - top).astype(jnp.bfloat16)
+        far = jnp.exp2(far * factor - top).astype(jnp.bfloat16)
+        total = jnp.dot(own, v_all[0, pl.ds(0, own.shape[1]), :], preferred_element_type=jnp.float32)
+        total = total + jnp.dot(far, v_all[1, pl.ds(0, far.shape[1]), :], preferred_element_type=jnp.float32)
+        result = total[:, :width] / total[:, width:]
+        out_all[piece, pl.ds(step * tile, tile), :] = result.astype(jnp.bfloat16)
+
+    pending = None
     for piece in range(pieces):
-        span = (piece + 1) * rows
+        ready(piece)
+    for piece in range(pieces):
         for step in range(rows // tile):
-            q = q_all[pl.ds(piece * rows + step * tile, tile), :]
-            own = lax.dot_general(q, k_all[0, pl.ds(0, span), :], contract, preferred_element_type=jnp.float32)
-            far = lax.dot_general(q, k_all[1, pl.ds(0, span), :], contract, preferred_element_type=jnp.float32)
-            before = piece * rows
-            row = lax.broadcasted_iota(jnp.int32, (tile, rows), 0) + step * tile
-            column = lax.broadcasted_iota(jnp.int32, (tile, rows), 1)
-            diagonal = jnp.where(column <= row, own[:, before:], -MISMATCH * 4.0)
-            last = far[:, before:] + far_bias
-            if piece:
-                own = jnp.concatenate([own[:, :before], diagonal], axis=1)
-                far = jnp.concatenate([far[:, :before], last], axis=1)
-            else:
-                own, far = diagonal, last
-            top = jnp.maximum(own[:, :width], far[:, :width])
-            for start in range(width, span, width):
-                top = jnp.maximum(top, own[:, start : start + width])
-                top = jnp.maximum(top, far[:, start : start + width])
-            top = jnp.max(top, axis=1, keepdims=True) * factor
-            own = jnp.exp2(own * factor - top).astype(jnp.bfloat16)
-            far = jnp.exp2(far * factor - top).astype(jnp.bfloat16)
-            total = jnp.dot(own, v_all[0, pl.ds(0, span), :], preferred_element_type=jnp.float32)
-            total = total + jnp.dot(far, v_all[1, pl.ds(0, span), :], preferred_element_type=jnp.float32)
-            result = total[:, :width] / total[:, width:]
-            out_all[piece, pl.ds(step * tile, tile), :] = result.astype(jnp.bfloat16)
-    started.clear()
-    for ref, slot in zip(out_refs, slots):
-        fetch(out_all.at[slot], ref)
-    for copy in started:
+            scores = scores_of(piece, step)
+            if pending is not None:
+                finish(*pending)
+            pending = (piece, step) + scores
+    finish(*pending)
+    copies = [
+        pltpu.make_async_copy(out_all.at[slot], ref, sems.at[0, offset])
+        for offset, (slot, ref) in enumerate(zip(slots, out_refs))
+    ]
+    for copy in copies:
+        copy.start()
+    for copy in copies:
         copy.wait()
 
 
@@ -235,10 +257,10 @@
             pltpu.VMEM((pieces * rows, 2 * width), jnp.bfloat16),
             pltpu.VMEM((2, pieces, ID_ROWS, width), jnp.bfloat16),
             pltpu.VMEM((pieces, rows, width), jnp.bfloat16),
-            pltpu.SemaphoreType.DMA((7 * pieces,)),
+            pltpu.SemaphoreType.DMA((7, pieces)),
         ],
         compiler_params=pltpu.CompilerParams(vmem_limit_bytes=48 * 1024 * 1024),
-        cost_estimate=pl.CostEstimate(flops=11600000000, bytes_accessed=38280000, transcendentals=0),
+        cost_estimate=pl.CostEstimate(flops=4000000000, bytes_accessed=13200000, transcendentals=0),
         name="attend",
     )(*kv_own, *kv_far, *q)
 

time: 80 us -> 78.8 us (0.985)
  starting transfers between devices: 34.2 us -> 31.4 us
  waiting for transfers between devices: 28.1 us -> 30.9 us
  Pallas kernels: 16.4 us -> 15.3 us
    ppermute x19, starting transfers between devices: 34.2 us -> 31.4 us  [swap(): lax.ppermute(array, axis, [(place, place ^ bits) for place in range(size)])]
    ppermute x19, waiting for transfers between devices: 28.1 us -> 30.9 us  [swap(): lax.ppermute(array, axis, [(place, place ^ bits) for place in range(size)])]
    pallas_call x1, Pallas kernels: 11.2 us -> 10.1 us  [attend(): pl.pallas_call(lambda *refs: attend_kernel(1.0 / math.sqrt(width), *refs)...]
  transfers between devices with their start and end apart: 19 -> 19, of which waited for: 9 -> 9; matrix products, arithmetic and copies ran while one was open for 0% -> 0% of each run, Pallas kernels for 15% -> 14%
where the time goes in v5:
time: 78.8 us; the launch traced here: 78.7 us
  starting transfers between devices  31.4 us (40%)
  waiting for transfers between devices  30.9 us (39%)
  Pallas kernels  15.3 us (19%)
  other arithmetic  0.95 us (1%)
    ppermute x19, starting transfers between devices, swap(): lax.ppermute(array, axis, [(place, place ^ bits) for place in range(size)])  31.4 us
    ppermute x19, waiting for transfers between devices, swap(): lax.ppermute(array, axis, [(place, place ^ bits) for place in range(size)])  30.9 us
    pallas_call x1, Pallas kernels, attend(): pl.pallas_call(lambda *refs: attend_kernel(1.0 / math.sqrt(width), *refs)...  10.1 us
    pallas_call x1, Pallas kernels, pack(): pl.pallas_call(pack_kernel, out_shape=tuple(pair * heads), in_specs=[loca...  2.95 us
  transfers between devices with their start and end apart: 19, of which 9 were waited for; matrix products, arithmetic and copies ran while one was open for 0% of the time, Pallas kernels for 14%

profile of v5, /device:TPU:0, one launch (start us, length us, event | category | flops | bytes accessed | tf_op | source)
XLA Modules:
  0.0 78.7 jit_solution(9582796810621375378)
XLA Ops:
  0.0 3.0 %pack.1 = (bf16[512,128]{1,0:T(8,128)(2,1)}, bf16[1040,128]{1,0:T(8,128)(2,1)}, bf16[512,128]{1,0:T(8,128)(2,1)}, bf16[1040,128]{1,0:T(8,128)(2,1)}, bf16[512,12...) custom-call(bf16[512,512]{1,0:T(8,128)(2,1)} %q_ref.1, ...), custom_call_target="tpu_custom_call" | custom-call | flops 2700000000 | bytes 8910000 | tf_op jit(solution)/shard_map/pack/pallas_call | solution.py:127
  3.0 3.1 %collective-permute-start.1 = (bf16[1040,128]{1,0:T(8,128)(2,1)}, bf16[1040,128]{1,0:T(8,128)(2,1)S(1)}, u32[]{:S(2)}, u32[]{:S(2)}) collective-permute-start(bf16[1040,128]{1,0:T(8,128)(2,1)} %get-tuple-element.24), channel_id=1, source_target_pairs={{0,8},{4,12},{8,0},{12,4},{16,24},{20,28},{24,16},{28,20},{1,9},{5... | collective-permute-start | bytes 798728 | tf_op jit(solution)/shard_map/ppermute | solution.py:352
  6.1 2.6 %collective-permute-start.2 = (bf16[1040,128]{1,0:T(8,128)(2,1)}, bf16[1040,128]{1,0:T(8,128)(2,1)S(1)}, u32[]{:S(2)}, u32[]{:S(2)}) collective-permute-start(bf16[1040,128]{1,0:T(8,128)(2,1)} %get-tuple-element.27), channel_id=1, source_target_pairs={{0,16},{4,20},{8,24},{12,28},{16,0},{20,4},{24,8},{28,12},{1,17},{... | collective-permute-start | bytes 798728 | tf_op jit(solution)/shard_map/ppermute | solution.py:352
  8.7 1.5 %collective-permute-start.4 = (bf16[1040,128]{1,0:T(8,128)(2,1)}, bf16[1040,128]{1,0:T(8,128)(2,1)S(1)}, u32[]{:S(2)}, u32[]{:S(2)}) collective-permute-start(bf16[1040,128]{1,0:T(8,128)(2,1)} %get-tuple-element.26.refs_0_), channel_id=1, source_target_pairs={{0,4},{4,0},{8,12},{12,8},{16,20},{20,16},{24,28},{28,24},{1,5},{5... | collective-permute-start | bytes 798728 | tf_op jit(solution)/shard_map/ppermute | solution.py:352
  10.2 8.1 %collective-permute-done.1.refs_1_ = bf16[1040,128]{1,0:T(8,128)(2,1)S(1)} collective-permute-done((bf16[1040,128]{1,0:T(8,128)(2,1)}, bf16[1040,128]{1,0:T(8,128)(2,1)S(1)}, u32[]{:S(2)}, u32[]{:S(2)}) %collective-permute-start.1) | collective-permute-done | bytes 266272 | tf_op jit(solution)/shard_map/ppermute | solution.py:352
  18.3 2.6 %collective-permute-start.3 = (bf16[1040,128]{1,0:T(8,128)(2,1)}, bf16[1040,128]{1,0:T(8,128)(2,1)S(1)}, u32[]{:S(2)}, u32[]{:S(2)}) collective-permute-start(bf16[1040,128]{1,0:T(8,128)(2,1)} %get-tuple-element.29), channel_id=1, source_target_pairs={{0,24},{4,28},{8,16},{12,20},{16,8},{20,12},{24,0},{28,4},{1,25},{... | collective-permute-start | bytes 798728 | tf_op jit(solution)/shard_map/ppermute | solution.py:352
  20.9 0.1 constant_dynamic-slice_fusion
  21.0 1.6 %collective-permute-start = (bf16[512,1024]{1,0:T(8,128)(2,1)S(1)}, bf16[512,1024]{1,0:T(8,128)(2,1)S(1)}, u32[]{:S(2)}, u32[]{:S(2)}) collective-permute-start(bf16[512,1024]{1,0:T(8,128)(2,1)S(1)} %constant_dynamic-slice_fusion), channel_id=1, source_target_pairs={{0,2},{1,3},{2,0},{3,1},{4,6},{5,7},{6,4},{7,5},{8,10},{9,11},{10,... | collective-permute-start | bytes 3145736 | tf_op jit(solution)/shard_map/ppermute | solution.py:352
  22.6 1.5 %collective-permute-start.6 = (bf16[1040,128]{1,0:T(8,128)(2,1)S(1)}, bf16[1040,128]{1,0:T(8,128)(2,1)S(1)}, u32[]{:S(2)}, u32[]{:S(2)}) collective-permute-start(bf16[1040,128]{1,0:T(8,128)(2,1)S(1)} %collective-permute-done.2.refs_2_), channel_id=1, source_target_pairs={{0,4},{4,0},{8,12},{12,8},{16,20},{20,16},{24,28},{28,24},{1,5},{5... | collective-permute-start | bytes 798728 | tf_op jit(solution)/shard_map/ppermute | solution.py:352
  24.1 0.5 collective-permute-start.5
  24.6 3.3 %collective-permute-done.3.refs_3_ = bf16[1040,128]{1,0:T(8,128)(2,1)S(1)} collective-permute-done((bf16[1040,128]{1,0:T(8,128)(2,1)}, bf16[1040,128]{1,0:T(8,128)(2,1)S(1)}, u32[]{:S(2)}, u32[]{:S(2)}) %collective-permute-start.3) | collective-permute-done | bytes 266272 | tf_op jit(solution)/shard_map/ppermute | solution.py:352
  28.0 1.3 %collective-permute-start.7 = (bf16[1040,128]{1,0:T(8,128)(2,1)S(1)}, bf16[1040,128]{1,0:T(8,128)(2,1)S(1)}, u32[]{:S(2)}, u32[]{:S(2)}) collective-permute-start(bf16[1040,128]{1,0:T(8,128)(2,1)S(1)} %collective-permute-done.3.refs_3_), channel_id=1, source_target_pairs={{0,4},{4,0},{8,12},{12,8},{16,20},{20,16},{24,28},{28,24},{1,5},{5... | collective-permute-start | bytes 798728 | tf_op jit(solution)/shard_map/ppermute | solution.py:352
  29.3 6.0 %collective-permute-start.9 = (bf16[512,128]{1,0:T(8,128)(2,1)S(1)}, bf16[512,128]{1,0:T(8,128)(2,1)S(1)}, u32[]{:S(2)}, u32[]{:S(2)}) collective-permute-start(bf16[512,128]{1,0:T(8,128)(2,1)S(1)} %copy-done.5), channel_id=1, source_target_pairs={{0,16},{4,20},{8,24},{12,28},{16,0},{20,4},{24,8},{28,12},{1,17},{... | collective-permute-start | bytes 393224 | tf_op jit(solution)/shard_map/ppermute | solution.py:352
  35.3 5.6 %collective-permute-done.9.refs_10_ = bf16[512,128]{1,0:T(8,128)(2,1)S(1)} collective-permute-done((bf16[512,128]{1,0:T(8,128)(2,1)S(1)}, bf16[512,128]{1,0:T(8,128)(2,1)S(1)}, u32[]{:S(2)}, u32[]{:S(2)}) %collective-permute-start.9) | collective-permute-done | bytes 131104 | tf_op jit(solution)/shard_map/ppermute | solution.py:352
  40.9 1.8 %collective-permute-start.10 = (bf16[512,128]{1,0:T(8,128)(2,1)S(1)}, bf16[512,128]{1,0:T(8,128)(2,1)S(1)}, u32[]{:S(2)}, u32[]{:S(2)}) collective-permute-start(bf16[512,128]{1,0:T(8,128)(2,1)S(1)} %copy-done.3), channel_id=1, source_target_pairs={{0,24},{4,28},{8,16},{12,20},{16,8},{20,12},{24,0},{28,4},{1,25},{... | collective-permute-start | bytes 393224 | tf_op jit(solution)/shard_map/ppermute | solution.py:352
  42.7 3.1 %collective-permute-done.8.refs_9_ = bf16[512,128]{1,0:T(8,128)(2,1)S(1)} collective-permute-done((bf16[512,128]{1,0:T(8,128)(2,1)S(1)}, bf16[512,128]{1,0:T(8,128)(2,1)S(1)}, u32[]{:S(2)}, u32[]{:S(2)}) %collective-permute-start.8) | collective-permute-done | bytes 131104 | tf_op jit(solution)/shard_map/ppermute | solution.py:352
  45.8 2.0 %collective-permute-done.10.refs_11_ = bf16[512,128]{1,0:T(8,128)(2,1)S(1)} collective-permute-done((bf16[512,128]{1,0:T(8,128)(2,1)S(1)}, bf16[512,128]{1,0:T(8,128)(2,1)S(1)}, u32[]{:S(2)}, u32[]{:S(2)}) %collective-permute-start.10) | collective-permute-done | bytes 131104 | tf_op jit(solution)/shard_map/ppermute | solution.py:352
  47.8 10.1 %attend.1 = (bf16[512,128]{1,0:T(8,128)(2,1)S(1)}, bf16[512,128]{1,0:T(8,128)(2,1)S(1)}, bf16[512,128]{1,0:T(8,128)(2,1)S(1)}, bf16[512,128]{1,0:T(8,128)(2,1)S(1)}) custom-call(bf16[1040,128]{1,0:T(8,128)(2,1)S(1)} %copy-done.1, bf16[1040,128]{1,0:T(8,128)(2,1)S(1)} %collective-permute-done.1.refs_1_, bf16[1040,128]{1,0:T(8,128)(2,1)S(1)} %collective-permute-done.2.refs_2_, ...), custom_call_target="tpu_custom_call" | custom-call | flops 4000000000 | bytes 13200000 | tf_op jit(solution)/shard_map/attend/pallas_call | solution.py:249
  57.9 1.5 %collective-permute-start.11 = (bf16[512,128]{1,0:T(8,128)(2,1)S(1)}, bf16[512,128]{1,0:T(8,128)(2,1)S(1)}, u32[]{:S(2)}, u32[]{:S(2)}) collective-permute-start(bf16[512,128]{1,0:T(8,128)(2,1)S(1)} %get-tuple-element.38), channel_id=1, source_target_pairs={{0,8},{4,12},{8,0},{12,4},{16,24},{20,28},{24,16},{28,20},{1,9},{5... | collective-permute-start | bytes 393224 | tf_op jit(solution)/shard_map/ppermute | solution.py:352
  59.4 0.9 %collective-permute-start.12 = (bf16[512,128]{1,0:T(8,128)(2,1)S(1)}, bf16[512,128]{1,0:T(8,128)(2,1)S(1)}, u32[]{:S(2)}, u32[]{:S(2)}) collective-permute-start(bf16[512,128]{1,0:T(8,128)(2,1)S(1)} %get-tuple-element.39), channel_id=1, source_target_pairs={{0,16},{4,20},{8,24},{12,28},{16,0},{20,4},{24,8},{28,12},{1,17},{... | collective-permute-start | bytes 393224 | tf_op jit(solution)/shard_map/ppermute | solution.py:352
  60.3 2.1 %collective-permute-start.13 = (bf16[512,128]{1,0:T(8,128)(2,1)S(1)}, bf16[512,128]{1,0:T(8,128)(2,1)S(1)}, u32[]{:S(2)}, u32[]{:S(2)}) collective-permute-start(bf16[512,128]{1,0:T(8,128)(2,1)S(1)} %get-tuple-element.40), channel_id=1, source_target_pairs={{0,24},{4,28},{8,16},{12,20},{16,8},{20,12},{24,0},{28,4},{1,25},{... | collective-permute-start | bytes 393224 | tf_op jit(solution)/shard_map/ppermute | solution.py:352
  62.4 1.5 %collective-permute-start.14 = (bf16[512,128]{1,0:T(8,128)(2,1)S(1)}, bf16[512,128]{1,0:T(8,128)(2,1)S(1)}, u32[]{:S(2)}, u32[]{:S(2)}) collective-permute-start(bf16[512,128]{1,0:T(8,128)(2,1)S(1)} %get-tuple-element.37.refs_0_), channel_id=1, source_target_pairs={{0,2},{1,3},{2,0},{3,1},{4,6},{5,7},{6,4},{7,5},{8,10},{9,11},{10,... | collective-permute-start | bytes 393224 | tf_op jit(solution)/shard_map/ppermute | solution.py:352
  63.9 0.7 collective-permute-start.15
  64.6 3.5 %collective-permute-done.12.refs_2_ = bf16[512,128]{1,0:T(8,128)(2,1)S(1)} collective-permute-done((bf16[512,128]{1,0:T(8,128)(2,1)S(1)}, bf16[512,128]{1,0:T(8,128)(2,1)S(1)}, u32[]{:S(2)}, u32[]{:S(2)}) %collective-permute-start.12) | collective-permute-done | bytes 131104 | tf_op jit(solution)/shard_map/ppermute | solution.py:352
  68.1 1.5 %collective-permute-start.16 = (bf16[512,128]{1,0:T(8,128)(2,1)S(1)}, bf16[512,128]{1,0:T(8,128)(2,1)S(1)}, u32[]{:S(2)}, u32[]{:S(2)}) collective-permute-start(bf16[512,128]{1,0:T(8,128)(2,1)S(1)} %collective-permute-done.12.refs_2_), channel_id=1, source_target_pairs={{0,2},{1,3},{2,0},{3,1},{4,6},{5,7},{6,4},{7,5},{8,10},{9,11},{10,... | collective-permute-start | bytes 393224 | tf_op jit(solution)/shard_map/ppermute | solution.py:352
  69.6 0.5 collective-permute-start.17
  70.1 1.1 %near_sums.1.near_ref = f32[512,1024]{1,0:T(8,128)S(1)} custom-call(bf16[512,2048]{1,0:T(8,128)(2,1)S(1)} %copy-done, bf16[512,128]{1,0:T(8,128)(2,1)S(1)} %get-tuple-element.37.refs_0_, bf16[512,128]{1,0:T(8,128)(2,1)S(1)} %collective-permute-done.11.refs_1_, bf16[512,128]{1,0:T(8,128)(2,1)S(1)} %collective-permute-done.12.refs_2_, ...), custom_call_target="tpu_custom_call" | custom-call | flops 1500000000 | bytes 4950000 | tf_op jit(solution)/shard_map/near_sums/pallas_call | solution.py:305
  71.2 1.8 %collective-permute-done.16.refs_2_ = bf16[512,128]{1,0:T(8,128)(2,1)S(1)} collective-permute-done((bf16[512,128]{1,0:T(8,128)(2,1)S(1)}, bf16[512,128]{1,0:T(8,128)(2,1)S(1)}, u32[]{:S(2)}, u32[]{:S(2)}) %collective-permute-start.16) | collective-permute-done | bytes 131104 | tf_op jit(solution)/shard_map/ppermute | solution.py:352
  73.1 1.5 %collective-permute-done.17.refs_3_ = bf16[512,128]{1,0:T(8,128)(2,1)S(1)} collective-permute-done((bf16[512,128]{1,0:T(8,128)(2,1)S(1)}, bf16[512,128]{1,0:T(8,128)(2,1)S(1)}, u32[]{:S(2)}, u32[]{:S(2)}) %collective-permute-start.17) | collective-permute-done | bytes 131104 | tf_op jit(solution)/shard_map/ppermute | solution.py:352
  74.6 1.2 %far_sums.1 = (f32[512,512]{1,0:T(8,128)S(1)}, bf16[512,512]{1,0:T(8,128)(2,1)S(1)}) custom-call(bf16[512,1024]{1,0:T(8,128)(2,1)S(1)} %collective-permute-done.w_ref, f32[512,1024]{1,0:T(8,128)S(1)} %near_sums.1.near_ref, bf16[512,128]{1,0:T(8,128)(2,1)S(1)} %collective-permute-done.14.refs_0_, bf16[512,128]{1,0:T(8,128)(2,1)S(1)} %collective-permute-done.15.refs_1_, ...), custom_call_target="tpu_custom_call" | custom-call | flops 1800000000 | bytes 5940000 | tf_op jit(solution)/shard_map/far_sums/pallas_call | solution.py:326
  75.8 1.9 %collective-permute-done.18 = bf16[512,512]{1,0:T(8,128)(2,1)S(1)} collective-permute-done((bf16[512,512]{1,0:T(8,128)(2,1)S(1)}, bf16[512,512]{1,0:T(8,128)(2,1)S(1)}, u32[]{:S(2)}, u32[]{:S(2)}) %collective-permute-start.18) | collective-permute-done | bytes 524320 | tf_op jit(solution)/shard_map/ppermute | solution.py:352
  77.7 1.0 %add_convert_fusion = bf16[512,512]{1,0:T(8,128)(2,1)} fusion(f32[512,512]{1,0:T(8,128)S(1)} %get-tuple-element.41, bf16[512,512]{1,0:T(8,128)(2,1)S(1)} %collective-permute-done.18), kind=kLoop, calls=%fused_computation | loop fusion | flops 786432 | bytes 2097152 | tf_op jit(solution)/shard_map/convert_element_type | solution.py:377
  (24 shorter events, 0.1 us)
Async XLA Ops:
  0.0 20.9 %copy-start = (bf16[512,2048]{1,0:T(8,128)(2,1)S(1)}, bf16[512,2048]{1,0:T(8,128)(2,1)}, u32[]{:S(2)}) copy-start(bf16[512,2048]{1,0:T(8,128)(2,1)} %w_ref.1) | copy-start | bytes 6291460
  3.0 37.9 %copy-start.4 = (bf16[512,128]{1,0:T(8,128)(2,1)S(1)}, bf16[512,128]{1,0:T(8,128)(2,1)}, u32[]{:S(2)}) copy-start(bf16[512,128]{1,0:T(8,128)(2,1)} %get-tuple-element.32) | copy-start | bytes 393220
  3.0 37.9 %copy-start.3 = (bf16[512,128]{1,0:T(8,128)(2,1)S(1)}, bf16[512,128]{1,0:T(8,128)(2,1)}, u32[]{:S(2)}) copy-start(bf16[512,128]{1,0:T(8,128)(2,1)} %get-tuple-element.36) | copy-start | bytes 393220
  3.0 44.9 %copy-start.1 = (bf16[1040,128]{1,0:T(8,128)(2,1)S(1)}, bf16[1040,128]{1,0:T(8,128)(2,1)}, u32[]{:S(2)}) copy-start(bf16[1040,128]{1,0:T(8,128)(2,1)} %get-tuple-element.26.refs_0_) | copy-start | bytes 798724
  3.0 44.8 %copy-start.2 = (bf16[512,128]{1,0:T(8,128)(2,1)S(1)}, bf16[512,128]{1,0:T(8,128)(2,1)}, u32[]{:S(2)}) copy-start(bf16[512,128]{1,0:T(8,128)(2,1)} %get-tuple-element.30.refs_8_) | copy-start | bytes 393220
  3.0 15.3 %collective-permute-start.1 = (bf16[1040,128]{1,0:T(8,128)(2,1)}, bf16[1040,128]{1,0:T(8,128)(2,1)S(1)}, u32[]{:S(2)}, u32[]{:S(2)}) collective-permute-start(bf16[1040,128]{1,0:T(8,128)(2,1)} %get-tuple-element.24), channel_id=1, source_target_pairs={{0,8},{4,12},{8,0},{12,4},{16,24},{20,28},{24,16},{28,20},{1,9},{5... | collective-permute-start | bytes 798728 | tf_op jit(solution)/shard_map/ppermute | solution.py:352
  6.1 16.5 %collective-permute-start.2 = (bf16[1040,128]{1,0:T(8,128)(2,1)}, bf16[1040,128]{1,0:T(8,128)(2,1)S(1)}, u32[]{:S(2)}, u32[]{:S(2)}) collective-permute-start(bf16[1040,128]{1,0:T(8,128)(2,1)} %get-tuple-element.27), channel_id=1, source_target_pairs={{0,16},{4,20},{8,24},{12,28},{16,0},{20,4},{24,8},{28,12},{1,17},{... | collective-permute-start | bytes 798728 | tf_op jit(solution)/shard_map/ppermute | solution.py:352
  8.7 20.6 %collective-permute-start.4 = (bf16[1040,128]{1,0:T(8,128)(2,1)}, bf16[1040,128]{1,0:T(8,128)(2,1)S(1)}, u32[]{:S(2)}, u32[]{:S(2)}) collective-permute-start(bf16[1040,128]{1,0:T(8,128)(2,1)} %get-tuple-element.26.refs_0_), channel_id=1, source_target_pairs={{0,4},{4,0},{8,12},{12,8},{16,20},{20,16},{24,28},{28,24},{1,5},{5... | collective-permute-start | bytes 798728 | tf_op jit(solution)/shard_map/ppermute | solution.py:352
  10.2 19.2 %copy-start.5 = (bf16[512,128]{1,0:T(8,128)(2,1)S(1)}, bf16[512,128]{1,0:T(8,128)(2,1)}, u32[]{:S(2)}) copy-start(bf16[512,128]{1,0:T(8,128)(2,1)} %get-tuple-element.34) | copy-start | bytes 393220
  18.3 9.7 %collective-permute-start.3 = (bf16[1040,128]{1,0:T(8,128)(2,1)}, bf16[1040,128]{1,0:T(8,128)(2,1)S(1)}, u32[]{:S(2)}, u32[]{:S(2)}) collective-permute-start(bf16[1040,128]{1,0:T(8,128)(2,1)} %get-tuple-element.29), channel_id=1, source_target_pairs={{0,24},{4,28},{8,16},{12,20},{16,8},{20,12},{24,0},{28,4},{1,25},{... | collective-permute-start | bytes 798728 | tf_op jit(solution)/shard_map/ppermute | solution.py:352
  21.0 50.2 %collective-permute-start = (bf16[512,1024]{1,0:T(8,128)(2,1)S(1)}, bf16[512,1024]{1,0:T(8,128)(2,1)S(1)}, u32[]{:S(2)}, u32[]{:S(2)}) collective-permute-start(bf16[512,1024]{1,0:T(8,128)(2,1)S(1)} %constant_dynamic-slice_fusion), channel_id=1, source_target_pairs={{0,2},{1,3},{2,0},{3,1},{4,6},{5,7},{6,4},{7,5},{8,10},{9,11},{10,... | collective-permute-start | bytes 3145736 | tf_op jit(solution)/shard_map/ppermute | solution.py:352
  22.6 18.3 %collective-permute-start.6 = (bf16[1040,128]{1,0:T(8,128)(2,1)S(1)}, bf16[1040,128]{1,0:T(8,128)(2,1)S(1)}, u32[]{:S(2)}, u32[]{:S(2)}) collective-permute-start(bf16[1040,128]{1,0:T(8,128)(2,1)S(1)} %collective-permute-done.2.refs_2_), channel_id=1, source_target_pairs={{0,4},{4,0},{8,12},{12,8},{16,20},{20,16},{24,28},{28,24},{1,5},{5... | collective-permute-start | bytes 798728 | tf_op jit(solution)/shard_map/ppermute | solution.py:352
  24.1 18.6 %collective-permute-start.5 = (bf16[1040,128]{1,0:T(8,128)(2,1)S(1)}, bf16[1040,128]{1,0:T(8,128)(2,1)S(1)}, u32[]{:S(2)}, u32[]{:S(2)}) collective-permute-start(bf16[1040,128]{1,0:T(8,128)(2,1)S(1)} %collective-permute-done.1.refs_1_), channel_id=1, source_target_pairs={{0,4},{4,0},{8,12},{12,8},{16,20},{20,16},{24,28},{28,24},{1,5},{5... | collective-permute-start | bytes 798728 | tf_op jit(solution)/shard_map/ppermute | solution.py:352
  28.0 19.8 %collective-permute-start.7 = (bf16[1040,128]{1,0:T(8,128)(2,1)S(1)}, bf16[1040,128]{1,0:T(8,128)(2,1)S(1)}, u32[]{:S(2)}, u32[]{:S(2)}) collective-permute-start(bf16[1040,128]{1,0:T(8,128)(2,1)S(1)} %collective-permute-done.3.refs_3_), channel_id=1, source_target_pairs={{0,4},{4,0},{8,12},{12,8},{16,20},{20,16},{24,28},{28,24},{1,5},{5... | collective-permute-start | bytes 798728 | tf_op jit(solution)/shard_map/ppermute | solution.py:352
  29.3 11.5 %collective-permute-start.9 = (bf16[512,128]{1,0:T(8,128)(2,1)S(1)}, bf16[512,128]{1,0:T(8,128)(2,1)S(1)}, u32[]{:S(2)}, u32[]{:S(2)}) collective-permute-start(bf16[512,128]{1,0:T(8,128)(2,1)S(1)} %copy-done.5), channel_id=1, source_target_pairs={{0,16},{4,20},{8,24},{12,28},{16,0},{20,4},{24,8},{28,12},{1,17},{... | collective-permute-start | bytes 393224 | tf_op jit(solution)/shard_map/ppermute | solution.py:352
  40.8 5.0 %collective-permute-start.8 = (bf16[512,128]{1,0:T(8,128)(2,1)S(1)}, bf16[512,128]{1,0:T(8,128)(2,1)S(1)}, u32[]{:S(2)}, u32[]{:S(2)}) collective-permute-start(bf16[512,128]{1,0:T(8,128)(2,1)S(1)} %copy-done.4), channel_id=1, source_target_pairs={{0,8},{4,12},{8,0},{12,4},{16,24},{20,28},{24,16},{28,20},{1,9},{5... | collective-permute-start | bytes 393224 | tf_op jit(solution)/shard_map/ppermute | solution.py:352
  40.9 6.9 %collective-permute-start.10 = (bf16[512,128]{1,0:T(8,128)(2,1)S(1)}, bf16[512,128]{1,0:T(8,128)(2,1)S(1)}, u32[]{:S(2)}, u32[]{:S(2)}) collective-permute-start(bf16[512,128]{1,0:T(8,128)(2,1)S(1)} %copy-done.3), channel_id=1, source_target_pairs={{0,24},{4,28},{8,16},{12,20},{16,8},{20,12},{24,0},{28,4},{1,25},{... | collective-permute-start | bytes 393224 | tf_op jit(solution)/shard_map/ppermute | solution.py:352
  57.9 6.0 %collective-permute-start.11 = (bf16[512,128]{1,0:T(8,128)(2,1)S(1)}, bf16[512,128]{1,0:T(8,128)(2,1)S(1)}, u32[]{:S(2)}, u32[]{:S(2)}) collective-permute-start(bf16[512,128]{1,0:T(8,128)(2,1)S(1)} %get-tuple-element.38), channel_id=1, source_target_pairs={{0,8},{4,12},{8,0},{12,4},{16,24},{20,28},{24,16},{28,20},{1,9},{5... | collective-permute-start | bytes 393224 | tf_op jit(solution)/shard_map/ppermute | solution.py:352
  59.4 8.7 %collective-permute-start.12 = (bf16[512,128]{1,0:T(8,128)(2,1)S(1)}, bf16[512,128]{1,0:T(8,128)(2,1)S(1)}, u32[]{:S(2)}, u32[]{:S(2)}) collective-permute-start(bf16[512,128]{1,0:T(8,128)(2,1)S(1)} %get-tuple-element.39), channel_id=1, source_target_pairs={{0,16},{4,20},{8,24},{12,28},{16,0},{20,4},{24,8},{28,12},{1,17},{... | collective-permute-start | bytes 393224 | tf_op jit(solution)/shard_map/ppermute | solution.py:352
  60.3 9.3 %collective-permute-start.13 = (bf16[512,128]{1,0:T(8,128)(2,1)S(1)}, bf16[512,128]{1,0:T(8,128)(2,1)S(1)}, u32[]{:S(2)}, u32[]{:S(2)}) collective-permute-start(bf16[512,128]{1,0:T(8,128)(2,1)S(1)} %get-tuple-element.40), channel_id=1, source_target_pairs={{0,24},{4,28},{8,16},{12,20},{16,8},{20,12},{24,0},{28,4},{1,25},{... | collective-permute-start | bytes 393224 | tf_op jit(solution)/shard_map/ppermute | solution.py:352
  62.4 8.8 %collective-permute-start.14 = (bf16[512,128]{1,0:T(8,128)(2,1)S(1)}, bf16[512,128]{1,0:T(8,128)(2,1)S(1)}, u32[]{:S(2)}, u32[]{:S(2)}) collective-permute-start(bf16[512,128]{1,0:T(8,128)(2,1)S(1)} %get-tuple-element.37.refs_0_), channel_id=1, source_target_pairs={{0,2},{1,3},{2,0},{3,1},{4,6},{5,7},{6,4},{7,5},{8,10},{9,11},{10,... | collective-permute-start | bytes 393224 | tf_op jit(solution)/shard_map/ppermute | solution.py:352
  63.9 7.3 %collective-permute-start.15 = (bf16[512,128]{1,0:T(8,128)(2,1)S(1)}, bf16[512,128]{1,0:T(8,128)(2,1)S(1)}, u32[]{:S(2)}, u32[]{:S(2)}) collective-permute-start(bf16[512,128]{1,0:T(8,128)(2,1)S(1)} %collective-permute-done.11.refs_1_), channel_id=1, source_target_pairs={{0,2},{1,3},{2,0},{3,1},{4,6},{5,7},{6,4},{7,5},{8,10},{9,11},{10,... | collective-permute-start | bytes 393224 | tf_op jit(solution)/shard_map/ppermute | solution.py:352
  68.1 5.0 %collective-permute-start.16 = (bf16[512,128]{1,0:T(8,128)(2,1)S(1)}, bf16[512,128]{1,0:T(8,128)(2,1)S(1)}, u32[]{:S(2)}, u32[]{:S(2)}) collective-permute-start(bf16[512,128]{1,0:T(8,128)(2,1)S(1)} %collective-permute-done.12.refs_2_), channel_id=1, source_target_pairs={{0,2},{1,3},{2,0},{3,1},{4,6},{5,7},{6,4},{7,5},{8,10},{9,11},{10,... | collective-permute-start | bytes 393224 | tf_op jit(solution)/shard_map/ppermute | solution.py:352
  69.6 5.0 %collective-permute-start.17 = (bf16[512,128]{1,0:T(8,128)(2,1)S(1)}, bf16[512,128]{1,0:T(8,128)(2,1)S(1)}, u32[]{:S(2)}, u32[]{:S(2)}) collective-permute-start(bf16[512,128]{1,0:T(8,128)(2,1)S(1)} %collective-permute-done.13.refs_3_), channel_id=1, source_target_pairs={{0,2},{1,3},{2,0},{3,1},{4,6},{5,7},{6,4},{7,5},{8,10},{9,11},{10,... | collective-permute-start | bytes 393224 | tf_op jit(solution)/shard_map/ppermute | solution.py:352
  75.8 2.0 %collective-permute-start.18 = (bf16[512,512]{1,0:T(8,128)(2,1)S(1)}, bf16[512,512]{1,0:T(8,128)(2,1)S(1)}, u32[]{:S(2)}, u32[]{:S(2)}) collective-permute-start(bf16[512,512]{1,0:T(8,128)(2,1)S(1)} %get-tuple-element.42), channel_id=1, source_target_pairs={{0,1},{1,0},{2,3},{3,2},{4,5},{5,4},{6,7},{7,6},{8,9},{9,8},{10,11... | collective-permute-start | bytes 1572872 | tf_op jit(solution)/shard_map/ppermute | solution.py:352

commit v6 on v5

--- a/solution.py
+++ b/solution.py
@@ -102,8 +102,10 @@
     rows, width = outs[0].shape
     parts = rows // width
     place = coordinates()[0]
+    queries_out = [outs[0], outs[1].at[pl.ds(2 * rows + ID_ROWS, rows)]] + list(outs[2:heads])
+    keys_out = [outs[heads], outs[1]] + list(outs[heads + 1 :])
     for offset in range(heads):
-        q_out, kv_out = outs[2 * offset], outs[2 * offset + 1]
+        q_out, kv_out = queries_out[offset], keys_out[offset]
         head = lax.bitwise_xor(place, offset)
         columns = pl.ds(pl.multiple_of(head * width, width), width)
         kv_out[pl.ds(0, rows), :] = k_ref[:, columns]
@@ -120,19 +122,16 @@
     rows = queries.shape[0]
     width = queries.shape[1] // heads
     local_memory = pl.BlockSpec(memory_space=pltpu.VMEM)
-    pair = [
-        jax.ShapeDtypeStruct((rows, width), jnp.bfloat16),
-        jax.ShapeDtypeStruct((2 * rows + ID_ROWS, width), jnp.bfloat16),
-    ]
+    sizes = [rows, 3 * rows + ID_ROWS] + [rows] * (heads - 2) + [2 * rows + ID_ROWS] * (heads - 1)
     outs = pl.pallas_call(
         pack_kernel,
-        out_shape=tuple(pair * heads),
+        out_shape=tuple(jax.ShapeDtypeStruct((size, width), jnp.bfloat16) for size in sizes),
         in_specs=[local_memory] * 4,
-        out_specs=(local_memory,) * (2 * heads),
+        out_specs=(local_memory,) * len(sizes),
         cost_estimate=pl.CostEstimate(flops=2700000000, bytes_accessed=8910000, transcendentals=0),
         name="pack",
     )(queries, keys, values, cluster_ids)
-    return outs[0::2], outs[1::2]
+    return list(outs[:heads]), [outs[heads], outs[1]] + list(outs[heads + 1 :])
 
 
 def attend_kernel(scale, *refs):
@@ -152,7 +151,10 @@
         for side, side_refs in enumerate(sides):
             ref = side_refs[offset]
             pairs.append((ref.at[pl.ds(2 * rows, ID_ROWS)], ids_all.at[side, slot]))
-        pairs.append((q_refs[offset], q_all.at[span, pl.ds(0, width)]))
+        source = q_refs[offset]
+        if source.shape[0] > rows:
+            source = source.at[pl.ds(2 * rows + ID_ROWS, rows)]
+        pairs.append((source, q_all.at[span, pl.ds(0, width)]))
         for side, side_refs in enumerate(sides):
             ref = side_refs[offset]
             pairs.append((ref.at[pl.ds(0, rows)], k_all.at[side, span, pl.ds(0, width)]))
@@ -359,15 +361,16 @@
     kv_own[2] = swap(kv[2], "seq", 4)
     kv_own[1] = swap(kv[1], "seq", 2)
     kv_far[0] = swap(kv[0], "seq", 1)
-    kv_own[3] = swap(after(kv[3], kv_own[1]), "seq", 6)
+    kv_own[3] = swap(after(kv[3], kv_own[2]), "seq", 6)
     half = out_weight.shape[1] // 2
     weights = lax.dynamic_slice_in_dim(after(out_weight, kv[1]), (1 - here // 2) * half, half, 1)
     weights = swap(weights, "head", 2)
-    for offset in (1, 2, 3):
+    q_own[1] = kv_own[1]
+    kv_far[1] = swap(kv_own[1][: kv[0].shape[0]], "seq", 1)
+    for offset in (2, 3):
         kv_far[offset] = swap(kv_own[offset], "seq", 1)
     q_own[2] = swap(after(q[2], kv_own[2]), "seq", 4)
-    for offset in (3, 1):
-        q_own[offset] = swap(after(q[offset], kv_own[3]), "seq", 2 * offset)
+    q_own[3] = swap(after(q[3], kv_own[2]), "seq", 6)
     attended = list(attend(kv_own, kv_far, q_own))
     for offset in range(1, heads):
         attended[offset] = swap(attended[offset], "seq", 2 * offset)

time: 78.8 us -> 77.9 us (0.989)
  waiting for transfers between devices: 30.9 us -> 28 us
  starting transfers between devices: 31.4 us -> 33.4 us
    ppermute x19 -> x18, waiting for transfers between devices: 30.9 us -> 28 us  [swap(): lax.ppermute(array, axis, [(place, place ^ bits) for place in range(size)])]
    ppermute x19 -> x18, starting transfers between devices: 31.4 us -> 33.4 us  [swap(): lax.ppermute(array, axis, [(place, place ^ bits) for place in range(size)])]
  transfers between devices with their start and end apart: 19 -> 18, of which waited for: 9 -> 9; matrix products, arithmetic and copies ran while one was open for 0% -> 0% of each run, Pallas kernels for 14% -> 14%
where the time goes in v6:
time: 77.9 us; the launch traced here: 77.8 us
  starting transfers between devices  33.4 us (43%)
  waiting for transfers between devices  28 us (36%)
  Pallas kernels  15.2 us (20%)
  other arithmetic  0.95 us (1%)
    ppermute x18, starting transfers between devices, swap(): lax.ppermute(array, axis, [(place, place ^ bits) for place in range(size)])  33.4 us
    ppermute x18, waiting for transfers between devices, swap(): lax.ppermute(array, axis, [(place, place ^ bits) for place in range(size)])  28 us
    pallas_call x1, Pallas kernels, attend(): pl.pallas_call(lambda *refs: attend_kernel(1.0 / math.sqrt(width), *refs)...  10.1 us
    pallas_call x1, Pallas kernels, pack(): pl.pallas_call(pack_kernel, out_shape=tuple((jax.ShapeDtypeStruct((size,...  2.93 us
  transfers between devices with their start and end apart: 18, of which 9 were waited for; matrix products, arithmetic and copies ran while one was open for 0% of the time, Pallas kernels for 14%

profile of v6, /device:TPU:0, one launch (start us, length us, event | category | flops | bytes accessed | tf_op | source)
XLA Modules:
  0.0 77.8 jit_solution(3886752095061837597)
XLA Ops:
  0.0 2.9 %pack.1 = (bf16[512,128]{1,0:T(8,128)(2,1)}, bf16[1552,128]{1,0:T(8,128)(2,1)}, bf16[512,128]{1,0:T(8,128)(2,1)}, bf16[512,128]{1,0:T(8,128)(2,1)}, bf16[1040,12...) custom-call(bf16[512,512]{1,0:T(8,128)(2,1)} %q_ref.1, bf16[512,512]{1,0:T(8,128)(2,1)} %k_ref.1, ...), custom_call_target="tpu_custom_call" | custom-call | flops 2700000000 | bytes 8910000 | tf_op jit(solution)/shard_map/pack/pallas_call | solution.py:126
  2.9 4.1 %collective-permute-start.2 = (bf16[1040,128]{1,0:T(8,128)(2,1)}, bf16[1040,128]{1,0:T(8,128)(2,1)S(1)}, u32[]{:S(2)}, u32[]{:S(2)}) collective-permute-start(bf16[1040,128]{1,0:T(8,128)(2,1)} %get-tuple-element.25), channel_id=1, source_target_pairs={{0,16},{4,20},{8,24},{12,28},{16,0},{20,4},{24,8},{28,12},{1,17},{... | collective-permute-start | bytes 798728 | tf_op jit(solution)/shard_map/ppermute | solution.py:354
  7.0 1.6 %collective-permute-start.1 = (bf16[1552,128]{1,0:T(8,128)(2,1)}, bf16[1552,128]{1,0:T(8,128)(2,1)S(1)}, u32[]{:S(2)}, u32[]{:S(2)}) collective-permute-start(bf16[1552,128]{1,0:T(8,128)(2,1)} %get-tuple-element.22), channel_id=1, source_target_pairs={{0,8},{4,12},{8,0},{12,4},{16,24},{20,28},{24,16},{28,20},{1,9},{5... | collective-permute-start | bytes 1191944 | tf_op jit(solution)/shard_map/ppermute | solution.py:354
  8.6 1.5 %collective-permute-start.4 = (bf16[1040,128]{1,0:T(8,128)(2,1)}, bf16[1040,128]{1,0:T(8,128)(2,1)S(1)}, u32[]{:S(2)}, u32[]{:S(2)}) collective-permute-start(bf16[1040,128]{1,0:T(8,128)(2,1)} %get-tuple-element.24.refs_0_), channel_id=1, source_target_pairs={{0,4},{4,0},{8,12},{12,8},{16,20},{20,16},{24,28},{28,24},{1,5},{5... | collective-permute-start | bytes 798728 | tf_op jit(solution)/shard_map/ppermute | solution.py:354
  10.1 9.3 %collective-permute-done.2.refs_2_ = bf16[1040,128]{1,0:T(8,128)(2,1)S(1)} collective-permute-done((bf16[1040,128]{1,0:T(8,128)(2,1)}, bf16[1040,128]{1,0:T(8,128)(2,1)S(1)}, u32[]{:S(2)}, u32[]{:S(2)}) %collective-permute-start.2) | collective-permute-done | bytes 266272 | tf_op jit(solution)/shard_map/ppermute | solution.py:354
  19.5 3.5 %collective-permute-start.3 = (bf16[1040,128]{1,0:T(8,128)(2,1)}, bf16[1040,128]{1,0:T(8,128)(2,1)S(1)}, u32[]{:S(2)}, u32[]{:S(2)}) collective-permute-start(bf16[1040,128]{1,0:T(8,128)(2,1)} %get-tuple-element.27), channel_id=1, source_target_pairs={{0,24},{4,28},{8,16},{12,20},{16,8},{20,12},{24,0},{28,4},{1,25},{... | collective-permute-start | bytes 798728 | tf_op jit(solution)/shard_map/ppermute | solution.py:354
  23.0 0.1 constant_dynamic-slice_fusion
  23.1 1.6 %collective-permute-start = (bf16[512,1024]{1,0:T(8,128)(2,1)S(1)}, bf16[512,1024]{1,0:T(8,128)(2,1)S(1)}, u32[]{:S(2)}, u32[]{:S(2)}) collective-permute-start(bf16[512,1024]{1,0:T(8,128)(2,1)S(1)} %constant_dynamic-slice_fusion), channel_id=1, source_target_pairs={{0,2},{1,3},{2,0},{3,1},{4,6},{5,7},{6,4},{7,5},{8,10},{9,11},{10,... | collective-permute-start | bytes 3145736 | tf_op jit(solution)/shard_map/ppermute | solution.py:354
  24.7 1.5 %collective-permute-start.6 = (bf16[1040,128]{1,0:T(8,128)(2,1)S(1)}, bf16[1040,128]{1,0:T(8,128)(2,1)S(1)}, u32[]{:S(2)}, u32[]{:S(2)}) collective-permute-start(bf16[1040,128]{1,0:T(8,128)(2,1)S(1)} %collective-permute-done.2.refs_2_), channel_id=1, source_target_pairs={{0,4},{4,0},{8,12},{12,8},{16,20},{20,16},{24,28},{28,24},{1,5},{5... | collective-permute-start | bytes 798728 | tf_op jit(solution)/shard_map/ppermute | solution.py:354
  26.2 0.6 collective-permute-start.5
  26.8 3.0 %collective-permute-done.3.refs_3_ = bf16[1040,128]{1,0:T(8,128)(2,1)S(1)} collective-permute-done((bf16[1040,128]{1,0:T(8,128)(2,1)}, bf16[1040,128]{1,0:T(8,128)(2,1)S(1)}, u32[]{:S(2)}, u32[]{:S(2)}) %collective-permute-start.3) | collective-permute-done | bytes 266272 | tf_op jit(solution)/shard_map/ppermute | solution.py:354
  29.8 1.5 %collective-permute-start.7 = (bf16[1040,128]{1,0:T(8,128)(2,1)S(1)}, bf16[1040,128]{1,0:T(8,128)(2,1)S(1)}, u32[]{:S(2)}, u32[]{:S(2)}) collective-permute-start(bf16[1040,128]{1,0:T(8,128)(2,1)S(1)} %collective-permute-done.3.refs_3_), channel_id=1, source_target_pairs={{0,4},{4,0},{8,12},{12,8},{16,20},{20,16},{24,28},{28,24},{1,5},{5... | collective-permute-start | bytes 798728 | tf_op jit(solution)/shard_map/ppermute | solution.py:354
  31.3 4.3 %collective-permute-start.8 = (bf16[512,128]{1,0:T(8,128)(2,1)S(1)}, bf16[512,128]{1,0:T(8,128)(2,1)S(1)}, u32[]{:S(2)}, u32[]{:S(2)}) collective-permute-start(bf16[512,128]{1,0:T(8,128)(2,1)S(1)} %copy-done.4), channel_id=1, source_target_pairs={{0,16},{4,20},{8,24},{12,28},{16,0},{20,4},{24,8},{28,12},{1,17},{... | collective-permute-start | bytes 393224 | tf_op jit(solution)/shard_map/ppermute | solution.py:354
  35.7 5.8 %collective-permute-done.8.refs_10_ = bf16[512,128]{1,0:T(8,128)(2,1)S(1)} collective-permute-done((bf16[512,128]{1,0:T(8,128)(2,1)S(1)}, bf16[512,128]{1,0:T(8,128)(2,1)S(1)}, u32[]{:S(2)}, u32[]{:S(2)}) %collective-permute-start.8) | collective-permute-done | bytes 131104 | tf_op jit(solution)/shard_map/ppermute | solution.py:354
  41.4 2.7 %collective-permute-start.9 = (bf16[512,128]{1,0:T(8,128)(2,1)S(1)}, bf16[512,128]{1,0:T(8,128)(2,1)S(1)}, u32[]{:S(2)}, u32[]{:S(2)}) collective-permute-start(bf16[512,128]{1,0:T(8,128)(2,1)S(1)} %copy-done.3), channel_id=1, source_target_pairs={{0,24},{4,28},{8,16},{12,20},{16,8},{20,12},{24,0},{28,4},{1,25},{... | collective-permute-start | bytes 393224 | tf_op jit(solution)/shard_map/ppermute | solution.py:354
  44.1 4.1 %collective-permute-done.9.refs_11_ = bf16[512,128]{1,0:T(8,128)(2,1)S(1)} collective-permute-done((bf16[512,128]{1,0:T(8,128)(2,1)S(1)}, bf16[512,128]{1,0:T(8,128)(2,1)S(1)}, u32[]{:S(2)}, u32[]{:S(2)}) %collective-permute-start.9) | collective-permute-done | bytes 131104 | tf_op jit(solution)/shard_map/ppermute | solution.py:354
  48.2 10.1 %attend.1 = (bf16[512,128]{1,0:T(8,128)(2,1)S(1)}, bf16[512,128]{1,0:T(8,128)(2,1)S(1)}, bf16[512,128]{1,0:T(8,128)(2,1)S(1)}, bf16[512,128]{1,0:T(8,128)(2,1)S(1)}) custom-call(bf16[1040,128]{1,0:T(8,128)(2,1)S(1)} %copy-done.1, bf16[1552,128]{1,0:T(8,128)(2,1)S(1)} %collective-permute-done.1.refs_1_.refs_9_, ...), custom_call_target="tpu_custom_call" | custom-call | flops 4000000000 | bytes 13200000 | tf_op jit(solution)/shard_map/attend/pallas_call | solution.py:251
  58.4 3.2 %collective-permute-start.11 = (bf16[512,128]{1,0:T(8,128)(2,1)S(1)}, bf16[512,128]{1,0:T(8,128)(2,1)S(1)}, u32[]{:S(2)}, u32[]{:S(2)}) collective-permute-start(bf16[512,128]{1,0:T(8,128)(2,1)S(1)} %get-tuple-element.35), channel_id=1, source_target_pairs={{0,16},{4,20},{8,24},{12,28},{16,0},{20,4},{24,8},{28,12},{1,17},{... | collective-permute-start | bytes 393224 | tf_op jit(solution)/shard_map/ppermute | solution.py:354
  61.6 1.2 %collective-permute-start.12 = (bf16[512,128]{1,0:T(8,128)(2,1)S(1)}, bf16[512,128]{1,0:T(8,128)(2,1)S(1)}, u32[]{:S(2)}, u32[]{:S(2)}) collective-permute-start(bf16[512,128]{1,0:T(8,128)(2,1)S(1)} %get-tuple-element.36), channel_id=1, source_target_pairs={{0,24},{4,28},{8,16},{12,20},{16,8},{20,12},{24,0},{28,4},{1,25},{... | collective-permute-start | bytes 393224 | tf_op jit(solution)/shard_map/ppermute | solution.py:354
  62.8 1.5 %collective-permute-start.13 = (bf16[512,128]{1,0:T(8,128)(2,1)S(1)}, bf16[512,128]{1,0:T(8,128)(2,1)S(1)}, u32[]{:S(2)}, u32[]{:S(2)}) collective-permute-start(bf16[512,128]{1,0:T(8,128)(2,1)S(1)} %get-tuple-element.33.refs_0_), channel_id=1, source_target_pairs={{0,2},{1,3},{2,0},{3,1},{4,6},{5,7},{6,4},{7,5},{8,10},{9,11},{10,... | collective-permute-start | bytes 393224 | tf_op jit(solution)/shard_map/ppermute | solution.py:354
  64.3 0.5 collective-permute-done.10.refs_1_
  64.8 1.5 %collective-permute-start.14 = (bf16[512,128]{1,0:T(8,128)(2,1)S(1)}, bf16[512,128]{1,0:T(8,128)(2,1)S(1)}, u32[]{:S(2)}, u32[]{:S(2)}) collective-permute-start(bf16[512,128]{1,0:T(8,128)(2,1)S(1)} %collective-permute-done.10.refs_1_), channel_id=1, source_target_pairs={{0,2},{1,3},{2,0},{3,1},{4,6},{5,7},{6,4},{7,5},{8,10},{9,11},{10,... | collective-permute-start | bytes 393224 | tf_op jit(solution)/shard_map/ppermute | solution.py:354
  66.3 0.7 collective-permute-done.11.refs_2_
  67.0 1.5 %collective-permute-start.15 = (bf16[512,128]{1,0:T(8,128)(2,1)S(1)}, bf16[512,128]{1,0:T(8,128)(2,1)S(1)}, u32[]{:S(2)}, u32[]{:S(2)}) collective-permute-start(bf16[512,128]{1,0:T(8,128)(2,1)S(1)} %collective-permute-done.11.refs_2_), channel_id=1, source_target_pairs={{0,2},{1,3},{2,0},{3,1},{4,6},{5,7},{6,4},{7,5},{8,10},{9,11},{10,... | collective-permute-start | bytes 393224 | tf_op jit(solution)/shard_map/ppermute | solution.py:354
  68.6 1.4 %collective-permute-start.16 = (bf16[512,128]{1,0:T(8,128)(2,1)S(1)}, bf16[512,128]{1,0:T(8,128)(2,1)S(1)}, u32[]{:S(2)}, u32[]{:S(2)}) collective-permute-start(bf16[512,128]{1,0:T(8,128)(2,1)S(1)} %collective-permute-done.12.refs_3_), channel_id=1, source_target_pairs={{0,2},{1,3},{2,0},{3,1},{4,6},{5,7},{6,4},{7,5},{8,10},{9,11},{10,... | collective-permute-start | bytes 393224 | tf_op jit(solution)/shard_map/ppermute | solution.py:354
  70.0 1.1 %near_sums.1.near_ref = f32[512,1024]{1,0:T(8,128)S(1)} custom-call(bf16[512,2048]{1,0:T(8,128)(2,1)S(1)} %copy-done, bf16[512,128]{1,0:T(8,128)(2,1)S(1)} %get-tuple-element.33.refs_0_, bf16[512,128]{1,0:T(8,128)(2,1)S(1)} %collective-permute-done.10.refs_1_, bf16[512,128]{1,0:T(8,128)(2,1)S(1)} %collective-permute-done.11.refs_2_, ...), custom_call_target="tpu_custom_call" | custom-call | flops 1500000000 | bytes 4950000 | tf_op jit(solution)/shard_map/near_sums/pallas_call | solution.py:307
  71.1 1.2 %collective-permute-done.15.refs_2_ = bf16[512,128]{1,0:T(8,128)(2,1)S(1)} collective-permute-done((bf16[512,128]{1,0:T(8,128)(2,1)S(1)}, bf16[512,128]{1,0:T(8,128)(2,1)S(1)}, u32[]{:S(2)}, u32[]{:S(2)}) %collective-permute-start.15) | collective-permute-done | bytes 131104 | tf_op jit(solution)/shard_map/ppermute | solution.py:354
  72.3 1.4 %collective-permute-done.16.refs_3_ = bf16[512,128]{1,0:T(8,128)(2,1)S(1)} collective-permute-done((bf16[512,128]{1,0:T(8,128)(2,1)S(1)}, bf16[512,128]{1,0:T(8,128)(2,1)S(1)}, u32[]{:S(2)}, u32[]{:S(2)}) %collective-permute-start.16) | collective-permute-done | bytes 131104 | tf_op jit(solution)/shard_map/ppermute | solution.py:354
  73.7 1.2 %far_sums.1 = (f32[512,512]{1,0:T(8,128)S(1)}, bf16[512,512]{1,0:T(8,128)(2,1)S(1)}) custom-call(bf16[512,1024]{1,0:T(8,128)(2,1)S(1)} %collective-permute-done.w_ref, f32[512,1024]{1,0:T(8,128)S(1)} %near_sums.1.near_ref, bf16[512,128]{1,0:T(8,128)(2,1)S(1)} %collective-permute-done.13.refs_0_, bf16[512,128]{1,0:T(8,128)(2,1)S(1)} %collective-permute-done.14.refs_1_, ...), custom_call_target="tpu_custom_call" | custom-call | flops 1800000000 | bytes 5940000 | tf_op jit(solution)/shard_map/far_sums/pallas_call | solution.py:328
  74.9 0.1 collective-permute-start.17
  74.9 1.9 %collective-permute-done.17 = bf16[512,512]{1,0:T(8,128)(2,1)S(1)} collective-permute-done((bf16[512,512]{1,0:T(8,128)(2,1)S(1)}, bf16[512,512]{1,0:T(8,128)(2,1)S(1)}, u32[]{:S(2)}, u32[]{:S(2)}) %collective-permute-start.17) | collective-permute-done | bytes 524320 | tf_op jit(solution)/shard_map/ppermute | solution.py:354
  76.8 1.0 %add_convert_fusion = bf16[512,512]{1,0:T(8,128)(2,1)} fusion(f32[512,512]{1,0:T(8,128)S(1)} %get-tuple-element.37, bf16[512,512]{1,0:T(8,128)(2,1)S(1)} %collective-permute-done.17), kind=kLoop, calls=%fused_computation | loop fusion | flops 786432 | bytes 2097152 | tf_op jit(solution)/shard_map/convert_element_type | solution.py:380
  (21 shorter events, 0.1 us)
Async XLA Ops:
  0.0 23.0 %copy-start = (bf16[512,2048]{1,0:T(8,128)(2,1)S(1)}, bf16[512,2048]{1,0:T(8,128)(2,1)}, u32[]{:S(2)}) copy-start(bf16[512,2048]{1,0:T(8,128)(2,1)} %w_ref.1) | copy-start | bytes 6291460
  2.9 38.5 %copy-start.3 = (bf16[512,128]{1,0:T(8,128)(2,1)S(1)}, bf16[512,128]{1,0:T(8,128)(2,1)}, u32[]{:S(2)}) copy-start(bf16[512,128]{1,0:T(8,128)(2,1)} %get-tuple-element.32) | copy-start | bytes 393220
  2.9 45.3 %copy-start.1 = (bf16[1040,128]{1,0:T(8,128)(2,1)S(1)}, bf16[1040,128]{1,0:T(8,128)(2,1)}, u32[]{:S(2)}) copy-start(bf16[1040,128]{1,0:T(8,128)(2,1)} %get-tuple-element.24.refs_0_) | copy-start | bytes 798724
  2.9 45.3 %copy-start.2 = (bf16[512,128]{1,0:T(8,128)(2,1)S(1)}, bf16[512,128]{1,0:T(8,128)(2,1)}, u32[]{:S(2)}) copy-start(bf16[512,128]{1,0:T(8,128)(2,1)} %get-tuple-element.28.refs_8_) | copy-start | bytes 393220
  2.9 16.5 %collective-permute-start.2 = (bf16[1040,128]{1,0:T(8,128)(2,1)}, bf16[1040,128]{1,0:T(8,128)(2,1)S(1)}, u32[]{:S(2)}, u32[]{:S(2)}) collective-permute-start(bf16[1040,128]{1,0:T(8,128)(2,1)} %get-tuple-element.25), channel_id=1, source_target_pairs={{0,16},{4,20},{8,24},{12,28},{16,0},{20,4},{24,8},{28,12},{1,17},{... | collective-permute-start | bytes 798728 | tf_op jit(solution)/shard_map/ppermute | solution.py:354
  7.0 19.1 %collective-permute-start.1 = (bf16[1552,128]{1,0:T(8,128)(2,1)}, bf16[1552,128]{1,0:T(8,128)(2,1)S(1)}, u32[]{:S(2)}, u32[]{:S(2)}) collective-permute-start(bf16[1552,128]{1,0:T(8,128)(2,1)} %get-tuple-element.22), channel_id=1, source_target_pairs={{0,8},{4,12},{8,0},{12,4},{16,24},{20,28},{24,16},{28,20},{1,9},{5... | collective-permute-start | bytes 1191944 | tf_op jit(solution)/shard_map/ppermute | solution.py:354
  8.6 22.7 %collective-permute-start.4 = (bf16[1040,128]{1,0:T(8,128)(2,1)}, bf16[1040,128]{1,0:T(8,128)(2,1)S(1)}, u32[]{:S(2)}, u32[]{:S(2)}) collective-permute-start(bf16[1040,128]{1,0:T(8,128)(2,1)} %get-tuple-element.24.refs_0_), channel_id=1, source_target_pairs={{0,4},{4,0},{8,12},{12,8},{16,20},{20,16},{24,28},{28,24},{1,5},{5... | collective-permute-start | bytes 798728 | tf_op jit(solution)/shard_map/ppermute | solution.py:354
  10.1 21.2 %copy-start.4 = (bf16[512,128]{1,0:T(8,128)(2,1)S(1)}, bf16[512,128]{1,0:T(8,128)(2,1)}, u32[]{:S(2)}) copy-start(bf16[512,128]{1,0:T(8,128)(2,1)} %get-tuple-element.30) | copy-start | bytes 393220
  19.5 10.4 %collective-permute-start.3 = (bf16[1040,128]{1,0:T(8,128)(2,1)}, bf16[1040,128]{1,0:T(8,128)(2,1)S(1)}, u32[]{:S(2)}, u32[]{:S(2)}) collective-permute-start(bf16[1040,128]{1,0:T(8,128)(2,1)} %get-tuple-element.27), channel_id=1, source_target_pairs={{0,24},{4,28},{8,16},{12,20},{16,8},{20,12},{24,0},{28,4},{1,25},{... | collective-permute-start | bytes 798728 | tf_op jit(solution)/shard_map/ppermute | solution.py:354
  23.1 48.0 %collective-permute-start = (bf16[512,1024]{1,0:T(8,128)(2,1)S(1)}, bf16[512,1024]{1,0:T(8,128)(2,1)S(1)}, u32[]{:S(2)}, u32[]{:S(2)}) collective-permute-start(bf16[512,1024]{1,0:T(8,128)(2,1)S(1)} %constant_dynamic-slice_fusion), channel_id=1, source_target_pairs={{0,2},{1,3},{2,0},{3,1},{4,6},{5,7},{6,4},{7,5},{8,10},{9,11},{10,... | collective-permute-start | bytes 3145736 | tf_op jit(solution)/shard_map/ppermute | solution.py:354
  24.7 23.5 %collective-permute-start.6 = (bf16[1040,128]{1,0:T(8,128)(2,1)S(1)}, bf16[1040,128]{1,0:T(8,128)(2,1)S(1)}, u32[]{:S(2)}, u32[]{:S(2)}) collective-permute-start(bf16[1040,128]{1,0:T(8,128)(2,1)S(1)} %collective-permute-done.2.refs_2_), channel_id=1, source_target_pairs={{0,4},{4,0},{8,12},{12,8},{16,20},{20,16},{24,28},{28,24},{1,5},{5... | collective-permute-start | bytes 798728 | tf_op jit(solution)/shard_map/ppermute | solution.py:354
  26.2 22.0 %collective-permute-start.5 = (bf16[1040,128]{1,0:T(8,128)(2,1)S(1)}, bf16[1040,128]{1,0:T(8,128)(2,1)S(1)}, u32[]{:S(2)}, u32[]{:S(2)}) collective-permute-start(bf16[1040,128]{1,0:T(8,128)(2,1)S(1)} %slice.4), channel_id=1, source_target_pairs={{0,4},{4,0},{8,12},{12,8},{16,20},{20,16},{24,28},{28,24},{1,5},{5... | collective-permute-start | bytes 798728 | tf_op jit(solution)/shard_map/ppermute | solution.py:354
  29.8 18.4 %collective-permute-start.7 = (bf16[1040,128]{1,0:T(8,128)(2,1)S(1)}, bf16[1040,128]{1,0:T(8,128)(2,1)S(1)}, u32[]{:S(2)}, u32[]{:S(2)}) collective-permute-start(bf16[1040,128]{1,0:T(8,128)(2,1)S(1)} %collective-permute-done.3.refs_3_), channel_id=1, source_target_pairs={{0,4},{4,0},{8,12},{12,8},{16,20},{20,16},{24,28},{28,24},{1,5},{5... | collective-permute-start | bytes 798728 | tf_op jit(solution)/shard_map/ppermute | solution.py:354
  31.3 10.1 %collective-permute-start.8 = (bf16[512,128]{1,0:T(8,128)(2,1)S(1)}, bf16[512,128]{1,0:T(8,128)(2,1)S(1)}, u32[]{:S(2)}, u32[]{:S(2)}) collective-permute-start(bf16[512,128]{1,0:T(8,128)(2,1)S(1)} %copy-done.4), channel_id=1, source_target_pairs={{0,16},{4,20},{8,24},{12,28},{16,0},{20,4},{24,8},{28,12},{1,17},{... | collective-permute-start | bytes 393224 | tf_op jit(solution)/shard_map/ppermute | solution.py:354
  41.4 6.8 %collective-permute-start.9 = (bf16[512,128]{1,0:T(8,128)(2,1)S(1)}, bf16[512,128]{1,0:T(8,128)(2,1)S(1)}, u32[]{:S(2)}, u32[]{:S(2)}) collective-permute-start(bf16[512,128]{1,0:T(8,128)(2,1)S(1)} %copy-done.3), channel_id=1, source_target_pairs={{0,24},{4,28},{8,16},{12,20},{16,8},{20,12},{24,0},{28,4},{1,25},{... | collective-permute-start | bytes 393224 | tf_op jit(solution)/shard_map/ppermute | solution.py:354
  58.3 6.5 %collective-permute-start.10 = (bf16[512,128]{1,0:T(8,128)(2,1)S(1)}, bf16[512,128]{1,0:T(8,128)(2,1)S(1)}, u32[]{:S(2)}, u32[]{:S(2)}) collective-permute-start(bf16[512,128]{1,0:T(8,128)(2,1)S(1)} %get-tuple-element.34), channel_id=1, source_target_pairs={{0,8},{4,12},{8,0},{12,4},{16,24},{20,28},{24,16},{28,20},{1,9},{5... | collective-permute-start | bytes 393224 | tf_op jit(solution)/shard_map/ppermute | solution.py:354
  58.4 8.6 %collective-permute-start.11 = (bf16[512,128]{1,0:T(8,128)(2,1)S(1)}, bf16[512,128]{1,0:T(8,128)(2,1)S(1)}, u32[]{:S(2)}, u32[]{:S(2)}) collective-permute-start(bf16[512,128]{1,0:T(8,128)(2,1)S(1)} %get-tuple-element.35), channel_id=1, source_target_pairs={{0,16},{4,20},{8,24},{12,28},{16,0},{20,4},{24,8},{28,12},{1,17},{... | collective-permute-start | bytes 393224 | tf_op jit(solution)/shard_map/ppermute | solution.py:354
  61.6 6.9 %collective-permute-start.12 = (bf16[512,128]{1,0:T(8,128)(2,1)S(1)}, bf16[512,128]{1,0:T(8,128)(2,1)S(1)}, u32[]{:S(2)}, u32[]{:S(2)}) collective-permute-start(bf16[512,128]{1,0:T(8,128)(2,1)S(1)} %get-tuple-element.36), channel_id=1, source_target_pairs={{0,24},{4,28},{8,16},{12,20},{16,8},{20,12},{24,0},{28,4},{1,25},{... | collective-permute-start | bytes 393224 | tf_op jit(solution)/shard_map/ppermute | solution.py:354
  62.8 8.3 %collective-permute-start.13 = (bf16[512,128]{1,0:T(8,128)(2,1)S(1)}, bf16[512,128]{1,0:T(8,128)(2,1)S(1)}, u32[]{:S(2)}, u32[]{:S(2)}) collective-permute-start(bf16[512,128]{1,0:T(8,128)(2,1)S(1)} %get-tuple-element.33.refs_0_), channel_id=1, source_target_pairs={{0,2},{1,3},{2,0},{3,1},{4,6},{5,7},{6,4},{7,5},{8,10},{9,11},{10,... | collective-permute-start | bytes 393224 | tf_op jit(solution)/shard_map/ppermute | solution.py:354
  64.8 6.3 %collective-permute-start.14 = (bf16[512,128]{1,0:T(8,128)(2,1)S(1)}, bf16[512,128]{1,0:T(8,128)(2,1)S(1)}, u32[]{:S(2)}, u32[]{:S(2)}) collective-permute-start(bf16[512,128]{1,0:T(8,128)(2,1)S(1)} %collective-permute-done.10.refs_1_), channel_id=1, source_target_pairs={{0,2},{1,3},{2,0},{3,1},{4,6},{5,7},{6,4},{7,5},{8,10},{9,11},{10,... | collective-permute-start | bytes 393224 | tf_op jit(solution)/shard_map/ppermute | solution.py:354
  67.0 5.3 %collective-permute-start.15 = (bf16[512,128]{1,0:T(8,128)(2,1)S(1)}, bf16[512,128]{1,0:T(8,128)(2,1)S(1)}, u32[]{:S(2)}, u32[]{:S(2)}) collective-permute-start(bf16[512,128]{1,0:T(8,128)(2,1)S(1)} %collective-permute-done.11.refs_2_), channel_id=1, source_target_pairs={{0,2},{1,3},{2,0},{3,1},{4,6},{5,7},{6,4},{7,5},{8,10},{9,11},{10,... | collective-permute-start | bytes 393224 | tf_op jit(solution)/shard_map/ppermute | solution.py:354
  68.6 5.1 %collective-permute-start.16 = (bf16[512,128]{1,0:T(8,128)(2,1)S(1)}, bf16[512,128]{1,0:T(8,128)(2,1)S(1)}, u32[]{:S(2)}, u32[]{:S(2)}) collective-permute-start(bf16[512,128]{1,0:T(8,128)(2,1)S(1)} %collective-permute-done.12.refs_3_), channel_id=1, source_target_pairs={{0,2},{1,3},{2,0},{3,1},{4,6},{5,7},{6,4},{7,5},{8,10},{9,11},{10,... | collective-permute-start | bytes 393224 | tf_op jit(solution)/shard_map/ppermute | solution.py:354
  74.9 2.0 %collective-permute-start.17 = (bf16[512,512]{1,0:T(8,128)(2,1)S(1)}, bf16[512,512]{1,0:T(8,128)(2,1)S(1)}, u32[]{:S(2)}, u32[]{:S(2)}) collective-permute-start(bf16[512,512]{1,0:T(8,128)(2,1)S(1)} %get-tuple-element.38), channel_id=1, source_target_pairs={{0,1},{1,0},{2,3},{3,2},{4,5},{5,4},{6,7},{7,6},{8,9},{9,8},{10,11... | collective-permute-start | bytes 1572872 | tf_op jit(solution)/shard_map/ppermute | solution.py:354

commit v7 on v6

--- a/solution.py
+++ b/solution.py
@@ -361,7 +361,7 @@
     kv_own[2] = swap(kv[2], "seq", 4)
     kv_own[1] = swap(kv[1], "seq", 2)
     kv_far[0] = swap(kv[0], "seq", 1)
-    kv_own[3] = swap(after(kv[3], kv_own[2]), "seq", 6)
+    kv_own[3] = swap(after(kv[3], kv_own[2], kv_far[0]), "seq", 6)
     half = out_weight.shape[1] // 2
     weights = lax.dynamic_slice_in_dim(after(out_weight, kv[1]), (1 - here // 2) * half, half, 1)
     weights = swap(weights, "head", 2)

time: 77.9 us -> 77.9 us (level)
  no operation moved by 1% of the time
where the time goes in v7:
time: 77.9 us; the launch traced here: 77.8 us
  starting transfers between devices  33.4 us (43%)
  waiting for transfers between devices  27.9 us (36%)
  Pallas kernels  15.2 us (20%)
  other arithmetic  0.95 us (1%)
    ppermute x18, starting transfers between devices, swap(): lax.ppermute(array, axis, [(place, place ^ bits) for place in range(size)])  33.4 us
    ppermute x18, waiting for transfers between devices, swap(): lax.ppermute(array, axis, [(place, place ^ bits) for place in range(size)])  27.9 us
    pallas_call x1, Pallas kernels, attend(): pl.pallas_call(lambda *refs: attend_kernel(1.0 / math.sqrt(width), *refs)...  10.1 us
    pallas_call x1, Pallas kernels, pack(): pl.pallas_call(pack_kernel, out_shape=tuple((jax.ShapeDtypeStruct((size,...  2.93 us
  transfers between devices with their start and end apart: 18, of which 9 were waited for; matrix products, arithmetic and copies ran while one was open for 0% of the time, Pallas kernels for 14%

profile of v7, /device:TPU:0, one launch (start us, length us, event | category | flops | bytes accessed | tf_op | source)
XLA Modules:
  0.0 77.8 jit_solution(12357169314918137491)
XLA Ops:
  0.0 2.9 %pack.1 = (bf16[512,128]{1,0:T(8,128)(2,1)}, bf16[1552,128]{1,0:T(8,128)(2,1)}, bf16[512,128]{1,0:T(8,128)(2,1)}, bf16[512,128]{1,0:T(8,128)(2,1)}, bf16[1040,12...) custom-call(bf16[512,512]{1,0:T(8,128)(2,1)} %q_ref.1, bf16[512,512]{1,0:T(8,128)(2,1)} %k_ref.1, ...), custom_call_target="tpu_custom_call" | custom-call | flops 2700000000 | bytes 8910000 | tf_op jit(solution)/shard_map/pack/pallas_call | solution.py:126
  2.9 4.1 %collective-permute-start.2 = (bf16[1040,128]{1,0:T(8,128)(2,1)}, bf16[1040,128]{1,0:T(8,128)(2,1)S(1)}, u32[]{:S(2)}, u32[]{:S(2)}) collective-permute-start(bf16[1040,128]{1,0:T(8,128)(2,1)} %get-tuple-element.25), channel_id=1, source_target_pairs={{0,16},{4,20},{8,24},{12,28},{16,0},{20,4},{24,8},{28,12},{1,17},{... | collective-permute-start | bytes 798728 | tf_op jit(solution)/shard_map/ppermute | solution.py:354
  7.0 1.5 %collective-permute-start.3 = (bf16[1040,128]{1,0:T(8,128)(2,1)}, bf16[1040,128]{1,0:T(8,128)(2,1)S(1)}, u32[]{:S(2)}, u32[]{:S(2)}) collective-permute-start(bf16[1040,128]{1,0:T(8,128)(2,1)} %get-tuple-element.24.refs_0_), channel_id=1, source_target_pairs={{0,4},{4,0},{8,12},{12,8},{16,20},{20,16},{24,28},{28,24},{1,5},{5... | collective-permute-start | bytes 798728 | tf_op jit(solution)/shard_map/ppermute | solution.py:354
  8.5 1.6 %collective-permute-start.1 = (bf16[1552,128]{1,0:T(8,128)(2,1)}, bf16[1552,128]{1,0:T(8,128)(2,1)S(1)}, u32[]{:S(2)}, u32[]{:S(2)}) collective-permute-start(bf16[1552,128]{1,0:T(8,128)(2,1)} %get-tuple-element.22), channel_id=1, source_target_pairs={{0,8},{4,12},{8,0},{12,4},{16,24},{20,28},{24,16},{28,20},{1,9},{5... | collective-permute-start | bytes 1191944 | tf_op jit(solution)/shard_map/ppermute | solution.py:354
  10.1 9.3 %collective-permute-done.2.refs_2_ = bf16[1040,128]{1,0:T(8,128)(2,1)S(1)} collective-permute-done((bf16[1040,128]{1,0:T(8,128)(2,1)}, bf16[1040,128]{1,0:T(8,128)(2,1)S(1)}, u32[]{:S(2)}, u32[]{:S(2)}) %collective-permute-start.2) | collective-permute-done | bytes 266272 | tf_op jit(solution)/shard_map/ppermute | solution.py:354
  19.5 3.5 %collective-permute-start.4 = (bf16[1040,128]{1,0:T(8,128)(2,1)}, bf16[1040,128]{1,0:T(8,128)(2,1)S(1)}, u32[]{:S(2)}, u32[]{:S(2)}) collective-permute-start(bf16[1040,128]{1,0:T(8,128)(2,1)} %get-tuple-element.27), channel_id=1, source_target_pairs={{0,24},{4,28},{8,16},{12,20},{16,8},{20,12},{24,0},{28,4},{1,25},{... | collective-permute-start | bytes 798728 | tf_op jit(solution)/shard_map/ppermute | solution.py:354
  23.0 0.1 constant_dynamic-slice_fusion
  23.1 1.6 %collective-permute-start = (bf16[512,1024]{1,0:T(8,128)(2,1)S(1)}, bf16[512,1024]{1,0:T(8,128)(2,1)S(1)}, u32[]{:S(2)}, u32[]{:S(2)}) collective-permute-start(bf16[512,1024]{1,0:T(8,128)(2,1)S(1)} %constant_dynamic-slice_fusion), channel_id=1, source_target_pairs={{0,2},{1,3},{2,0},{3,1},{4,6},{5,7},{6,4},{7,5},{8,10},{9,11},{10,... | collective-permute-start | bytes 3145736 | tf_op jit(solution)/shard_map/ppermute | solution.py:354
  24.7 1.5 %collective-permute-start.6 = (bf16[1040,128]{1,0:T(8,128)(2,1)S(1)}, bf16[1040,128]{1,0:T(8,128)(2,1)S(1)}, u32[]{:S(2)}, u32[]{:S(2)}) collective-permute-start(bf16[1040,128]{1,0:T(8,128)(2,1)S(1)} %collective-permute-done.2.refs_2_), channel_id=1, source_target_pairs={{0,4},{4,0},{8,12},{12,8},{16,20},{20,16},{24,28},{28,24},{1,5},{5... | collective-permute-start | bytes 798728 | tf_op jit(solution)/shard_map/ppermute | solution.py:354
  26.2 0.6 collective-permute-start.5
  26.8 3.0 %collective-permute-done.4.refs_3_ = bf16[1040,128]{1,0:T(8,128)(2,1)S(1)} collective-permute-done((bf16[1040,128]{1,0:T(8,128)(2,1)}, bf16[1040,128]{1,0:T(8,128)(2,1)S(1)}, u32[]{:S(2)}, u32[]{:S(2)}) %collective-permute-start.4) | collective-permute-done | bytes 266272 | tf_op jit(solution)/shard_map/ppermute | solution.py:354
  29.8 1.5 %collective-permute-start.7 = (bf16[1040,128]{1,0:T(8,128)(2,1)S(1)}, bf16[1040,128]{1,0:T(8,128)(2,1)S(1)}, u32[]{:S(2)}, u32[]{:S(2)}) collective-permute-start(bf16[1040,128]{1,0:T(8,128)(2,1)S(1)} %collective-permute-done.4.refs_3_), channel_id=1, source_target_pairs={{0,4},{4,0},{8,12},{12,8},{16,20},{20,16},{24,28},{28,24},{1,5},{5... | collective-permute-start | bytes 798728 | tf_op jit(solution)/shard_map/ppermute | solution.py:354
  31.3 4.3 %collective-permute-start.8 = (bf16[512,128]{1,0:T(8,128)(2,1)S(1)}, bf16[512,128]{1,0:T(8,128)(2,1)S(1)}, u32[]{:S(2)}, u32[]{:S(2)}) collective-permute-start(bf16[512,128]{1,0:T(8,128)(2,1)S(1)} %copy-done.4), channel_id=1, source_target_pairs={{0,16},{4,20},{8,24},{12,28},{16,0},{20,4},{24,8},{28,12},{1,17},{... | collective-permute-start | bytes 393224 | tf_op jit(solution)/shard_map/ppermute | solution.py:354
  35.7 5.8 %collective-permute-done.8.refs_10_ = bf16[512,128]{1,0:T(8,128)(2,1)S(1)} collective-permute-done((bf16[512,128]{1,0:T(8,128)(2,1)S(1)}, bf16[512,128]{1,0:T(8,128)(2,1)S(1)}, u32[]{:S(2)}, u32[]{:S(2)}) %collective-permute-start.8) | collective-permute-done | bytes 131104 | tf_op jit(solution)/shard_map/ppermute | solution.py:354
  41.4 2.7 %collective-permute-start.9 = (bf16[512,128]{1,0:T(8,128)(2,1)S(1)}, bf16[512,128]{1,0:T(8,128)(2,1)S(1)}, u32[]{:S(2)}, u32[]{:S(2)}) collective-permute-start(bf16[512,128]{1,0:T(8,128)(2,1)S(1)} %copy-done.3), channel_id=1, source_target_pairs={{0,24},{4,28},{8,16},{12,20},{16,8},{20,12},{24,0},{28,4},{1,25},{... | collective-permute-start | bytes 393224 | tf_op jit(solution)/shard_map/ppermute | solution.py:354
  44.1 4.1 %collective-permute-done.9.refs_11_ = bf16[512,128]{1,0:T(8,128)(2,1)S(1)} collective-permute-done((bf16[512,128]{1,0:T(8,128)(2,1)S(1)}, bf16[512,128]{1,0:T(8,128)(2,1)S(1)}, u32[]{:S(2)}, u32[]{:S(2)}) %collective-permute-start.9) | collective-permute-done | bytes 131104 | tf_op jit(solution)/shard_map/ppermute | solution.py:354
  48.2 10.1 %attend.1 = (bf16[512,128]{1,0:T(8,128)(2,1)S(1)}, bf16[512,128]{1,0:T(8,128)(2,1)S(1)}, bf16[512,128]{1,0:T(8,128)(2,1)S(1)}, bf16[512,128]{1,0:T(8,128)(2,1)S(1)}) custom-call(bf16[1040,128]{1,0:T(8,128)(2,1)S(1)} %copy-done.1, bf16[1552,128]{1,0:T(8,128)(2,1)S(1)} %collective-permute-done.1.refs_1_.refs_9_, ...), custom_call_target="tpu_custom_call" | custom-call | flops 4000000000 | bytes 13200000 | tf_op jit(solution)/shard_map/attend/pallas_call | solution.py:251
  58.3 0.1 collective-permute-start.10
  58.4 3.2 %collective-permute-start.11 = (bf16[512,128]{1,0:T(8,128)(2,1)S(1)}, bf16[512,128]{1,0:T(8,128)(2,1)S(1)}, u32[]{:S(2)}, u32[]{:S(2)}) collective-permute-start(bf16[512,128]{1,0:T(8,128)(2,1)S(1)} %get-tuple-element.35), channel_id=1, source_target_pairs={{0,16},{4,20},{8,24},{12,28},{16,0},{20,4},{24,8},{28,12},{1,17},{... | collective-permute-start | bytes 393224 | tf_op jit(solution)/shard_map/ppermute | solution.py:354
  61.6 1.2 %collective-permute-start.12 = (bf16[512,128]{1,0:T(8,128)(2,1)S(1)}, bf16[512,128]{1,0:T(8,128)(2,1)S(1)}, u32[]{:S(2)}, u32[]{:S(2)}) collective-permute-start(bf16[512,128]{1,0:T(8,128)(2,1)S(1)} %get-tuple-element.36), channel_id=1, source_target_pairs={{0,24},{4,28},{8,16},{12,20},{16,8},{20,12},{24,0},{28,4},{1,25},{... | collective-permute-start | bytes 393224 | tf_op jit(solution)/shard_map/ppermute | solution.py:354
  62.8 1.5 %collective-permute-start.13 = (bf16[512,128]{1,0:T(8,128)(2,1)S(1)}, bf16[512,128]{1,0:T(8,128)(2,1)S(1)}, u32[]{:S(2)}, u32[]{:S(2)}) collective-permute-start(bf16[512,128]{1,0:T(8,128)(2,1)S(1)} %get-tuple-element.33.refs_0_), channel_id=1, source_target_pairs={{0,2},{1,3},{2,0},{3,1},{4,6},{5,7},{6,4},{7,5},{8,10},{9,11},{10,... | collective-permute-start | bytes 393224 | tf_op jit(solution)/shard_map/ppermute | solution.py:354
  64.3 0.5 collective-permute-done.10.refs_1_
  64.8 1.5 %collective-permute-start.14 = (bf16[512,128]{1,0:T(8,128)(2,1)S(1)}, bf16[512,128]{1,0:T(8,128)(2,1)S(1)}, u32[]{:S(2)}, u32[]{:S(2)}) collective-permute-start(bf16[512,128]{1,0:T(8,128)(2,1)S(1)} %collective-permute-done.10.refs_1_), channel_id=1, source_target_pairs={{0,2},{1,3},{2,0},{3,1},{4,6},{5,7},{6,4},{7,5},{8,10},{9,11},{10,... | collective-permute-start | bytes 393224 | tf_op jit(solution)/shard_map/ppermute | solution.py:354
  66.3 0.7 collective-permute-done.11.refs_2_
  67.0 1.5 %collective-permute-start.15 = (bf16[512,128]{1,0:T(8,128)(2,1)S(1)}, bf16[512,128]{1,0:T(8,128)(2,1)S(1)}, u32[]{:S(2)}, u32[]{:S(2)}) collective-permute-start(bf16[512,128]{1,0:T(8,128)(2,1)S(1)} %collective-permute-done.11.refs_2_), channel_id=1, source_target_pairs={{0,2},{1,3},{2,0},{3,1},{4,6},{5,7},{6,4},{7,5},{8,10},{9,11},{10,... | collective-permute-start | bytes 393224 | tf_op jit(solution)/shard_map/ppermute | solution.py:354
  68.6 1.4 %collective-permute-start.16 = (bf16[512,128]{1,0:T(8,128)(2,1)S(1)}, bf16[512,128]{1,0:T(8,128)(2,1)S(1)}, u32[]{:S(2)}, u32[]{:S(2)}) collective-permute-start(bf16[512,128]{1,0:T(8,128)(2,1)S(1)} %collective-permute-done.12.refs_3_), channel_id=1, source_target_pairs={{0,2},{1,3},{2,0},{3,1},{4,6},{5,7},{6,4},{7,5},{8,10},{9,11},{10,... | collective-permute-start | bytes 393224 | tf_op jit(solution)/shard_map/ppermute | solution.py:354
  70.0 1.1 %near_sums.1.near_ref = f32[512,1024]{1,0:T(8,128)S(1)} custom-call(bf16[512,2048]{1,0:T(8,128)(2,1)S(1)} %copy-done, bf16[512,128]{1,0:T(8,128)(2,1)S(1)} %get-tuple-element.33.refs_0_, bf16[512,128]{1,0:T(8,128)(2,1)S(1)} %collective-permute-done.10.refs_1_, bf16[512,128]{1,0:T(8,128)(2,1)S(1)} %collective-permute-done.11.refs_2_, ...), custom_call_target="tpu_custom_call" | custom-call | flops 1500000000 | bytes 4950000 | tf_op jit(solution)/shard_map/near_sums/pallas_call | solution.py:307
  71.1 1.2 %collective-permute-done.15.refs_2_ = bf16[512,128]{1,0:T(8,128)(2,1)S(1)} collective-permute-done((bf16[512,128]{1,0:T(8,128)(2,1)S(1)}, bf16[512,128]{1,0:T(8,128)(2,1)S(1)}, u32[]{:S(2)}, u32[]{:S(2)}) %collective-permute-start.15) | collective-permute-done | bytes 131104 | tf_op jit(solution)/shard_map/ppermute | solution.py:354
  72.3 1.4 %collective-permute-done.16.refs_3_ = bf16[512,128]{1,0:T(8,128)(2,1)S(1)} collective-permute-done((bf16[512,128]{1,0:T(8,128)(2,1)S(1)}, bf16[512,128]{1,0:T(8,128)(2,1)S(1)}, u32[]{:S(2)}, u32[]{:S(2)}) %collective-permute-start.16) | collective-permute-done | bytes 131104 | tf_op jit(solution)/shard_map/ppermute | solution.py:354
  73.7 1.2 %far_sums.1 = (f32[512,512]{1,0:T(8,128)S(1)}, bf16[512,512]{1,0:T(8,128)(2,1)S(1)}) custom-call(bf16[512,1024]{1,0:T(8,128)(2,1)S(1)} %collective-permute-done.w_ref, f32[512,1024]{1,0:T(8,128)S(1)} %near_sums.1.near_ref, bf16[512,128]{1,0:T(8,128)(2,1)S(1)} %collective-permute-done.13.refs_0_, bf16[512,128]{1,0:T(8,128)(2,1)S(1)} %collective-permute-done.14.refs_1_, ...), custom_call_target="tpu_custom_call" | custom-call | flops 1800000000 | bytes 5940000 | tf_op jit(solution)/shard_map/far_sums/pallas_call | solution.py:328
  74.9 1.9 %collective-permute-done.17 = bf16[512,512]{1,0:T(8,128)(2,1)S(1)} collective-permute-done((bf16[512,512]{1,0:T(8,128)(2,1)S(1)}, bf16[512,512]{1,0:T(8,128)(2,1)S(1)}, u32[]{:S(2)}, u32[]{:S(2)}) %collective-permute-start.17) | collective-permute-done | bytes 524320 | tf_op jit(solution)/shard_map/ppermute | solution.py:354
  76.8 1.0 %add_convert_fusion = bf16[512,512]{1,0:T(8,128)(2,1)} fusion(f32[512,512]{1,0:T(8,128)S(1)} %get-tuple-element.37, bf16[512,512]{1,0:T(8,128)(2,1)S(1)} %collective-permute-done.17), kind=kLoop, calls=%fused_computation | loop fusion | flops 786432 | bytes 2097152 | tf_op jit(solution)/shard_map/convert_element_type | solution.py:380
  (21 shorter events, 0.1 us)
Async XLA Ops:
  0.0 23.0 %copy-start = (bf16[512,2048]{1,0:T(8,128)(2,1)S(1)}, bf16[512,2048]{1,0:T(8,128)(2,1)}, u32[]{:S(2)}) copy-start(bf16[512,2048]{1,0:T(8,128)(2,1)} %w_ref.1) | copy-start | bytes 6291460
  2.9 38.5 %copy-start.3 = (bf16[512,128]{1,0:T(8,128)(2,1)S(1)}, bf16[512,128]{1,0:T(8,128)(2,1)}, u32[]{:S(2)}) copy-start(bf16[512,128]{1,0:T(8,128)(2,1)} %get-tuple-element.32) | copy-start | bytes 393220
  2.9 45.3 %copy-start.1 = (bf16[1040,128]{1,0:T(8,128)(2,1)S(1)}, bf16[1040,128]{1,0:T(8,128)(2,1)}, u32[]{:S(2)}) copy-start(bf16[1040,128]{1,0:T(8,128)(2,1)} %get-tuple-element.24.refs_0_) | copy-start | bytes 798724
  2.9 45.3 %copy-start.2 = (bf16[512,128]{1,0:T(8,128)(2,1)S(1)}, bf16[512,128]{1,0:T(8,128)(2,1)}, u32[]{:S(2)}) copy-start(bf16[512,128]{1,0:T(8,128)(2,1)} %get-tuple-element.28.refs_8_) | copy-start | bytes 393220
  2.9 16.5 %collective-permute-start.2 = (bf16[1040,128]{1,0:T(8,128)(2,1)}, bf16[1040,128]{1,0:T(8,128)(2,1)S(1)}, u32[]{:S(2)}, u32[]{:S(2)}) collective-permute-start(bf16[1040,128]{1,0:T(8,128)(2,1)} %get-tuple-element.25), channel_id=1, source_target_pairs={{0,16},{4,20},{8,24},{12,28},{16,0},{20,4},{24,8},{28,12},{1,17},{... | collective-permute-start | bytes 798728 | tf_op jit(solution)/shard_map/ppermute | solution.py:354
  7.0 12.4 %collective-permute-start.3 = (bf16[1040,128]{1,0:T(8,128)(2,1)}, bf16[1040,128]{1,0:T(8,128)(2,1)S(1)}, u32[]{:S(2)}, u32[]{:S(2)}) collective-permute-start(bf16[1040,128]{1,0:T(8,128)(2,1)} %get-tuple-element.24.refs_0_), channel_id=1, source_target_pairs={{0,4},{4,0},{8,12},{12,8},{16,20},{20,16},{24,28},{28,24},{1,5},{5... | collective-permute-start | bytes 798728 | tf_op jit(solution)/shard_map/ppermute | solution.py:354
  8.5 17.6 %collective-permute-start.1 = (bf16[1552,128]{1,0:T(8,128)(2,1)}, bf16[1552,128]{1,0:T(8,128)(2,1)S(1)}, u32[]{:S(2)}, u32[]{:S(2)}) collective-permute-start(bf16[1552,128]{1,0:T(8,128)(2,1)} %get-tuple-element.22), channel_id=1, source_target_pairs={{0,8},{4,12},{8,0},{12,4},{16,24},{20,28},{24,16},{28,20},{1,9},{5... | collective-permute-start | bytes 1191944 | tf_op jit(solution)/shard_map/ppermute | solution.py:354
  10.1 21.2 %copy-start.4 = (bf16[512,128]{1,0:T(8,128)(2,1)S(1)}, bf16[512,128]{1,0:T(8,128)(2,1)}, u32[]{:S(2)}) copy-start(bf16[512,128]{1,0:T(8,128)(2,1)} %get-tuple-element.30) | copy-start | bytes 393220
  19.5 10.4 %collective-permute-start.4 = (bf16[1040,128]{1,0:T(8,128)(2,1)}, bf16[1040,128]{1,0:T(8,128)(2,1)S(1)}, u32[]{:S(2)}, u32[]{:S(2)}) collective-permute-start(bf16[1040,128]{1,0:T(8,128)(2,1)} %get-tuple-element.27), channel_id=1, source_target_pairs={{0,24},{4,28},{8,16},{12,20},{16,8},{20,12},{24,0},{28,4},{1,25},{... | collective-permute-start | bytes 798728 | tf_op jit(solution)/shard_map/ppermute | solution.py:354
  23.1 48.0 %collective-permute-start = (bf16[512,1024]{1,0:T(8,128)(2,1)S(1)}, bf16[512,1024]{1,0:T(8,128)(2,1)S(1)}, u32[]{:S(2)}, u32[]{:S(2)}) collective-permute-start(bf16[512,1024]{1,0:T(8,128)(2,1)S(1)} %constant_dynamic-slice_fusion), channel_id=1, source_target_pairs={{0,2},{1,3},{2,0},{3,1},{4,6},{5,7},{6,4},{7,5},{8,10},{9,11},{10,... | collective-permute-start | bytes 3145736 | tf_op jit(solution)/shard_map/ppermute | solution.py:354
  24.7 23.5 %collective-permute-start.6 = (bf16[1040,128]{1,0:T(8,128)(2,1)S(1)}, bf16[1040,128]{1,0:T(8,128)(2,1)S(1)}, u32[]{:S(2)}, u32[]{:S(2)}) collective-permute-start(bf16[1040,128]{1,0:T(8,128)(2,1)S(1)} %collective-permute-done.2.refs_2_), channel_id=1, source_target_pairs={{0,4},{4,0},{8,12},{12,8},{16,20},{20,16},{24,28},{28,24},{1,5},{5... | collective-permute-start | bytes 798728 | tf_op jit(solution)/shard_map/ppermute | solution.py:354
  26.2 22.0 %collective-permute-start.5 = (bf16[1040,128]{1,0:T(8,128)(2,1)S(1)}, bf16[1040,128]{1,0:T(8,128)(2,1)S(1)}, u32[]{:S(2)}, u32[]{:S(2)}) collective-permute-start(bf16[1040,128]{1,0:T(8,128)(2,1)S(1)} %slice.4), channel_id=1, source_target_pairs={{0,4},{4,0},{8,12},{12,8},{16,20},{20,16},{24,28},{28,24},{1,5},{5... | collective-permute-start | bytes 798728 | tf_op jit(solution)/shard_map/ppermute | solution.py:354
  29.8 18.4 %collective-permute-start.7 = (bf16[1040,128]{1,0:T(8,128)(2,1)S(1)}, bf16[1040,128]{1,0:T(8,128)(2,1)S(1)}, u32[]{:S(2)}, u32[]{:S(2)}) collective-permute-start(bf16[1040,128]{1,0:T(8,128)(2,1)S(1)} %collective-permute-done.4.refs_3_), channel_id=1, source_target_pairs={{0,4},{4,0},{8,12},{12,8},{16,20},{20,16},{24,28},{28,24},{1,5},{5... | collective-permute-start | bytes 798728 | tf_op jit(solution)/shard_map/ppermute | solution.py:354
  31.3 10.1 %collective-permute-start.8 = (bf16[512,128]{1,0:T(8,128)(2,1)S(1)}, bf16[512,128]{1,0:T(8,128)(2,1)S(1)}, u32[]{:S(2)}, u32[]{:S(2)}) collective-permute-start(bf16[512,128]{1,0:T(8,128)(2,1)S(1)} %copy-done.4), channel_id=1, source_target_pairs={{0,16},{4,20},{8,24},{12,28},{16,0},{20,4},{24,8},{28,12},{1,17},{... | collective-permute-start | bytes 393224 | tf_op jit(solution)/shard_map/ppermute | solution.py:354
  41.4 6.8 %collective-permute-start.9 = (bf16[512,128]{1,0:T(8,128)(2,1)S(1)}, bf16[512,128]{1,0:T(8,128)(2,1)S(1)}, u32[]{:S(2)}, u32[]{:S(2)}) collective-permute-start(bf16[512,128]{1,0:T(8,128)(2,1)S(1)} %copy-done.3), channel_id=1, source_target_pairs={{0,24},{4,28},{8,16},{12,20},{16,8},{20,12},{24,0},{28,4},{1,25},{... | collective-permute-start | bytes 393224 | tf_op jit(solution)/shard_map/ppermute | solution.py:354
  58.3 6.5 %collective-permute-start.10 = (bf16[512,128]{1,0:T(8,128)(2,1)S(1)}, bf16[512,128]{1,0:T(8,128)(2,1)S(1)}, u32[]{:S(2)}, u32[]{:S(2)}) collective-permute-start(bf16[512,128]{1,0:T(8,128)(2,1)S(1)} %get-tuple-element.34), channel_id=1, source_target_pairs={{0,8},{4,12},{8,0},{12,4},{16,24},{20,28},{24,16},{28,20},{1,9},{5... | collective-permute-start | bytes 393224 | tf_op jit(solution)/shard_map/ppermute | solution.py:354
  58.4 8.6 %collective-permute-start.11 = (bf16[512,128]{1,0:T(8,128)(2,1)S(1)}, bf16[512,128]{1,0:T(8,128)(2,1)S(1)}, u32[]{:S(2)}, u32[]{:S(2)}) collective-permute-start(bf16[512,128]{1,0:T(8,128)(2,1)S(1)} %get-tuple-element.35), channel_id=1, source_target_pairs={{0,16},{4,20},{8,24},{12,28},{16,0},{20,4},{24,8},{28,12},{1,17},{... | collective-permute-start | bytes 393224 | tf_op jit(solution)/shard_map/ppermute | solution.py:354
  61.6 6.9 %collective-permute-start.12 = (bf16[512,128]{1,0:T(8,128)(2,1)S(1)}, bf16[512,128]{1,0:T(8,128)(2,1)S(1)}, u32[]{:S(2)}, u32[]{:S(2)}) collective-permute-start(bf16[512,128]{1,0:T(8,128)(2,1)S(1)} %get-tuple-element.36), channel_id=1, source_target_pairs={{0,24},{4,28},{8,16},{12,20},{16,8},{20,12},{24,0},{28,4},{1,25},{... | collective-permute-start | bytes 393224 | tf_op jit(solution)/shard_map/ppermute | solution.py:354
  62.8 8.3 %collective-permute-start.13 = (bf16[512,128]{1,0:T(8,128)(2,1)S(1)}, bf16[512,128]{1,0:T(8,128)(2,1)S(1)}, u32[]{:S(2)}, u32[]{:S(2)}) collective-permute-start(bf16[512,128]{1,0:T(8,128)(2,1)S(1)} %get-tuple-element.33.refs_0_), channel_id=1, source_target_pairs={{0,2},{1,3},{2,0},{3,1},{4,6},{5,7},{6,4},{7,5},{8,10},{9,11},{10,... | collective-permute-start | bytes 393224 | tf_op jit(solution)/shard_map/ppermute | solution.py:354
  64.8 6.3 %collective-permute-start.14 = (bf16[512,128]{1,0:T(8,128)(2,1)S(1)}, bf16[512,128]{1,0:T(8,128)(2,1)S(1)}, u32[]{:S(2)}, u32[]{:S(2)}) collective-permute-start(bf16[512,128]{1,0:T(8,128)(2,1)S(1)} %collective-permute-done.10.refs_1_), channel_id=1, source_target_pairs={{0,2},{1,3},{2,0},{3,1},{4,6},{5,7},{6,4},{7,5},{8,10},{9,11},{10,... | collective-permute-start | bytes 393224 | tf_op jit(solution)/shard_map/ppermute | solution.py:354
  67.0 5.2 %collective-permute-start.15 = (bf16[512,128]{1,0:T(8,128)(2,1)S(1)}, bf16[512,128]{1,0:T(8,128)(2,1)S(1)}, u32[]{:S(2)}, u32[]{:S(2)}) collective-permute-start(bf16[512,128]{1,0:T(8,128)(2,1)S(1)} %collective-permute-done.11.refs_2_), channel_id=1, source_target_pairs={{0,2},{1,3},{2,0},{3,1},{4,6},{5,7},{6,4},{7,5},{8,10},{9,11},{10,... | collective-permute-start | bytes 393224 | tf_op jit(solution)/shard_map/ppermute | solution.py:354
  68.6 5.1 %collective-permute-start.16 = (bf16[512,128]{1,0:T(8,128)(2,1)S(1)}, bf16[512,128]{1,0:T(8,128)(2,1)S(1)}, u32[]{:S(2)}, u32[]{:S(2)}) collective-permute-start(bf16[512,128]{1,0:T(8,128)(2,1)S(1)} %collective-permute-done.12.refs_3_), channel_id=1, source_target_pairs={{0,2},{1,3},{2,0},{3,1},{4,6},{5,7},{6,4},{7,5},{8,10},{9,11},{10,... | collective-permute-start | bytes 393224 | tf_op jit(solution)/shard_map/ppermute | solution.py:354
  74.8 2.0 %collective-permute-start.17 = (bf16[512,512]{1,0:T(8,128)(2,1)S(1)}, bf16[512,512]{1,0:T(8,128)(2,1)S(1)}, u32[]{:S(2)}, u32[]{:S(2)}) collective-permute-start(bf16[512,512]{1,0:T(8,128)(2,1)S(1)} %get-tuple-element.38), channel_id=1, source_target_pairs={{0,1},{1,0},{2,3},{3,2},{4,5},{5,4},{6,7},{7,6},{8,9},{9,8},{10,11... | collective-permute-start | bytes 1572872 | tf_op jit(solution)/shard_map/ppermute | solution.py:354
